TPU v7x, 32 devices: a whole 2x2x4 slice. The times are simulated.
32 devices in a mesh: dp: 8 (over z, y), rep: 4 (over x, core).
Axes of the slice: x: 2, y: 2, z: 4, core: 2. Of those that a mesh axis runs over, the one named last changes fastest.
Arguments:
- inputs: bfloat16 [512, 14, 14, 1024], P(('dp', 'rep')), may hold values from -6 to 6
- cotangent: bfloat16 [512, 7, 7, 2048], P(('dp', 'rep')), may hold values from -6 to 6
- image_group: int32 [512], P(('dp', 'rep')), may hold values from 0 to 2, as said below
- group_side: int32 [3], replicated, may hold values from 10 to 14, as said below
- group_width: int32 [3], replicated, may hold values from 2 to 4, as said below
- group_depth: int32 [3], replicated, may hold values from 0 to 1, as said below
- entry_reduce: bfloat16 [1024, 512], P('dp'), may hold values from -0.1875 to 0.1875
- entry_spatial: bfloat16 [9, 512, 512], P(None, 'dp'), may hold values from -0.09375 to 0.09375
- entry_expand: bfloat16 [512, 2048], P('dp'), may hold values from -0.25 to 0.25
- entry_project: bfloat16 [1024, 2048], P('dp'), may hold values from -0.1875 to 0.1875
- entry_norm_reduce: bfloat16 [2, 3, 512], P(None, None, 'dp'), may hold values from 0.099609375 to 1.8984375
- entry_norm_spatial: bfloat16 [2, 3, 512], P(None, None, 'dp'), may hold values from 0.099609375 to 1.8984375
- entry_norm_expand: bfloat16 [2, 3, 2048], P(None, None, 'dp'), may hold values from 0.099609375 to 1.8984375
- entry_norm_project: bfloat16 [2, 3, 2048], P(None, None, 'dp'), may hold values from 0.099609375 to 1.8984375
- inner_reduce: bfloat16 [2048, 512], P('dp'), may hold values from -0.125 to 0.125
- inner_spatial: bfloat16 [9, 512, 512], P(None, 'dp'), may hold values from -0.09375 to 0.09375
- inner_expand: bfloat16 [512, 2048], P('dp'), may hold values from -0.25 to 0.25
- inner_norm_reduce: bfloat16 [2, 3, 512], P(None, None, 'dp'), may hold values from 0.099609375 to 1.8984375
- inner_norm_spatial: bfloat16 [2, 3, 512], P(None, None, 'dp'), may hold values from 0.099609375 to 1.8984375
- inner_norm_expand: bfloat16 [2, 3, 2048], P(None, None, 'dp'), may hold values from 0.099609375 to 1.8984375
Outputs:
- result: bfloat16 [512, 7, 7, 2048], P(('dp', 'rep'))
- input_grad: float32 [512, 14, 14, 1024], P(('dp', 'rep'))
- entry_reduce_grad: float32 [1024, 512], P('dp')
- entry_spatial_grad: float32 [9, 512, 512], P(None, 'dp')
- entry_expand_grad: float32 [512, 2048], P('dp')
- entry_project_grad: float32 [1024, 2048], P('dp')
- entry_norm_reduce_grad: float32 [2, 3, 512], P(None, None, 'dp')
- entry_norm_spatial_grad: float32 [2, 3, 512], P(None, None, 'dp')
- entry_norm_expand_grad: float32 [2, 3, 2048], P(None, None, 'dp')
- entry_norm_project_grad: float32 [2, 3, 2048], P(None, None, 'dp')
- inner_reduce_grad: float32 [2048, 512], P('dp')
- inner_spatial_grad: float32 [9, 512, 512], P(None, 'dp')
- inner_expand_grad: float32 [512, 2048], P('dp')
- inner_norm_reduce_grad: float32 [2, 3, 512], P(None, None, 'dp')
- inner_norm_spatial_grad: float32 [2, 3, 512], P(None, None, 'dp')
- inner_norm_expand_grad: float32 [2, 3, 2048], P(None, None, 'dp')
Inputs may be any that keep to these rules, and one draw needn't show every extreme that they name: `image_group`: the group of each image; every group has images. `group_side`: even sides, distinct between groups, one of them 14; a group's images fill the upper left side x side pixels and the rest of the map is padding. `group_width`: a group uses the first width * 128 inner channels; the groups' values are distinct. `group_depth`: 1 where a group's images pass the second block, 0 where they skip it; exactly one group skips.
All inputs are finite; a program needn't handle non-finite values.
Results may differ from a plain program's by a relative error of at most 0.02.
Values may be sent and summed in bfloat16 or wider, within the bound.
No kernel may reach another device: no remote copies, remote signals or barrier semaphores. Data moves between devices by JAX's collectives and lax.ppermute only.
A program may use at most 256 MiB of HBM per device.

v0:
```python
import jax
import jax.numpy as jnp
from jax import lax
from jax.sharding import PartitionSpec as P

EPSILON = 1e-05
HIGHEST = lax.Precision.HIGHEST


def pixel_mask(limits, extent):
    across = jnp.arange(extent, dtype=jnp.int32)
    inside = (across[None, :, None] < limits[:, None, None]) & (
        across[None, None, :] < limits[:, None, None]
    )
    return inside.astype(jnp.float32)


def group_sums(values, onehot):
    per_image = jnp.sum(values, axis=(1, 2))
    return jnp.dot(onehot.T, per_image, precision=HIGHEST)


def spread_rows(group_table, onehot):
    return jnp.dot(onehot, group_table, precision=HIGHEST)[:, None, None, :]


def conv_single(source, weights):
    return jnp.einsum("nhwc,ck->nhwk", source, weights, preferred_element_type=jnp.float32)


def conv_three(source, weights, stride):
    padded = jnp.pad(source, ((0, 0), (1, 1), (1, 1), (0, 0)))
    out_side = source.shape[1] // stride
    extent = stride * (out_side - 1) + 1
    accumulated = jnp.zeros((source.shape[0], out_side, out_side, weights.shape[2]), jnp.float32)
    for offset in range(9):
        vertical = offset // 3
        lateral = offset % 3
        window = padded[
            :, vertical : vertical + extent : stride, lateral : lateral + extent : stride, :
        ]
        accumulated = accumulated + jnp.einsum(
            "nhwc,ck->nhwk", window, weights[offset], preferred_element_type=jnp.float32
        )
    return accumulated


def conv_three_back(source, upstream, weights, stride):
    padded = jnp.pad(source, ((0, 0), (1, 1), (1, 1), (0, 0)))
    out_side = upstream.shape[1]
    extent = stride * (out_side - 1) + 1
    spread_back = jnp.zeros(padded.shape, jnp.float32)
    pieces = []
    for offset in range(9):
        vertical = offset // 3
        lateral = offset % 3
        window = padded[
            :, vertical : vertical + extent : stride, lateral : lateral + extent : stride, :
        ]
        pieces.append(
            jnp.einsum("nhwc,nhwk->ck", window, upstream, preferred_element_type=jnp.float32)
        )
        placed = jnp.einsum(
            "nhwk,ck->nhwc", upstream, weights[offset], preferred_element_type=jnp.float32
        )
        spread_back = spread_back.at[
            :, vertical : vertical + extent : stride, lateral : lateral + extent : stride, :
        ].add(placed)
    return (jnp.stack(pieces), spread_back[:, 1:-1, 1:-1, :])


def gelu_back(values, upstream):
    return jax.vjp(jax.nn.gelu, values)[1](upstream)[0]


def weight_grad(source, upstream):
    return jnp.einsum("nhwc,nhwk->ck", source, upstream, preferred_element_type=jnp.float32)


def input_back(upstream, weights):
    return jnp.einsum("nhwk,ck->nhwc", upstream, weights, preferred_element_type=jnp.float32)


def body(
    inputs,
    cotangent,
    image_group,
    group_side,
    group_width,
    group_depth,
    entry_reduce,
    entry_spatial,
    entry_expand,
    entry_project,
    entry_norm_reduce,
    entry_norm_spatial,
    entry_norm_expand,
    entry_norm_project,
    inner_reduce,
    inner_spatial,
    inner_expand,
    inner_norm_reduce,
    inner_norm_spatial,
    inner_norm_expand,
):
    groups = group_side.shape[0]
    full_side = inputs.shape[1]
    half_side = full_side // 2
    inner_width = entry_reduce.shape[1]
    onehot_int = (image_group[:, None] == jnp.arange(groups, dtype=jnp.int32)[None, :]).astype(
        jnp.int32
    )
    onehot = onehot_int.astype(jnp.float32)
    totals = lax.psum(jnp.sum(onehot, axis=0), ("dp", "rep"))
    side_real = group_side.astype(jnp.float32)
    half_real = (group_side // 2).astype(jnp.float32)
    counts_in = totals * side_real * side_real
    counts_out = totals * half_real * half_real
    own_side = jnp.sum(onehot_int * group_side[None, :], axis=1)
    own_width = jnp.sum(onehot_int * group_width[None, :], axis=1)
    own_gate = jnp.sum(onehot_int * group_depth[None, :], axis=1).astype(jnp.float32)[
        :, None, None, None
    ]
    valid_in = pixel_mask(own_side, full_side)
    valid_out = pixel_mask(own_side // 2, half_side)
    channel_keep = (
        jnp.arange(inner_width, dtype=jnp.int32)[None, :] < (own_width * inner_width // 4)[:, None]
    ).astype(jnp.float32)
    mask_in = valid_in[..., None] * channel_keep[:, None, None, :]
    mask_out = valid_out[..., None] * channel_keep[:, None, None, :]
    edge_out = valid_out[..., None]
    shards = lax.axis_size("dp")
    position = lax.axis_index("dp")

    def fetch_entry():
        return (
            lax.all_gather(entry_reduce, "dp", axis=0, tiled=True),
            lax.all_gather(entry_spatial, "dp", axis=1, tiled=True),
            lax.all_gather(entry_expand, "dp", axis=0, tiled=True),
            lax.all_gather(entry_project, "dp", axis=0, tiled=True),
            lax.all_gather(entry_norm_reduce, "dp", axis=2, tiled=True),
            lax.all_gather(entry_norm_spatial, "dp", axis=2, tiled=True),
            lax.all_gather(entry_norm_expand, "dp", axis=2, tiled=True),
            lax.all_gather(entry_norm_project, "dp", axis=2, tiled=True),
        )

    def fetch_inner():
        return (
            lax.all_gather(inner_reduce, "dp", axis=0, tiled=True),
            lax.all_gather(inner_spatial, "dp", axis=1, tiled=True),
            lax.all_gather(inner_expand, "dp", axis=0, tiled=True),
            lax.all_gather(inner_norm_reduce, "dp", axis=2, tiled=True),
            lax.all_gather(inner_norm_spatial, "dp", axis=2, tiled=True),
            lax.all_gather(inner_norm_expand, "dp", axis=2, tiled=True),
        )

    def normalize(values, affine, valid, counts):
        masked = values * valid[..., None]
        first_sum, second_sum = lax.psum(
            (group_sums(masked, onehot), group_sums(masked * values, onehot)), ("dp", "rep")
        )
        center = first_sum / counts[:, None]
        inverse = lax.rsqrt(second_sum / counts[:, None] - center * center + EPSILON)
        affine_real = affine.astype(jnp.float32)
        scale_table = affine_real[0] * inverse
        shift_table = affine_real[1] - center * scale_table
        normed = values * spread_rows(scale_table, onehot) + spread_rows(shift_table, onehot)
        return (normed, (values, affine_real[0], center, inverse, counts, valid))

    def normalize_back(upstream, kept_state):
        values, gain_table, center, inverse, counts, valid = kept_state
        centered = (values - spread_rows(center, onehot)) * spread_rows(inverse, onehot)
        local_gain = group_sums(upstream * centered, onehot)
        local_bias = group_sums(upstream, onehot)
        gain_total, bias_total = lax.psum((local_gain, local_bias), ("dp", "rep"))
        factor = spread_rows(gain_table * inverse, onehot)
        mean_bias = spread_rows(bias_total / counts[:, None], onehot)
        mean_gain = spread_rows(gain_total / counts[:, None], onehot)
        grad_values = factor * (upstream - mean_bias - centered * mean_gain) * valid[..., None]
        return (grad_values.astype(jnp.bfloat16), jnp.stack([gain_total, bias_total]))

    def own_share(stacked):
        share_width = stacked.shape[2] // shards
        return lax.dynamic_slice_in_dim(stacked, position * share_width, share_width, 2)

    entry_parts = fetch_entry()
    reduced = conv_single(inputs, entry_parts[0])
    pre_one, state_one = normalize(reduced, entry_parts[4], valid_in, counts_in)
    first_act = (jax.nn.gelu(pre_one) * mask_in).astype(jnp.bfloat16)
    spatial = conv_three(first_act, entry_parts[1], 2)
    pre_two, state_two = normalize(spatial, entry_parts[5], valid_out, counts_out)
    second_act = (jax.nn.gelu(pre_two) * mask_out).astype(jnp.bfloat16)
    expanded = conv_single(second_act, entry_parts[2])
    strided = inputs[:, ::2, ::2, :]
    projected = conv_single(strided, entry_parts[3])
    pre_three, state_three = normalize(expanded, entry_parts[6], valid_out, counts_out)
    pre_skip, state_skip = normalize(projected, entry_parts[7], valid_out, counts_out)
    summed = pre_three + pre_skip
    middle = jax.nn.gelu(summed) * edge_out
    middle_low = middle.astype(jnp.bfloat16)
    inner_parts = fetch_inner()
    inner_reduced = conv_single(middle_low, inner_parts[0])
    pre_four, state_four = normalize(inner_reduced, inner_parts[3], valid_out, counts_out)
    third_act = (jax.nn.gelu(pre_four) * mask_out).astype(jnp.bfloat16)
    inner_mixed = conv_three(third_act, inner_parts[1], 1)
    pre_five, state_five = normalize(inner_mixed, inner_parts[4], valid_out, counts_out)
    fourth_act = (jax.nn.gelu(pre_five) * mask_out).astype(jnp.bfloat16)
    inner_expanded = conv_single(fourth_act, inner_parts[2])
    pre_six, state_six = normalize(inner_expanded, inner_parts[5], valid_out, counts_out)
    closing = pre_six + middle
    closed_value = jax.nn.gelu(closing) * edge_out
    final_value = middle + own_gate * (closed_value - middle)
    upstream = cotangent.astype(jnp.float32)
    inner_back = fetch_inner()
    grad_closing = gelu_back(closing, own_gate * upstream * edge_out)
    grad_middle = (1.0 - own_gate) * upstream + grad_closing
    low_six, table_six = normalize_back(grad_closing, state_six)
    grad_inner_expand = weight_grad(fourth_act, low_six)
    grad_fourth = input_back(low_six, inner_back[2])
    low_five, table_five = normalize_back(gelu_back(pre_five, grad_fourth * mask_out), state_five)
    grad_inner_spatial, grad_third = conv_three_back(third_act, low_five, inner_back[1], 1)
    low_four, table_four = normalize_back(gelu_back(pre_four, grad_third * mask_out), state_four)
    grad_inner_reduce = weight_grad(middle_low, low_four)
    grad_middle = grad_middle + input_back(low_four, inner_back[0])
    inner_shares = (
        lax.psum_scatter(grad_inner_reduce, "dp", scatter_dimension=0, tiled=True),
        lax.psum_scatter(grad_inner_spatial, "dp", scatter_dimension=1, tiled=True),
        lax.psum_scatter(grad_inner_expand, "dp", scatter_dimension=0, tiled=True),
    )
    inner_final = (
        lax.psum(inner_shares[0].astype(jnp.bfloat16), "rep").astype(jnp.float32),
        lax.psum(inner_shares[1].astype(jnp.bfloat16), "rep").astype(jnp.float32),
        lax.psum(inner_shares[2].astype(jnp.bfloat16), "rep").astype(jnp.float32),
    )
    entry_back = fetch_entry()
    grad_summed = gelu_back(summed, grad_middle * edge_out)
    low_three, table_three = normalize_back(grad_summed, state_three)
    low_skip, table_skip = normalize_back(grad_summed, state_skip)
    grad_entry_expand = weight_grad(second_act, low_three)
    grad_second = input_back(low_three, entry_back[2])
    grad_entry_project = weight_grad(strided, low_skip)
    grad_strided = input_back(low_skip, entry_back[3])
    low_two, table_two = normalize_back(gelu_back(pre_two, grad_second * mask_out), state_two)
    grad_entry_spatial, grad_first = conv_three_back(first_act, low_two, entry_back[1], 2)
    low_one, table_one = normalize_back(gelu_back(pre_one, grad_first * mask_in), state_one)
    grad_entry_reduce = weight_grad(inputs, low_one)
    grad_inputs = input_back(low_one, entry_back[0])
    grad_inputs = grad_inputs.at[:, ::2, ::2, :].add(grad_strided)
    entry_shares = (
        lax.psum_scatter(grad_entry_reduce, "dp", scatter_dimension=0, tiled=True),
        lax.psum_scatter(grad_entry_spatial, "dp", scatter_dimension=1, tiled=True),
        lax.psum_scatter(grad_entry_expand, "dp", scatter_dimension=0, tiled=True),
        lax.psum_scatter(grad_entry_project, "dp", scatter_dimension=0, tiled=True),
    )
    entry_final = (
        lax.psum(entry_shares[0].astype(jnp.bfloat16), "rep").astype(jnp.float32),
        lax.psum(entry_shares[1].astype(jnp.bfloat16), "rep").astype(jnp.float32),
        lax.psum(entry_shares[2].astype(jnp.bfloat16), "rep").astype(jnp.float32),
        lax.psum(entry_shares[3].astype(jnp.bfloat16), "rep").astype(jnp.float32),
    )
    return (
        final_value.astype(jnp.bfloat16),
        grad_inputs,
        entry_final[0],
        entry_final[1],
        entry_final[2],
        entry_final[3],
        own_share(table_one),
        own_share(table_two),
        own_share(table_three),
        own_share(table_skip),
        inner_final[0],
        inner_final[1],
        inner_final[2],
        own_share(table_four),
        own_share(table_five),
        own_share(table_six),
    )


def solution(mesh):
    placed = (
        P(("dp", "rep"), None, None, None),
        P(("dp", "rep"), None, None, None),
        P(("dp", "rep")),
        P(),
        P(),
        P(),
        P("dp", None),
        P(None, "dp", None),
        P("dp", None),
        P("dp", None),
        P(None, None, "dp"),
        P(None, None, "dp"),
        P(None, None, "dp"),
        P(None, None, "dp"),
        P("dp", None),
        P(None, "dp", None),
        P("dp", None),
        P(None, None, "dp"),
        P(None, None, "dp"),
        P(None, None, "dp"),
    )
    return jax.shard_map(
        body,
        mesh=mesh,
        in_specs=placed,
        out_specs=(
            P(("dp", "rep"), None, None, None),
            P(("dp", "rep"), None, None, None),
            P("dp", None),
            P(None, "dp", None),
            P("dp", None),
            P("dp", None),
            P(None, None, "dp"),
            P(None, None, "dp"),
            P(None, None, "dp"),
            P(None, None, "dp"),
            P("dp", None),
            P(None, "dp", None),
            P("dp", None),
            P(None, None, "dp"),
            P(None, None, "dp"),
            P(None, None, "dp"),
        ),
        check_vma=False,
    )
```

profile of v0, /device:TPU:0, one launch (start us, length us, event | category | flops | bytes accessed | tf_op | source)
XLA Modules:
  0.0 2013.2 jit_solution(8201225547146966910)
XLA Ops:
  12.4 33.2 %all_gather.50 = bf16[2,3,512]{1,0,2:T(2,128)(2,1)S(1)} all-gather(bf16[2,3,64]{1,0,2:T(2,128)(2,1)S(1)} %copy.88), channel_id=1, replica_groups=mesh['dp'=8,'rep'=4] {'dp'}, dimensions={2}, use_global_device_ids=true | all-gather | bytes 6912 | tf_op jit(solution)/shard_map/all_gather | solution.py:141
  46.7 31.4 %all_gather.52 = bf16[2,3,512]{1,0,2:T(2,128)(2,1)S(1)} all-gather(bf16[2,3,64]{1,0,2:T(2,128)(2,1)S(1)} %copy.90), channel_id=1, replica_groups=mesh['dp'=8,'rep'=4] {'dp'}, dimensions={2}, use_global_device_ids=true | all-gather | bytes 6912 | tf_op jit(solution)/shard_map/all_gather | solution.py:142
  88.3 42.2 %all-reduce.14 = (f32[3,512]{1,0:T(4,128)S(1)}, f32[3]{0:T(128)S(1)}, f32[3,512]{1,0:T(4,128)S(1)}) all-reduce(f32[3,512]{1,0:T(4,128)S(1)} %fusion.342, f32[3]{0:T(128)S(1)} %convert_reduce_fusion, f32[3,512]{1,0:T(4,128)S(1)} %fusion.344), channel_id=1, replica_groups=mesh['dp'=8,'rep'=4] {'dp','rep'}, use_global_device_ids=true, to_apply=%region_6.7 | all-reduce | flops 3075 | bytes 24600 | tf_op jit(solution)/shard_map/psum | solution.py:159
  146.8 63.5 %all-gather.10.cloned.1.call-done = bf16[9,512,512]{2,1,0:T(8,128)(2,1)} async-done(((bf16[9,64,512]{2,1,0:T(8,128)(2,1)}), bf16[9,512,512]{2,1,0:T(8,128)(2,1)}) %all-gather.10.cloned.1.call-update) | async-done | bytes 4718608 | tf_op jit(solution)/shard_map/all_gather | solution.py:138
  219.3 40.0 %all-reduce.13 = (f32[3,512]{1,0:T(4,128)S(1)}, f32[3,512]{1,0:T(4,128)S(1)}) all-reduce(f32[3,512]{1,0:T(4,128)S(1)} %fusion.336, f32[3,512]{1,0:T(4,128)S(1)} %fusion.338), channel_id=1, replica_groups=mesh['dp'=8,'rep'=4] {'dp','rep'}, use_global_device_ids=true, to_apply=%region_11.12 | all-reduce | flops 3072 | bytes 24576 | tf_op jit(solution)/shard_map/psum | solution.py:159
  330.6 30.9 %all_gather.58 = bf16[2,3,512]{1,0,2:T(2,128)(2,1)S(1)} all-gather(bf16[2,3,64]{1,0,2:T(2,128)(2,1)S(1)} %copy.94), channel_id=1, replica_groups=mesh['dp'=8,'rep'=4] {'dp'}, dimensions={2}, use_global_device_ids=true | all-gather | bytes 6912 | tf_op jit(solution)/shard_map/all_gather | solution.py:152
  361.8 30.9 %all_gather.60 = bf16[2,3,512]{1,0,2:T(2,128)(2,1)S(1)} all-gather(bf16[2,3,64]{1,0,2:T(2,128)(2,1)S(1)} %copy.96), channel_id=1, replica_groups=mesh['dp'=8,'rep'=4] {'dp'}, dimensions={2}, use_global_device_ids=true | all-gather | bytes 6912 | tf_op jit(solution)/shard_map/all_gather | solution.py:153
  453.7 40.2 %all-reduce.11 = (f32[3,512]{1,0:T(4,128)S(1)}, f32[3,512]{1,0:T(4,128)S(1)}) all-reduce(f32[3,512]{1,0:T(4,128)S(1)} %fusion.318, f32[3,512]{1,0:T(4,128)S(1)} %fusion.320), channel_id=1, replica_groups=mesh['dp'=8,'rep'=4] {'dp','rep'}, use_global_device_ids=true, to_apply=%region_24.25 | all-reduce | flops 3072 | bytes 24576 | tf_op jit(solution)/shard_map/psum | solution.py:159
  495.1 35.0 %all-gather.18.cloned.1.call-done = bf16[9,512,512]{2,1,0:T(8,128)(2,1)} async-done(((bf16[9,64,512]{2,1,0:T(8,128)(2,1)}), bf16[9,512,512]{2,1,0:T(8,128)(2,1)}) %all-gather.18.cloned.1.call-update) | async-done | bytes 4718608 | tf_op jit(solution)/shard_map/all_gather | solution.py:150
  539.6 39.4 %all-reduce.10 = (f32[3,512]{1,0:T(4,128)S(1)}, f32[3,512]{1,0:T(4,128)S(1)}) all-reduce(f32[3,512]{1,0:T(4,128)S(1)} %fusion.312, f32[3,512]{1,0:T(4,128)S(1)} %fusion.314), channel_id=1, replica_groups=mesh['dp'=8,'rep'=4] {'dp','rep'}, use_global_device_ids=true, to_apply=%region_28.29 | all-reduce | flops 3072 | bytes 24576 | tf_op jit(solution)/shard_map/psum | solution.py:159
  587.6 40.9 %all-reduce.9 = (f32[3,2048]{1,0:T(4,128)S(1)}, f32[3,2048]{1,0:T(4,128)S(1)}) all-reduce(f32[3,2048]{1,0:T(4,128)S(1)} %fusion.306, f32[3,2048]{1,0:T(4,128)S(1)} %fusion.308), channel_id=1, replica_groups=mesh['dp'=8,'rep'=4] {'dp','rep'}, use_global_device_ids=true, to_apply=%region_32.33 | all-reduce | flops 12288 | bytes 98304 | tf_op jit(solution)/shard_map/psum | solution.py:159
  648.4 40.7 %all-reduce.8 = (f32[3,2048]{1,0:T(4,128)}, f32[3,2048]{1,0:T(4,128)S(1)}) all-reduce(f32[3,2048]{1,0:T(4,128)S(1)} %fusion.295, f32[3,2048]{1,0:T(4,128)S(1)} %fusion.302), channel_id=1, replica_groups=mesh['dp'=8,'rep'=4] {'dp','rep'}, use_global_device_ids=true, to_apply=%region_36.37 | all-reduce | flops 12288 | bytes 98304 | tf_op jit(solution)/shard_map/psum | solution.py:175
  701.3 40.9 %all-reduce.7 = (f32[3,512]{1,0:T(4,128)S(1)}, f32[3,512]{1,0:T(4,128)S(1)}) all-reduce(f32[3,512]{1,0:T(4,128)S(1)} %fusion.285, f32[3,512]{1,0:T(4,128)S(1)} %fusion.292), channel_id=1, replica_groups=mesh['dp'=8,'rep'=4] {'dp','rep'}, use_global_device_ids=true, to_apply=%region_40.41 | all-reduce | flops 3072 | bytes 24576 | tf_op jit(solution)/shard_map/psum | solution.py:175
  760.2 39.9 %all-reduce.6 = (f32[3,512]{1,0:T(4,128)S(1)}, f32[3,512]{1,0:T(4,128)S(1)}) all-reduce(f32[3,512]{1,0:T(4,128)S(1)} %fusion.275, f32[3,512]{1,0:T(4,128)S(1)} %fusion.282), channel_id=1, replica_groups=mesh['dp'=8,'rep'=4] {'dp','rep'}, use_global_device_ids=true, to_apply=%region_45.46 | all-reduce | flops 3072 | bytes 24576 | tf_op jit(solution)/shard_map/psum | solution.py:175
  818.1 40.9 %all-reduce.5 = (f32[3,2048]{1,0:T(4,128)S(1)}, f32[3,2048]{1,0:T(4,128)S(1)}) all-reduce(f32[3,2048]{1,0:T(4,128)S(1)} %fusion.265, f32[3,2048]{1,0:T(4,128)S(1)} %fusion.272), channel_id=1, replica_groups=mesh['dp'=8,'rep'=4] {'dp','rep'}, use_global_device_ids=true, to_apply=%region_49.50 | all-reduce | flops 12288 | bytes 98304 | tf_op jit(solution)/shard_map/psum | solution.py:175
  870.3 40.0 %all-reduce.4 = (f32[3,512]{1,0:T(4,128)S(1)}, f32[3,512]{1,0:T(4,128)S(1)}) all-reduce(f32[3,512]{1,0:T(4,128)S(1)} %fusion.255, f32[3,512]{1,0:T(4,128)S(1)} %fusion.262), channel_id=1, replica_groups=mesh['dp'=8,'rep'=4] {'dp','rep'}, use_global_device_ids=true, to_apply=%region_53.54 | all-reduce | flops 3072 | bytes 24576 | tf_op jit(solution)/shard_map/psum | solution.py:175
  1047.5 40.9 %all-reduce.3 = (f32[3,512]{1,0:T(4,128)S(1)}, f32[3,512]{1,0:T(4,128)S(1)}, f32[3,2048]{1,0:T(4,128)S(1)}) all-reduce(f32[3,512]{1,0:T(4,128)S(1)} %fusion.245, f32[3,512]{1,0:T(4,128)S(1)} %fusion.252, f32[3,2048]{1,0:T(4,128)S(1)} %fusion.238), channel_id=1, replica_groups=mesh['dp'=8,'rep'=4] {'dp','rep'}, use_global_device_ids=true, to_apply=%region_66.67 | all-reduce | flops 9216 | bytes 73728 | tf_op jit(solution)/shard_map/psum | solution.py:175
  1186.5 77.3 %reduce-scatter.20.cloned.1.call-done = f32[64,2048]{1,0:T(8,128)} async-done(((f32[512,2048]{1,0:T(8,128)}), f32[64,2048]{1,0:T(8,128)}) %reduce-scatter.20.cloned.1.call-update) | async-done | bytes 524304 | tf_op jit(solution)/shard_map/reduce_scatter | solution.py:228
  1265.5 90.0 %reduce-scatter.12.cloned.1.call-done = f32[64,2048]{1,0:T(8,128)} async-done(((f32[512,2048]{1,0:T(8,128)}), f32[64,2048]{1,0:T(8,128)}) %reduce-scatter.12.cloned.1.call-update) | async-done | bytes 524304 | tf_op jit(solution)/shard_map/reduce_scatter | solution.py:252
  1357.3 89.6 %reduce-scatter.16.cloned.1.call-done = f32[256,512]{1,0:T(8,128)} async-done(((f32[2048,512]{1,0:T(8,128)}), f32[256,512]{1,0:T(8,128)}) %reduce-scatter.16.cloned.1.call-update) | async-done | bytes 524304 | tf_op jit(solution)/shard_map/reduce_scatter | solution.py:226
  1448.6 151.5 %reduce-scatter.14.cloned.1.call-done = f32[128,2048]{0,1:T(8,128)} async-done(((f32[1024,2048]{0,1:T(8,128)}), f32[128,2048]{0,1:T(8,128)}) %reduce-scatter.14.cloned.1.call-update) | async-done | bytes 1048592 | tf_op jit(solution)/shard_map/reduce_scatter | solution.py:253
  1602.2 164.2 %reduce-scatter.18.cloned.1.call-done = f32[9,64,512]{2,1,0:T(8,128)} async-done(((f32[9,512,512]{2,1,0:T(8,128)}), f32[9,64,512]{2,1,0:T(8,128)}) %reduce-scatter.18.cloned.1.call-update) | async-done | bytes 1179664 | tf_op jit(solution)/shard_map/reduce_scatter | solution.py:227
  1768.6 164.7 %reduce-scatter.10.cloned.1.call-done = f32[9,64,512]{2,1,0:T(8,128)} async-done(((f32[9,512,512]{2,1,0:T(8,128)}), f32[9,64,512]{2,1,0:T(8,128)}) %reduce-scatter.10.cloned.1.call-update) | async-done | bytes 1179664 | tf_op jit(solution)/shard_map/reduce_scatter | solution.py:251
  1959.1 38.2 %all-reduce.21.cloned.1.call-done = (bf16[128,512]{0,1:T(8,128)(2,1)}, bf16[128,2048]{0,1:T(8,128)(2,1)}, bf16[9,64,512]{2,1,0:T(8,128)(2,1)}, bf16[64,2048]{1,0...) async-done(((bf16[128,512]{0,1:T(8,128)(2,1)}, bf16[128,2048]{0,1:T(8,128)(2,1)}, bf16[9,64,512]{2,1,0:T(8,128)(2,1)}, ...) | async-done | bytes 2621456 | tf_op jit(solution)/shard_map/psum | solution.py:256
  (495 shorter events, 551.2 us)
Async XLA Ops:
  7.2 71.1 %all-gather.8.cloned.1.call-start = ((), (), s32[]{:S(2)}) async-start(), calls=%async_computation.7 | async-start | bytes 1179648 | tf_op jit(solution)/shard_map/all_gather | solution.py:137
  7.9 128.6 %all-gather.14.cloned.1.call-start = ((), (), s32[]{:S(2)}) async-start(), calls=%async_computation.10 | async-start | bytes 4718592 | tf_op jit(solution)/shard_map/all_gather | solution.py:140
  8.7 201.6 %all-gather.10.cloned.1.call-start = ((), (), s32[]{:S(2)}) async-start(), calls=%async_computation.8 | async-start | bytes 5308416 | tf_op jit(solution)/shard_map/all_gather | solution.py:138
  9.4 250.9 %all-gather.12.cloned.1.call-start = ((), (), s32[]{:S(2)}) async-start(), calls=%async_computation.9 | async-start | bytes 2359296 | tf_op jit(solution)/shard_map/all_gather | solution.py:139
  10.0 414.6 %all-reduce.19.cloned.1.call-start = ((), (), s32[]{:S(2)}) async-start(), calls=%async_computation.21 | async-start | bytes 262144 | tf_op jit(solution)/shard_map/psum | solution.py:159
  130.5 291.4 %copy-start.92 = (f32[3]{0:T(128)}, f32[3]{0:T(128)S(1)}, u32[]{:S(2)}) copy-start(f32[3]{0:T(128)S(1)} %get-tuple-element.271) | copy-start | bytes 40
  130.6 501.6 %copy-start.90 = (f32[3]{0:T(128)}, f32[3]{0:T(128)S(1)}, u32[]{:S(2)}) copy-start(f32[3]{0:T(128)S(1)} %get-tuple-element.270) | copy-start | bytes 40
  270.3 122.5 %copy-start.82 = (bf16[2,3,256]{2,0,1:T(2,128)(2,1)S(1)}, bf16[2,3,256]{2,0,1:T(2,128)(2,1)}, u32[]{:S(2)}) copy-start(bf16[2,3,256]{2,0,1:T(2,128)(2,1)} %param.57) | copy-start | bytes 9220
  270.3 150.6 %copy-start.94 = (s32[4]{0:T(128)S(1)}, s32[4]{0:T(128)}, u32[]{:S(2)}) copy-start(s32[4]{0:T(128)} %constant.348.clone.1) | copy-start | bytes 52
  273.6 174.5 %all-gather.16.cloned.1.call-start = ((), (), s32[]{:S(2)}) async-start(), calls=%async_computation.11 | async-start | bytes 2359296 | tf_op jit(solution)/shard_map/all_gather | solution.py:149
  274.2 256.0 %all-gather.18.cloned.1.call-start = ((), (), s32[]{:S(2)}) async-start(), calls=%async_computation.12 | async-start | bytes 5308416 | tf_op jit(solution)/shard_map/all_gather | solution.py:150
  274.9 305.0 %all-gather.20.cloned.1.call-start = ((), (), s32[]{:S(2)}) async-start(), calls=%async_computation.13 | async-start | bytes 2359296 | tf_op jit(solution)/shard_map/all_gather | solution.py:151
  275.7 909.2 %reduce-scatter.8.cloned.1.call-start = ((), (), s32[]{:S(2)}) async-start(), calls=%async_computation.14 | async-start | bytes 2359296 | tf_op jit(solution)/shard_map/reduce_scatter | solution.py:250
  579.3 163.4 %copy-start.36 = (f32[16,512]{1,0:T(8,128)}, f32[16,512]{1,0:T(8,128)S(1)}, u32[]{:S(2)}) copy-start(f32[16,512]{1,0:T(8,128)S(1)} %fusion.235) | copy-start | bytes 98308
  634.6 168.3 %copy-start.27 = (f32[16,2048]{1,0:T(8,128)}, f32[16,2048]{1,0:T(8,128)S(1)}, u32[]{:S(2)}) copy-start(f32[16,2048]{1,0:T(8,128)S(1)} %fusion.242) | copy-start | bytes 393220
  912.7 110.3 %copy-start.2 = (bf16[16,7,7,512]{3,0,2,1:T(8,128)(2,1)}, bf16[16,7,7,512]{3,0,2,1:T(8,128)(2,1)S(1)}, u32[]{:S(2)}) copy-start(bf16[16,7,7,512]{3,0,2,1:T(8,128)(2,1)S(1)} %multiply_convert_fusion.4) | copy-start | bytes 2408452
  1104.5 159.3 %reduce-scatter.20.cloned.1.call-start = ((), (), s32[]{:S(2)}) async-start(), calls=%async_computation.20 | async-start | bytes 4718592 | tf_op jit(solution)/shard_map/reduce_scatter | solution.py:228
  1111.7 243.9 %reduce-scatter.12.cloned.1.call-start = ((), (), s32[]{:S(2)}) async-start(), calls=%async_computation.16 | async-start | bytes 4718592 | tf_op jit(solution)/shard_map/reduce_scatter | solution.py:252
  1119.0 327.9 %reduce-scatter.16.cloned.1.call-start = ((), (), s32[]{:S(2)}) async-start(), calls=%async_computation.18 | async-start | bytes 4718592 | tf_op jit(solution)/shard_map/reduce_scatter | solution.py:226
  1127.5 472.7 %reduce-scatter.14.cloned.1.call-start = ((), (), s32[]{:S(2)}) async-start(), calls=%async_computation.17 | async-start | bytes 9437184 | tf_op jit(solution)/shard_map/reduce_scatter | solution.py:253
  1144.0 622.4 %reduce-scatter.18.cloned.1.call-start = ((), (), s32[]{:S(2)}) async-start(), calls=%async_computation.19 | async-start | bytes 10616832 | tf_op jit(solution)/shard_map/reduce_scatter | solution.py:227
  1161.0 772.3 %reduce-scatter.10.cloned.1.call-start = ((), (), s32[]{:S(2)}) async-start(), calls=%async_computation.15 | async-start | bytes 10616832 | tf_op jit(solution)/shard_map/reduce_scatter | solution.py:251
  1179.7 817.7 %all-reduce.21.cloned.1.call-start = ((), (), s32[]{:S(2)}) async-start(), calls=%async_computation.22 | async-start | bytes 5242880 | tf_op jit(solution)/shard_map/psum | solution.py:256
  1602.2 333.3 %copy-start.15 = (bf16[16,14,14,512]{3,0,2,1:T(8,128)(2,1)S(1)}, bf16[16,14,14,512]{3,0,2,1:T(8,128)(2,1)}, u32[]{:S(2)}) copy-start(bf16[16,14,14,512]{3,0,2,1:T(8,128)(2,1)} %copy-done.14) | copy-start | bytes 9633796
  (97 other events, 1508.8 us)
Sparse Core Ops, SparseCore 0:
  10.1 43.8 all-gather.7
  56.2 73.6 all-gather.13
  132.1 78.1 all-gather.9
  212.3 47.9 all-gather.11
  273.7 123.8 all-reduce.18
  399.6 48.4 all-gather.15
  450.3 79.8 all-gather.17
  532.3 47.5 all-gather.19
  1104.6 68.6 reduce-scatter.7
  1176.8 86.9 reduce-scatter.19
  1267.8 87.6 reduce-scatter.11
  1359.0 87.8 reduce-scatter.15
  1450.9 149.1 reduce-scatter.13
  1603.6 162.8 reduce-scatter.17
  1770.5 162.8 reduce-scatter.9
  1937.2 60.1 all-reduce.20
where the time goes:
time: 2020 us; the launch traced here: 2010 us
  waiting for transfers between devices  890 us (44%)
  blocking collectives  650 us (32%)
  matrix products  228 us (11%)
  other arithmetic  200 us (10%)
  local copies, waits for them, and re-layouts  26.8 us (1%)
    psum x6, blocking collectives, normalize_back(): gain_total, bias_total = lax.psum((local_gain, local_bias), ('dp', 'rep'))  243 us
    psum x5, blocking collectives, normalize(): lax.psum((group_sums(masked, onehot), group_sums(masked * values, onehot)...  203 us
    reduce_scatter x1, waiting for transfers between devices, body(): lax.psum_scatter(grad_entry_spatial, 'dp', scatter_dimension=1, tiled=True)  165 us
    reduce_scatter x1, waiting for transfers between devices, body(): lax.psum_scatter(grad_inner_spatial, 'dp', scatter_dimension=1, tiled=True)  164 us
    reduce_scatter x1, waiting for transfers between devices, body(): lax.psum_scatter(grad_entry_project, 'dp', scatter_dimension=0, tiled=True)  151 us
    scatter-add x9, other arithmetic, conv_three_back(): spread_back = spread_back.at[:, vertical:vertical + extent:stride, latera...  93.8 us
    reduce_scatter x1, waiting for transfers between devices, body(): lax.psum_scatter(grad_entry_expand, 'dp', scatter_dimension=0, tiled=True)  90 us
    reduce_scatter x1, waiting for transfers between devices, body(): lax.psum_scatter(grad_inner_reduce, 'dp', scatter_dimension=0, tiled=True)  89.6 us
  transfers between devices with their start and end apart: 16, of which 12 were waited for; matrix products, arithmetic and copies ran while one was open for 9% of the time, Pallas kernels for 0%

commit v1 on v0

v1 whole, which is shorter than its diff:
```python
import functools

import jax
import jax.numpy as jnp
from jax import lax
from jax.experimental import pallas as pl
from jax.experimental.pallas import tpu as pltpu
from jax.sharding import PartitionSpec as P

EPSILON = 1e-05
AXES = ("dp", "rep")
BF = jnp.bfloat16
F32 = jnp.float32
GROUPS = 3
LANES = 512
VMEM = 56 * 1024 * 1024


def xor_swap(value, distance):
    count = lax.axis_size("dp") * lax.axis_size("rep")
    return lax.ppermute(value, AXES, [(d, d ^ distance) for d in range(count)])


def sum_everywhere(value):
    count = lax.axis_size("dp") * lax.axis_size("rep")
    bits = [1 << b for b in range(count.bit_length() - 1)]
    stages = [bits[:1]] + [bits[i : i + 2] for i in range(1, len(bits), 2)]
    for stage in stages:
        distances = [0]
        for bit in stage:
            distances = distances + [d | bit for d in distances]
        parts = [xor_swap(value, d) for d in distances[1:]]
        for part in parts:
            value = value + part
    return value


def gelu_parts(u):
    k = 0.7978845608028654
    square = u * u
    t = jnp.tanh(k * u * (1.0 + 0.044715 * square))
    half = 0.5 * (1.0 + t)
    slope = half + 0.5 * u * (1.0 - t * t) * (k + (3 * 0.044715 * k) * square)
    return u * half, slope


def dot(a, b):
    return lax.dot_general(a, b, (((1,), (0,)), ((), ())), preferred_element_type=F32)


def dot_nt(a, b):
    return lax.dot_general(a, b, (((1,), (1,)), ((), ())), preferred_element_type=F32)


def dot_tn(a, b):
    return lax.dot_general(a, b, (((0,), (0,)), ((), ())), preferred_element_type=F32)


def flat(field):
    return field.reshape(-1, field.shape[-1])


def whole(shape):
    return pl.BlockSpec(shape, lambda *_: (0,) * len(shape))


def along(shape, axis):
    return pl.BlockSpec(shape, lambda s: tuple(s if a == axis else 0 for a in range(len(shape))))


def call(kernel, name, steps, ins, outs, scratch=(), flops=0):
    arrays = [a for a, _ in ins]
    size = sum(a.size * a.dtype.itemsize for a in arrays)
    return pl.pallas_call(
        kernel,
        name=name,
        grid=(steps,),
        in_specs=[s for _, s in ins],
        out_specs=[s for _, _, s in outs],
        out_shape=[jax.ShapeDtypeStruct(shape, dtype) for shape, dtype, _ in outs],
        scratch_shapes=list(scratch),
        compiler_params=pltpu.CompilerParams(
            vmem_limit_bytes=VMEM, dimension_semantics=("arbitrary",)
        ),
        cost_estimate=pl.CostEstimate(flops=flops, bytes_accessed=size, transcendentals=0),
    )(*arrays)


def rows3(ref, first):
    return [ref[first + g : first + g + 1, :] for g in range(GROUPS)]


def spread(onehot, rows):
    total = onehot[0] * rows[0]
    for g in range(1, GROUPS):
        total = total + onehot[g] * rows[g]
    return total


def group_rows(onehot, *sums):
    rows = [
        jnp.sum(onehot[g] * image, axis=0, keepdims=True) for image in sums for g in range(GROUPS)
    ]
    return rows


def put_rows(ref, rows):
    for r, row in enumerate(rows):
        ref[r : r + 1, :] = row
    if len(rows) < ref.shape[0]:
        ref[len(rows) :, :] = jnp.zeros((ref.shape[0] - len(rows), ref.shape[1]), F32)


def moments(sums, counts):
    first, second, count = rows3(sums, 0), rows3(sums, GROUPS), rows3(counts, 0)
    center = [a / c for a, c in zip(first, count)]
    inverse = [lax.rsqrt(b / c - m * m + EPSILON) for b, c, m in zip(second, count, center)]
    return center, inverse


def forward_coefs(sums, table, counts, onehot):
    center, inverse = moments(sums, counts)
    scale = [a * i for a, i in zip(rows3(table, 0), inverse)]
    shift = [b - m * s for b, m, s in zip(rows3(table, GROUPS), center, scale)]
    return spread(onehot, scale), spread(onehot, shift)


def backward_coefs(sums, back, table, counts, onehot, gain_at=0):
    center, inverse = moments(sums, counts)
    count = rows3(counts, 0)
    factor = [a * i for a, i in zip(rows3(table, 0), inverse)]
    gain = [g / c for g, c in zip(rows3(back, gain_at), count)]
    bias = [b / c for b, c in zip(rows3(back, GROUPS), count)]
    on_z = [-f * i * g for f, i, g in zip(factor, inverse, gain)]
    on_one = [f * (m * i * g - b) for f, m, i, g, b in zip(factor, center, inverse, gain, bias)]
    return spread(onehot, factor), spread(onehot, on_z), spread(onehot, on_one)


def gain_rows(sums, counts, onehot, with_z, plain):
    center, inverse = moments(sums, counts)
    raw_z, raw = group_rows(onehot, with_z), group_rows(onehot, plain)
    return [i * (e - m * d) for i, e, m, d in zip(inverse, raw_z, center, raw)]


def inside(limits, row, count, step=1, start=0):
    column = lax.broadcasted_iota(jnp.int32, (count,) + limits.shape, 0) * step + start
    return (column < limits[None]) & (row < limits)[None]


def add_stats(values, mask, first, second):
    kept = jnp.where(mask, values, 0.0)
    return first + jnp.sum(kept, axis=0), second + jnp.sum(kept * values, axis=0)


def k_first(x, w, limits, onehot, count_row, z, sums, acc):
    step = pl.program_id(0)

    @pl.when(step == 0)
    def _():
        acc[...] = jnp.zeros_like(acc)

    rows, cols = x.shape[0], x.shape[1]
    values = dot(flat(x[...]), w[...]).reshape(rows, cols, x.shape[2], w.shape[1])
    z[...] = values.astype(BF)
    first, second = acc[0], acc[1]
    for r in range(rows):
        mask = inside(limits[...], step * rows + r, cols)
        first, second = add_stats(values[r], mask, first, second)
    acc[0] = first
    acc[1] = second

    @pl.when(step == pl.num_programs(0) - 1)
    def _():
        put_rows(sums, group_rows(onehot, first, second) + [count_row[0:1, :]])


def stats_of(field, limits, onehot, z, sums):
    side = field.shape[0]
    shape = field.shape[2:]

    def row(i, carry):
        values = field[i]
        z[i] = values.astype(BF)
        return add_stats(values, inside(limits[...], i, side), *carry)

    first, second = lax.fori_loop(
        0, side, row, (jnp.zeros(shape, F32), jnp.zeros(shape, F32))
    )
    put_rows(sums, group_rows(onehot, first, second))


def k_strided(x, w, limits, onehot, z, sums, acc):
    side = z.shape[0]
    acc[...] = dot(flat(x[:, 0, :, 0]), w[0]).reshape(acc.shape)
    stats_of(acc, limits, onehot, z, sums)


def k_entry_spatial(
    z1, in_sums, table, counts, counts_out, limits, limits_out, onehot, w,
    planes, slope, z2, sums, acc,
):
    step = pl.program_id(0)
    side = z2.shape[0]

    @pl.when(step == 0)
    def _():
        planes[1, :, 0] = jnp.zeros(planes.shape[1:2] + planes.shape[3:], BF)
        planes[:, 1, :, 0] = jnp.zeros(planes.shape[:1] + planes.shape[2:3] + planes.shape[4:], BF)

    scale, shift = forward_coefs(in_sums, table, counts, onehot)
    for a in range(2):
        for b in range(2):
            u = z1[0, a, :, b].astype(F32) * scale + shift
            act, grad = gelu_parts(u)
            mask = inside(limits[...], 2 * step + a, side, 2, b)
            planes[a, b, step + a, b : b + side] = jnp.where(mask, act, 0.0).astype(BF)
            slope[0, a, :, b] = jnp.where(mask, grad, 0.0).astype(BF)

    @pl.when(step == pl.num_programs(0) - 1)
    def _():
        for t in range(9):
            v, h = t // 3, t % 3
            rows = planes[(v + 1) % 2, (h + 1) % 2, v // 2 : v // 2 + side, h // 2 : h // 2 + side]
            part = dot(flat(rows), w[t]).reshape(acc.shape)
            if t == 0:
                acc[...] = part
            else:
                acc[...] += part
        stats_of(acc, limits_out, onehot, z2, sums)


def activate(z, coefs, limits, store):
    scale, shift = coefs
    side = z.shape[0]

    def row(i, carry):
        act, grad = gelu_parts(z[i].astype(F32) * scale + shift)
        mask = inside(limits[...], i, side)
        store(i, jnp.where(mask, act, 0.0).astype(BF), jnp.where(mask, grad, 0.0).astype(BF))
        return carry

    lax.fori_loop(0, side, row, 0)


def k_expand(z, in_sums, table, counts, keeps, limits, onehot, w, a, slope, z_out, sums, acc):
    @pl.when(pl.program_id(0) == 0)
    def _():
        def store(i, act, grad):
            a[i] = act
            slope[i] = grad

        activate(z, forward_coefs(in_sums, table, counts, onehot), keeps, store)

    acc[...] = dot(flat(a[...]), w[0]).reshape(acc.shape)
    stats_of(acc, limits, onehot, z_out, sums)


def k_middle(
    z3, zs, sums3, sums_s, table3, table_s, counts, limits, onehot, w,
    middle, slope, z4, sums, acc,
):
    step = pl.program_id(0)
    side = z3.shape[0]
    scale, shift = forward_coefs(sums3, table3, counts, onehot)
    scale_s, shift_s = forward_coefs(sums_s, table_s, counts, onehot)
    shift = shift + shift_s

    def row(i, carry):
        act, grad = gelu_parts(z3[i].astype(F32) * scale + zs[i].astype(F32) * scale_s + shift)
        mask = inside(limits[...], i, side)
        middle[i] = jnp.where(mask, act, 0.0).astype(BF)
        slope[i] = jnp.where(mask, grad, 0.0).astype(BF)
        return carry

    lax.fori_loop(0, side, row, 0)
    part = dot(flat(middle[...]), w[...]).reshape(acc.shape)

    @pl.when(step == 0)
    def _():
        acc[...] = part

    @pl.when(step > 0)
    def _():
        acc[...] += part

    @pl.when(step == pl.num_programs(0) - 1)
    def _():
        stats_of(acc, limits, onehot, z4, sums)


def clear_edges(padded):
    edge = jnp.zeros(padded.shape[1:], BF)
    last = padded.shape[0] - 1
    padded[0] = edge
    padded[last] = edge
    for i in range(1, last):
        padded[i, 0] = edge[0]
        padded[i, last] = edge[0]


def k_inner_spatial(z4, in_sums, table, counts, keeps, limits, onehot, w, padded, slope, z5, sums, acc):
    side = z4.shape[0]
    clear_edges(padded)

    def store(i, act, grad):
        padded[i + 1, 1 : 1 + side] = act
        slope[i] = grad

    activate(z4, forward_coefs(in_sums, table, counts, onehot), keeps, store)
    for t in range(9):
        v, h = t // 3, t % 3
        part = dot(flat(padded[v : v + side, h : h + side]), w[t]).reshape(acc.shape)
        if t == 0:
            acc[...] = part
        else:
            acc[...] += part
    stats_of(acc, limits, onehot, z5, sums)


def k_close(z6, in_sums, table, counts, limits, onehot, gate, middle, cot, result, du6, sums):
    side = z6.shape[0]
    scale, shift = forward_coefs(in_sums, table, counts, onehot)
    opened = gate[...]
    zero = jnp.zeros(opened.shape, F32)

    def row(i, carry):
        plain, with_z = carry
        z = z6[i].astype(F32)
        mid = middle[i].astype(F32)
        act, grad = gelu_parts(z * scale + shift + mid)
        mask = inside(limits[...], i, side)
        closed = jnp.where(mask, act, 0.0)
        result[i] = (mid + opened * (closed - mid)).astype(BF)
        du = jnp.where(mask, grad, 0.0) * opened * cot[i].astype(F32)
        du6[i] = du.astype(BF)
        return plain + jnp.sum(du, axis=0), with_z + jnp.sum(du * z, axis=0)

    plain, with_z = lax.fori_loop(0, side, row, (zero, zero))
    put_rows(
        sums,
        gain_rows(in_sums, counts, onehot, with_z, plain) + group_rows(onehot, plain),
    )


def finish_back(acc, slope, z, in_sums, counts, onehot, du_out, sums):
    zero = jnp.zeros(slope.shape[2:], F32)

    def row(i, carry):
        plain, with_z = carry
        du = acc[i] * slope[i].astype(F32)
        du_out[i] = du.astype(du_out.dtype)
        return plain + jnp.sum(du, axis=0), with_z + jnp.sum(du * z[i].astype(F32), axis=0)

    plain, with_z = lax.fori_loop(0, slope.shape[0], row, (zero, zero))
    put_rows(
        sums,
        gain_rows(in_sums, counts, onehot, with_z, plain) + group_rows(onehot, plain),
    )


def norm_back(du, z, coefs, limits, store):
    factor, on_z, on_one = coefs
    side = z.shape[0]

    def row(i, carry):
        dz = du[i].astype(F32) * factor + z[i].astype(F32) * on_z + on_one
        store(i, jnp.where(inside(limits[...], i, side), dz, 0.0).astype(BF))
        return carry

    lax.fori_loop(0, side, row, 0)


def k_back_expand(
    du6, z6, sums6, back6, table6, counts, limits, onehot, w, slope, z5, sums5,
    dz6, du5, sums, acc,
):
    step = pl.program_id(0)

    def store(i, dz):
        dz6[i] = dz

    norm_back(du6, z6, backward_coefs(sums6, back6, table6, counts, onehot), limits, store)
    part = dot_nt(flat(dz6[...]), w[0]).reshape(acc.shape)

    @pl.when(step == 0)
    def _():
        acc[...] = part

    @pl.when(step > 0)
    def _():
        acc[...] += part

    @pl.when(step == pl.num_programs(0) - 1)
    def _():
        finish_back(acc, slope, z5, sums5, counts, onehot, du5, sums)


def k_back_inner_spatial(
    du5, z5, sums5, back5, table5, counts, limits, onehot, w, slope, z4, sums4,
    dz5, du4, sums, padded, acc,
):
    side = z5.shape[0]
    clear_edges(padded)

    def store(i, dz):
        dz5[i] = dz
        padded[i + 1, 1 : 1 + side] = dz

    norm_back(du5, z5, backward_coefs(sums5, back5, table5, counts, onehot), limits, store)
    for t in range(9):
        v, h = t // 3, t % 3
        rows = padded[2 - v : 2 - v + side, 2 - h : 2 - h + side]
        part = dot_nt(flat(rows), w[t]).reshape(acc.shape)
        if t == 0:
            acc[...] = part
        else:
            acc[...] += part
    finish_back(acc, slope, z4, sums4, counts, onehot, du4, sums)


def k_back_middle(
    du4, z4, sums4, back4, table4, counts, limits, onehot, w, gate, cot, du6, slope3,
    z3, zs, sums3, sums_s, dz4, du3, sums, acc,
):
    side = z4.shape[0]

    @pl.when(pl.program_id(0) == 0)
    def _():
        def store(i, dz):
            dz4[i] = dz

        norm_back(du4, z4, backward_coefs(sums4, back4, table4, counts, onehot), limits, store)

    acc[...] = dot_nt(flat(dz4[...]), w[...]).reshape(acc.shape)
    shut = 1.0 - gate[...]
    zero = jnp.zeros(shut.shape, F32)

    def row(i, carry):
        plain, with_z3, with_zs = carry
        grad = shut * cot[i].astype(F32) + du6[i].astype(F32) + acc[i]
        du = grad * slope3[i].astype(F32)
        du3[i] = du.astype(BF)
        return (
            plain + jnp.sum(du, axis=0),
            with_z3 + jnp.sum(du * z3[i].astype(F32), axis=0),
            with_zs + jnp.sum(du * zs[i].astype(F32), axis=0),
        )

    plain, with_z3, with_zs = lax.fori_loop(0, side, row, (zero, zero, zero))
    put_rows(
        sums,
        gain_rows(sums3, counts, onehot, with_z3, plain)
        + group_rows(onehot, plain)
        + gain_rows(sums_s, counts, onehot, with_zs, plain),
    )


def k_back_entry_expand(
    du3, z3, zs, sums3, sums_s, back3, table3, table_s, counts, limits, onehot, w,
    slope, z2, sums2, dz3, dzs, du2, sums, acc,
):
    step = pl.program_id(0)
    side = z3.shape[0]
    factor, on_z, on_one = backward_coefs(sums3, back3, table3, counts, onehot)
    factor_s, on_zs, on_one_s = backward_coefs(
        sums_s, back3, table_s, counts, onehot, 2 * GROUPS
    )

    def row(i, carry):
        du = du3[i].astype(F32)
        mask = inside(limits[...], i, side)
        dz = du * factor + z3[i].astype(F32) * on_z + on_one
        dz3[i] = jnp.where(mask, dz, 0.0).astype(BF)
        dz = du * factor_s + zs[i].astype(F32) * on_zs + on_one_s
        dzs[i] = jnp.where(mask, dz, 0.0).astype(BF)
        return carry

    lax.fori_loop(0, side, row, 0)
    part = dot_nt(flat(dz3[...]), w[0]).reshape(acc.shape)

    @pl.when(step == 0)
    def _():
        acc[...] = part

    @pl.when(step > 0)
    def _():
        acc[...] += part

    @pl.when(step == pl.num_programs(0) - 1)
    def _():
        finish_back(acc, slope, z2, sums2, counts, onehot, du2, sums)


def k_back_strided(dzs, w, out):
    part = dot_nt(flat(dzs[...]), w[0]).reshape(out.shape)

    @pl.when(pl.program_id(0) == 0)
    def _():
        out[...] = part

    @pl.when(pl.program_id(0) > 0)
    def _():
        out[...] += part


def k_back_entry_spatial(
    du2, z2, sums2, back2, table2, counts, counts_in, limits, onehot, w, slope, z1, sums1,
    dz2, du1, sums, padded, total, acc,
):
    step = pl.program_id(0)
    side = z2.shape[0]

    @pl.when(step == 0)
    def _():
        total[...] = jnp.zeros_like(total)
        padded[...] = jnp.zeros_like(padded)

        def store(i, dz):
            dz2[i] = dz
            padded[i, 0:side] = dz

        norm_back(du2, z2, backward_coefs(sums2, back2, table2, counts, onehot), limits, store)

    steps = {0: [(1, 0)], 1: [(2, 0), (0, 1)]}
    for a in range(2):
        for b in range(2):

            @pl.when(step == 2 * a + b)
            def _():
                started = False
                for v, down in steps[a]:
                    for h, right in steps[b]:
                        rows = padded[down : down + side, right : right + side]
                        part = dot_nt(flat(rows), w[3 * v + h]).reshape(acc.shape)
                        if started:
                            acc[...] += part
                        else:
                            acc[...] = part
                        started = True

    def row(i, carry):
        plain, with_z = carry
        du = acc[i] * slope[i, 0, :, 0].astype(F32)
        du1[i, 0, :, 0] = du.astype(BF)
        z = z1[i, 0, :, 0].astype(F32)
        return plain + jnp.sum(du, axis=0), with_z + jnp.sum(du * z, axis=0)

    plain, with_z = lax.fori_loop(0, side, row, (total[0], total[1]))
    total[0] = plain
    total[1] = with_z

    @pl.when(step == pl.num_programs(0) - 1)
    def _():
        put_rows(
            sums,
            gain_rows(sums1, counts_in, onehot, with_z, plain) + group_rows(onehot, plain),
        )


def k_back_first(du1, z1, sums1, back1, table1, counts, limits, onehot, w, strided, dz1, dx):
    step = pl.program_id(0)
    rows, cols = du1.shape[0], du1.shape[1]
    factor, on_z, on_one = backward_coefs(sums1, back1, table1, counts, onehot)
    for r in range(rows):
        dz = du1[r].astype(F32) * factor + z1[r].astype(F32) * on_z + on_one
        mask = inside(limits[...], rows * step + r, cols)
        dz1[r] = jnp.where(mask, dz, 0.0).astype(BF)
    for r in range(rows):
        part = dot_nt(flat(dz1[r]), w[...]).reshape(dx.shape[1:])
        dx[r] = part
    for j in range(cols // 2):
        dx[0, 2 * j] += strided[0, j]


def k_taps(field, dz, out):
    t = pl.program_id(0)
    v, h = t // 3, t % 3
    side = dz.shape[0]
    rows = field[pl.ds(v, side), pl.ds(h, side)]
    out[0] = dot_tn(flat(rows), flat(dz[...])).astype(BF)


def k_taps_strided(planes, dz, out):
    t = pl.program_id(0)
    v, h = t // 3, t % 3
    side = dz.shape[0]
    rows = planes[(v + 1) % 2, (h + 1) % 2, pl.ds(v // 2, side), pl.ds(h // 2, side)]
    out[0] = dot_tn(flat(rows), flat(dz[...])).astype(BF)


def body(
    inputs,
    cotangent,
    image_group,
    group_side,
    group_width,
    group_depth,
    entry_reduce,
    entry_spatial,
    entry_expand,
    entry_project,
    entry_norm_reduce,
    entry_norm_spatial,
    entry_norm_expand,
    entry_norm_project,
    inner_reduce,
    inner_spatial,
    inner_expand,
    inner_norm_reduce,
    inner_norm_spatial,
    inner_norm_expand,
):
    images, full, _, wide = inputs.shape
    half = full // 2
    mid, out = entry_reduce.shape[1], entry_expand.shape[1]
    blocks = out // LANES
    shards, copies = lax.axis_size("dp"), lax.axis_size("rep")
    devices = shards * copies
    position, copy = lax.axis_index("dp"), lax.axis_index("rep")

    onehot_int = (image_group[None, :] == jnp.arange(GROUPS, dtype=jnp.int32)[:, None]).astype(
        jnp.int32
    )
    own_side = jnp.sum(onehot_int * group_side[:, None], axis=0)
    own_width = jnp.sum(onehot_int * group_width[:, None], axis=0)
    own_gate = jnp.sum(onehot_int * group_depth[:, None], axis=0)

    def lanes(vector):
        return jnp.broadcast_to(vector[:, None], (images, LANES))

    onehot = jnp.broadcast_to(
        onehot_int.astype(F32)[:, :, None], (GROUPS, images, LANES)
    )
    gate = lanes(own_gate).astype(F32)
    limits_in, limits_out = lanes(own_side), lanes(own_side // 2)
    kept = jnp.arange(mid, dtype=jnp.int32)[None, :] < (own_width * mid // 4)[:, None]
    keeps_in = jnp.where(kept, limits_in, 0)
    keeps_out = jnp.where(kept, limits_out, 0)

    def quarter(weights):
        rows = weights.shape[-2] // copies
        part = lax.dynamic_slice_in_dim(weights, copy * rows, rows, weights.ndim - 2)
        part = part.reshape((-1,) + part.shape[-2:])
        return jnp.concatenate(
            [part[..., i : i + LANES] for i in range(0, part.shape[-1], LANES)], axis=0
        )

    def gather_weights(weights):
        parts = [quarter(w) for w in weights]
        rows = jnp.concatenate([flat(p) for p in parts], axis=0)
        gathered = lax.all_gather(rows, AXES, axis=0, tiled=False)
        result, at = [], 0
        for p in parts:
            size = p.shape[0] * p.shape[1]
            field = gathered[:, at : at + size].reshape((devices,) + p.shape)
            result.append(field.transpose(1, 0, 2, 3).reshape(p.shape[0], -1, LANES))
            at += size
        return result

    def scatter_grads(grads, shapes):
        parts = []
        for g in grads:
            q = g.shape[1] // devices
            field = g.reshape(g.shape[0], devices, q, LANES).transpose(1, 0, 2, 3)
            parts.append(field.reshape(devices, -1, LANES))
        rows = jnp.concatenate(parts, axis=1).reshape(-1, LANES)
        own = lax.psum_scatter(rows, AXES, scatter_dimension=0, tiled=True)
        gathered = lax.all_gather(own, "rep", axis=0, tiled=False)
        result, at = [], 0
        for g, shape in zip(grads, shapes):
            t, q = g.shape[0], g.shape[1] // devices
            field = gathered[:, at : at + t * q].reshape(copies, t, q, LANES)
            if len(shape) == 3:
                field = field.transpose(1, 0, 2, 3)
            else:
                field = field.transpose(0, 2, 1, 3)
            result.append(field.reshape(shape).astype(F32))
            at += t * q
        return result

    tables_all = (
        entry_norm_reduce,
        entry_norm_spatial,
        entry_norm_expand,
        entry_norm_project,
        inner_norm_reduce,
        inner_norm_spatial,
        inner_norm_expand,
    )
    w_reduce = lax.all_gather(entry_reduce, "dp", axis=0, tiled=True)
    tables_flat = jnp.concatenate([t.reshape(2 * GROUPS, -1) for t in tables_all], axis=1)
    tables_flat = lax.all_gather(tables_flat, "dp", axis=0, tiled=False)
    tables, at = [], 0
    for t in tables_all:
        width = t.shape[2]
        field = tables_flat[:, :, at : at + width].transpose(1, 0, 2)
        tables.append(field.reshape(2 * GROUPS, shards * width).astype(F32))
        at += width
    w_spatial, w_expand, w_project, w_ireduce, w_ispatial, w_iexpand = gather_weights(
        [entry_spatial, entry_expand, entry_project, inner_reduce, inner_spatial, inner_expand]
    )
    w_ireduce = w_ireduce[0]

    x = inputs.transpose(1, 2, 0, 3)
    x_split = x.reshape(half, 2, half, 2, images, wide)
    cot = cotangent.transpose(1, 2, 0, 3)

    small = (half, half, images, LANES)
    large = (half, half, images, out)
    split = (half, 2, half, 2, images, LANES)
    rows_out, rows_in = half * half * images, full * full * images
    six = (2 * GROUPS, LANES)
    sums_block = (8, LANES)

    def fixed(array):
        return (array, whole(array.shape))

    def column(array):
        return (array, along(array.shape[:-1] + (LANES,), array.ndim - 1))

    def tap(array):
        return (array, along((1,) + array.shape[1:], 0))

    small_out = (small, BF, whole(small))
    large_out = (large, BF, along(small, 3))
    sums_out = ((8, LANES), F32, whole((8, LANES)))
    sums_wide = ((8, out), F32, along((8, LANES), 1))
    acc = pltpu.VMEM(small, F32)

    count_row = jnp.concatenate(
        [
            jnp.broadcast_to(jnp.sum(onehot_int[g]).astype(F32), (1, 128))
            for g in range(GROUPS)
        ]
        + [jnp.zeros((1, LANES - 128 * GROUPS), F32)],
        axis=1,
    )
    z1, sums1 = call(
        k_first, "first", half,
        [(x, along((2, full, images, wide), 0)), fixed(w_reduce), fixed(limits_in), fixed(onehot),
         fixed(count_row)],
        [((full, full, images, mid), BF, along((2, full, images, mid), 0)), sums_out],
        [pltpu.VMEM((2, images, mid), F32)], flops=2 * rows_in * wide * mid,
    )
    sums1 = sum_everywhere(sums1)
    totals = sums1[2 * GROUPS, 0 : 128 * GROUPS : 128]
    side_real = group_side.astype(F32)
    half_real = (group_side // 2).astype(F32)
    counts_in = jnp.broadcast_to((totals * side_real * side_real)[:, None], (GROUPS, LANES))
    counts = jnp.broadcast_to((totals * half_real * half_real)[:, None], (GROUPS, LANES))
    counts_in, counts = fixed(counts_in), fixed(counts)
    onehot, gate = fixed(onehot), fixed(gate)
    limits_in, limits_out = fixed(limits_in), fixed(limits_out)
    keeps_in, keeps_out = fixed(keeps_in), fixed(keeps_out)

    zs, sums_s = call(
        k_strided, "strided", blocks,
        [(x_split, whole((half, 1, half, 1, images, wide))), tap(w_project), limits_out, onehot],
        [large_out, sums_wide], [acc], flops=2 * rows_out * wide * out,
    )
    z1_split = z1.reshape(split)
    row_split = (1, 2, half, 2, images, LANES)
    planes_shape = (2, 2, half + 1, half + 1, images, mid)
    planes, slope1, z2, sums2 = call(
        k_entry_spatial, "entry_spatial", half,
        [(z1_split, along(row_split, 0)), fixed(sums1), fixed(tables[0]), counts_in, counts,
         keeps_in, limits_out, onehot, fixed(w_spatial)],
        [(planes_shape, BF, whole(planes_shape)), (split, BF, along(row_split, 0)), small_out,
         sums_out],
        [acc], flops=18 * rows_out * mid * mid,
    )
    sums2 = sum_everywhere(sums2)
    a2, slope2, z3, sums3 = call(
        k_expand, "expand", blocks,
        [fixed(z2), fixed(sums2), fixed(tables[1]), counts, keeps_out, limits_out, onehot,
         tap(w_expand)],
        [small_out, small_out, large_out, sums_wide], [acc], flops=2 * rows_out * mid * out,
    )
    joined = sum_everywhere(jnp.concatenate([sums3, sums_s], axis=1))
    sums3, sums_s = joined[:, :out], joined[:, out:]
    w_rows = (w_ireduce, along((LANES, mid), 0))
    middle, slope3, z4, sums4 = call(
        k_middle, "middle", blocks,
        [column(z3), column(zs), column(sums3), column(sums_s), column(tables[2]),
         column(tables[3]), counts, limits_out, onehot, w_rows],
        [large_out, large_out, small_out, sums_out], [acc], flops=2 * rows_out * mid * out,
    )
    sums4 = sum_everywhere(sums4)
    padded_shape = (half + 2, half + 2, images, mid)
    padded4, slope4, z5, sums5 = call(
        k_inner_spatial, "inner_spatial", 1,
        [fixed(z4), fixed(sums4), fixed(tables[4]), counts, keeps_out, limits_out, onehot,
         fixed(w_ispatial)],
        [(padded_shape, BF, whole(padded_shape)), small_out, small_out, sums_out], [acc],
        flops=18 * rows_out * mid * mid,
    )
    sums5 = sum_everywhere(sums5)
    a5, slope5, z6, sums6 = call(
        k_expand, "inner_expand", blocks,
        [fixed(z5), fixed(sums5), fixed(tables[5]), counts, keeps_out, limits_out, onehot,
         tap(w_iexpand)],
        [small_out, small_out, large_out, sums_wide], [acc], flops=2 * rows_out * mid * out,
    )
    sums6 = sum_everywhere(sums6)
    result, du6, back6 = call(
        k_close, "close", blocks,
        [column(z6), column(sums6), column(tables[6]), counts, limits_out, onehot, gate,
         column(middle), column(cot)],
        [large_out, large_out, sums_wide],
    )
    back6 = sum_everywhere(back6)
    dz6, du5, back5 = call(
        k_back_expand, "back_inner_expand", blocks,
        [column(du6), column(z6), column(sums6), column(back6), column(tables[6]), counts,
         limits_out, onehot, tap(w_iexpand), fixed(slope5), fixed(z5), fixed(sums5)],
        [large_out, (small, F32, whole(small)), sums_out], [acc],
        flops=2 * rows_out * mid * out,
    )
    back5 = sum_everywhere(back5)
    g_iexpand = weight_blocks(a5, dz6)
    dz5, du4, back4 = call(
        k_back_inner_spatial, "back_inner_spatial", 1,
        [fixed(du5), fixed(z5), fixed(sums5), fixed(back5), fixed(tables[5]), counts, limits_out,
         onehot, fixed(w_ispatial), fixed(slope4), fixed(z4), fixed(sums4)],
        [small_out, (small, F32, whole(small)), sums_out],
        [pltpu.VMEM(padded_shape, BF), acc], flops=18 * rows_out * mid * mid,
    )
    back4 = sum_everywhere(back4)
    taps_out = ((9, mid, mid), BF, along((1, mid, mid), 0))
    (g_ispatial,) = call(
        k_taps, "inner_spatial_grad", 9, [fixed(padded4), fixed(dz5)], [taps_out],
        flops=18 * rows_out * mid * mid,
    )
    dz4, du3, back3 = call(
        k_back_middle, "back_middle", blocks,
        [fixed(du4), fixed(z4), fixed(sums4), fixed(back4), fixed(tables[4]), counts, limits_out,
         onehot, w_rows, gate, column(cot), column(du6), column(slope3), column(z3), column(zs),
         column(sums3), column(sums_s)],
        [small_out, large_out, ((16, out), F32, along((16, LANES), 1))], [acc],
        flops=2 * rows_out * mid * out,
    )
    back3 = sum_everywhere(back3)
    g_ireduce = dot_tn(flat(middle), flat(dz4)).astype(BF)[None]
    inner_grads = scatter_grads(
        (g_ireduce, g_ispatial, g_iexpand),
        (inner_reduce.shape, inner_spatial.shape, inner_expand.shape),
    )
    dz3, dzs, du2, back2 = call(
        k_back_entry_expand, "back_entry_expand", blocks,
        [column(du3), column(z3), column(zs), column(sums3), column(sums_s), column(back3),
         column(tables[2]), column(tables[3]), counts, limits_out, onehot, tap(w_expand),
         fixed(slope2), fixed(z2), fixed(sums2)],
        [large_out, large_out, (small, F32, whole(small)), sums_out], [acc],
        flops=2 * rows_out * mid * out,
    )
    back2 = sum_everywhere(back2)
    strided_shape = (half, half, images, wide)
    (d_strided,) = call(
        k_back_strided, "back_strided", blocks, [column(dzs), tap(w_project)],
        [(strided_shape, F32, whole(strided_shape))], flops=2 * rows_out * wide * out,
    )
    g_expand = weight_blocks(a2, dz3)
    g_project = weight_blocks(x_split[:, 0, :, 0], dzs)
    plane = (half, 1, half, 1, images, LANES)

    def parity(array):
        return (array, pl.BlockSpec(plane, lambda s: (0, s // 2, 0, s % 2, 0, 0)))

    dz2, du1, back1 = call(
        k_back_entry_spatial, "back_entry_spatial", 4,
        [fixed(du2), fixed(z2), fixed(sums2), fixed(back2), fixed(tables[1]), counts, counts_in,
         limits_out, onehot, fixed(w_spatial), parity(slope1), parity(z1_split), fixed(sums1)],
        [small_out, (split, BF, parity(z1_split)[1]), sums_out],
        [pltpu.VMEM((half + 1, half + 1, images, mid), BF), pltpu.VMEM((2, images, mid), F32), acc],
        flops=18 * rows_out * mid * mid,
    )
    back1 = sum_everywhere(back1)
    (g_spatial,) = call(
        k_taps_strided, "entry_spatial_grad", 9, [fixed(planes), fixed(dz2)], [taps_out],
        flops=18 * rows_out * mid * mid,
    )
    two = (2, full, images, mid)
    dz1, d_inputs = call(
        k_back_first, "back_first", half,
        [(du1.reshape(z1.shape), along(two, 0)), (z1, along(two, 0)), fixed(sums1), fixed(back1),
         fixed(tables[0]), counts_in, limits_in, onehot, fixed(w_reduce),
         (d_strided, along((1, half, images, wide), 0))],
        [(z1.shape, BF, along(two, 0)),
         ((full, full, images, wide), F32, along((2, full, images, wide), 0))],
        flops=2 * rows_in * wide * mid,
    )
    g_reduce = dot_tn(flat(x), flat(dz1)).astype(BF)[None]
    entry_grads = scatter_grads(
        (g_reduce, g_spatial, g_expand, g_project),
        (entry_reduce.shape, entry_spatial.shape, entry_expand.shape, entry_project.shape),
    )

    def own_share(back, gain_at=0):
        width = back.shape[1] // shards
        own = lax.dynamic_slice_in_dim(back, position * width, width, 1)
        return jnp.stack([own[gain_at : gain_at + GROUPS], own[GROUPS : 2 * GROUPS]])

    return (
        result.transpose(2, 0, 1, 3),
        d_inputs.transpose(2, 0, 1, 3),
        *entry_grads,
        own_share(back1),
        own_share(back2),
        own_share(back3),
        own_share(back3, 2 * GROUPS),
        *inner_grads,
        own_share(back4),
        own_share(back5),
        own_share(back6),
    )


def weight_blocks(source, dz):
    grad = dot_tn(flat(source), flat(dz)).astype(BF)
    return jnp.stack([grad[:, i : i + LANES] for i in range(0, grad.shape[1], LANES)])


def solution(mesh):
    images = P(("dp", "rep"), None, None, None)
    rows = P("dp", None)
    taps = P(None, "dp", None)
    table = P(None, None, "dp")
    entry = (rows, taps, rows, rows, table, table, table, table)
    inner = (rows, taps, rows, table, table, table)
    return jax.shard_map(
        body,
        mesh=mesh,
        in_specs=(images, images, P(("dp", "rep")), P(), P(), P(), *entry, *inner),
        out_specs=(images, images, *entry, *inner),
        check_vma=False,
    )
```

time: 2020 us -> 856 us (0.42)
  blocking collectives: 650 us -> 32.6 us
  waiting for transfers between devices: 890 us -> 368 us
  matrix products: 228 us -> 26.6 us
  Pallas kernels: 0 us -> 200 us
  other arithmetic: 200 us -> 33.2 us
  starting transfers between devices: 1.22 us -> 96.9 us
  local copies, waits for them, and re-layouts: 26.8 us -> 75.8 us
    reduce_scatter x7 -> x2, waiting for transfers between devices: 737 us -> 151 us  [scatter_grads(): own = lax.psum_scatter(rows, AXES, scatter_dimension=0, tiled=True)]
    psum x11 -> x0, blocking collectives: 446 us -> none  [the longest x6 243 us: normalize_back(): gain_total, bias_total = lax.psum((local_gain, local_bias), ('dp', 'rep'))]
    dot_general x137 -> x5, matrix products: 228 us -> 26.6 us  [dot_tn(): lax.dot_general(a, b, (((0,), (0,)), ((), ())), preferred_element_type=F32)]
    pallas_call x0 -> x17, Pallas kernels: none -> 200 us  [call(): pl.pallas_call(kernel, name=name, grid=(steps,), in_specs=[s for _, s in...]
    all_gather x7 -> x1, blocking collectives: 204 us -> 32.6 us  [body(): tables_flat = lax.all_gather(tables_flat, 'dp', axis=0, tiled=False)]
    scatter-add x10 -> x0, other arithmetic: 106 us -> none  [the longest x9 93.8 us: conv_three_back(): spread_back = spread_back.at[:, vertical:vertical + extent:stride, latera...]
    ppermute x0 -> x84, starting transfers between devices: none -> 96.7 us  [xor_swap(): return lax.ppermute(value, AXES, [(d, d ^ distance) for d in range(count)])]
    ppermute x0 -> x84, waiting for transfers between devices: none -> 81.6 us  [xor_swap(): return lax.ppermute(value, AXES, [(d, d ^ distance) for d in range(count)])]
  transfers between devices with their start and end apart: 16 -> 90, of which waited for: 12 -> 59; matrix products, arithmetic and copies ran while one was open for 9% -> 11% of each run, Pallas kernels for 0% -> 10%
where the time goes in v1:
time: 856 us; the launch traced here: 850 us
  waiting for transfers between devices  368 us (43%)
  Pallas kernels  200 us (23%)
  starting transfers between devices  96.9 us (11%)
  local copies, waits for them, and re-layouts  75.8 us (9%)
  other arithmetic  33.2 us (4%)
  blocking collectives  32.6 us (4%)
  matrix products  26.6 us (3%)
  between operations  17.2 us (2%)
    pallas_call x17, Pallas kernels, call(): pl.pallas_call(kernel, name=name, grid=(steps,), in_specs=[s for _, s in...  200 us
    reduce_scatter x2, waiting for transfers between devices, scatter_grads(): own = lax.psum_scatter(rows, AXES, scatter_dimension=0, tiled=True)  151 us
    all_gather x1, waiting for transfers between devices, gather_weights(): gathered = lax.all_gather(rows, AXES, axis=0, tiled=False)  106 us
    ppermute x84, starting transfers between devices, xor_swap(): return lax.ppermute(value, AXES, [(d, d ^ distance) for d in range(count)])  96.7 us
    ppermute x84, waiting for transfers between devices, xor_swap(): return lax.ppermute(value, AXES, [(d, d ^ distance) for d in range(count)])  81.6 us
    all_gather x1, blocking collectives, body(): tables_flat = lax.all_gather(tables_flat, 'dp', axis=0, tiled=False)  32.6 us
    dot_general x5, matrix products, dot_tn(): lax.dot_general(a, b, (((0,), (0,)), ((), ())), preferred_element_type=F32)  26.6 us
    all_gather x2, waiting for transfers between devices, scatter_grads(): gathered = lax.all_gather(own, 'rep', axis=0, tiled=False)  24.1 us
  transfers between devices with their start and end apart: 90, of which 59 were waited for; matrix products, arithmetic and copies ran while one was open for 11% of the time, Pallas kernels for 10%

profile of v1, /device:TPU:0, one launch (start us, length us, event | category | flops | bytes accessed | tf_op | source)
XLA Modules:
  0.0 850.5 jit_solution(12776908401584479336)
XLA Ops:
  15.1 32.6 %all-gather.4 = bf16[8,6,1024]{2,1,0:T(8,128)(2,1)S(1)} all-gather(bf16[1,6,1024]{2,1,0:T(8,128)(2,1)S(1)} %bitcast.304), channel_id=2, replica_groups=mesh['dp'=8,'rep'=4] {'dp'}, dimensions={0}, use_global_device_ids=true | all-gather | bytes 110592 | tf_op jit(solution)/shard_map/all_gather | solution.py:692
  54.9 9.4 %first.1 = (bf16[14,14,16,512]{3,2,1,0:T(8,128)(2,1)}, f32[8,512]{1,0:T(8,128)}) custom-call(bf16[14,14,16,1024]{3,2,1,0:T(8,128)(2,1)} %bitcast.299, bf16[1024,512]{1,0:T(8,128)(2,1)} %all-gather.10.cloned.1.call-done.w, s32[16,512]{1,0:T(8,128)} %broadcast_in_dim.24.limits, f32[3,16,512]{2,1,0:T(8,128)} %broadcast_in_dim.26.onehot, ...), custom_call_target="tpu_custom_call" | custom-call | flops 3288334336 | bytes 7604224 | tf_op jit(solution)/shard_map/first/pallas_call | solution.py:74
  81.1 105.6 %all-gather.12.cloned.1.call-done = bf16[19456,512]{1,0:T(8,128)(2,1)} async-done(((bf16[608,512]{1,0:T(8,128)(2,1)}), bf16[19456,512]{1,0:T(8,128)(2,1)}) %all-gather.12.cloned.1.call-update) | async-done | bytes 19922960 | tf_op jit(solution)/shard_map/all_gather | solution.py:651
  198.0 16.4 %entry_spatial.1 = (bf16[2,2,8,8,16,512]{5,4,3,2,1,0:T(8,128)(2,1)}, bf16[7,2,7,2,16,512]{5,4,3,2,1,0:T(8,128)(2,1)}, bf16[7,7,16,512]{3,2,1,0:T(8,128)(2,1)}, f32[8,512]{1,0:T(8,128)}) custom-call(bf16[7,2,7,2,16,512]{5,4,3,2,1,0:T(8,128)(2,1)} %bitcast.260, f32[8,512]{1,0:T(8,128)} %copy-done.4, f32[6,512]{1,0:T(8,128)} %reshape.335.table.table1, ...), custom_call_target="tpu_custom_call" | custom-call | flops 3699376128 | bytes 8134656 | tf_op jit(solution)/shard_map/entry_spatial/pallas_call | solution.py:74
  234.5 8.5 %strided.1 = (bf16[7,7,16,2048]{3,2,1,0:T(8,128)(2,1)}, f32[8,2048]{1,0:T(8,128)}) custom-call(bf16[7,2,7,2,16,1024]{5,4,3,2,1,0:T(8,128)(2,1)} %bitcast.300, bf16[4,1024,512]{2,1,0:T(8,128)(2,1)} %bitcast.253, s32[16,512]{1,0:T(8,128)} %broadcast_in_dim.34.limits_out.limits, f32[3,16,512]{2,1,0:T(8,128)} %broadcast_in_dim.26.onehot), custom_call_target="tpu_custom_call" | custom-call | flops 3288334336 | bytes 10747904 | tf_op jit(solution)/shard_map/strided/pallas_call | solution.py:74
  245.1 8.7 %expand.1 = (bf16[7,7,16,512]{3,2,1,0:T(8,128)(2,1)}, bf16[7,7,16,512]{3,2,1,0:T(8,128)(2,1)}, bf16[7,7,16,2048]{3,2,1,0:T(8,128)(2,1)}, f32[8,2048]{1,0:T(8,128)}) custom-call(bf16[7,7,16,512]{3,2,1,0:T(8,128)(2,1)} %get-tuple-element.63.z.z2, f32[8,512]{1,0:T(8,128)} %add_add_fusion.20.in_sums.sums2, f32[6,512]{1,0:T(8,128)} %reshape.336.table.table2, ...), custom_call_target="tpu_custom_call" | custom-call | flops 1644167168 | bytes 3098624 | tf_op jit(solution)/shard_map/expand/pallas_call | solution.py:74
  279.6 13.4 %middle.1 = (bf16[7,7,16,2048]{3,2,1,0:T(8,128)(2,1)}, bf16[7,7,16,2048]{3,2,1,0:T(8,128)(2,1)}, bf16[7,7,16,512]{3,2,1,0:T(8,128)(2,1)}, f32[8,512]{1,0:T(8,128)}) custom-call(bf16[7,7,16,2048]{3,2,1,0:T(8,128)(2,1)} %get-tuple-element.65.z3, bf16[7,7,16,2048]{3,2,1,0:T(8,128)(2,1)} %get-tuple-element.66.zs, f32[8,2048]{1,0:T(8,128)} %get-tuple-element.206.sums3, ...), custom_call_target="tpu_custom_call" | custom-call | flops 1644167168 | bytes 8886272 | tf_op jit(solution)/shard_map/middle/pallas_call | solution.py:74
  312.4 22.3 %inner_spatial.1 = (bf16[9,9,16,512]{3,2,1,0:T(8,128)(2,1)}, bf16[7,7,16,512]{3,2,1,0:T(8,128)(2,1)}, bf16[7,7,16,512]{3,2,1,0:T(8,128)(2,1)}, f32[8,512]{1,0:T(8,128)}) custom-call(bf16[7,7,16,512]{3,2,1,0:T(8,128)(2,1)} %get-tuple-element.69.z4, f32[8,512]{1,0:T(8,128)} %add_add_fusion.18.in_sums.sums4, f32[6,512]{1,0:T(8,128)} %reshape.339.table.table4, ...), custom_call_target="tpu_custom_call" | custom-call | flops 3699376128 | bytes 5720064 | tf_op jit(solution)/shard_map/inner_spatial/pallas_call | solution.py:74
  350.1 8.7 %inner_expand.1 = (bf16[7,7,16,512]{3,2,1,0:T(8,128)(2,1)}, bf16[7,7,16,512]{3,2,1,0:T(8,128)(2,1)}, bf16[7,7,16,2048]{3,2,1,0:T(8,128)(2,1)}, f32[8,2048]{1,0:T(8,128)}) custom-call(bf16[7,7,16,512]{3,2,1,0:T(8,128)(2,1)} %get-tuple-element.71.z.z5, f32[8,512]{1,0:T(8,128)} %add_add_fusion.16.in_sums.sums5, f32[6,512]{1,0:T(8,128)} %reshape.340.table.table5, ...), custom_call_target="tpu_custom_call" | custom-call | flops 1644167168 | bytes 3098624 | tf_op jit(solution)/shard_map/inner_expand/pallas_call | solution.py:74
  378.3 12.0 %close.1 = (bf16[7,7,16,2048]{3,2,1,0:T(8,128)(2,1)}, bf16[7,7,16,2048]{3,2,1,0:T(8,128)(2,1)}, f32[8,2048]{1,0:T(8,128)}) custom-call(bf16[7,7,16,2048]{3,2,1,0:T(8,128)(2,1)} %get-tuple-element.73.z6, f32[8,2048]{1,0:T(8,128)} %add_add_fusion.6.in_sums.sums6, f32[6,2048]{1,0:T(8,128)} %bitcast.292, f32[3,512]{1,0:T(4,128)} %broadcast_in_dim.32.counts_out.counts, ...), custom_call_target="tpu_custom_call" | custom-call | bytes 9918464 | tf_op jit(solution)/shard_map/close/pallas_call | solution.py:74
  408.5 10.4 %back_inner_expand.1 = (bf16[7,7,16,2048]{3,2,1,0:T(8,128)(2,1)}, f32[7,7,16,512]{3,2,1,0:T(8,128)}, f32[8,512]{1,0:T(8,128)}) custom-call(bf16[7,7,16,2048]{3,2,1,0:T(8,128)(2,1)} %get-tuple-element.77.du6, bf16[7,7,16,2048]{3,2,1,0:T(8,128)(2,1)} %get-tuple-element.73.z6, f32[8,2048]{1,0:T(8,128)} %add_add_fusion.6.in_sums.sums6, ...), custom_call_target="tpu_custom_call" | custom-call | flops 1644167168 | bytes 10459136 | tf_op jit(solution)/shard_map/back_inner_expand/pallas_call | solution.py:74
  436.7 9.8 %back_inner_spatial.1 = (bf16[7,7,16,512]{3,2,1,0:T(8,128)(2,1)}, f32[7,7,16,512]{3,2,1,0:T(8,128)}, f32[8,512]{1,0:T(8,128)}) custom-call(f32[7,7,16,512]{3,2,1,0:T(8,128)} %get-tuple-element.80.du5, bf16[7,7,16,512]{3,2,1,0:T(8,128)(2,1)} %get-tuple-element.71.z.z5, f32[8,512]{1,0:T(8,128)} %add_add_fusion.16.in_sums.sums5, ...), custom_call_target="tpu_custom_call" | custom-call | flops 3699376128 | bytes 8931328 | tf_op jit(solution)/shard_map/back_inner_spatial/pallas_call | solution.py:74
  458.5 9.2 %inner_spatial_grad.1 = bf16[9,512,512]{2,1,0:T(8,128)(2,1)} custom-call(bf16[9,9,16,512]{3,2,1,0:T(8,128)(2,1)} %get-tuple-element.102.field, bf16[7,7,16,512]{3,2,1,0:T(8,128)(2,1)} %get-tuple-element.103.dz), custom_call_target="tpu_custom_call" | custom-call | flops 3699376128 | bytes 2129920 | tf_op jit(solution)/shard_map/inner_spatial_grad/pallas_call | solution.py:74
  471.2 12.9 %back_middle.1 = (bf16[7,7,16,512]{3,2,1,0:T(8,128)(2,1)}, bf16[7,7,16,2048]{3,2,1,0:T(8,128)(2,1)}, f32[16,2048]{1,0:T(8,128)}) custom-call(f32[7,7,16,512]{3,2,1,0:T(8,128)} %get-tuple-element.83.du4, bf16[7,7,16,512]{3,2,1,0:T(8,128)(2,1)} %get-tuple-element.69.z4, f32[8,512]{1,0:T(8,128)} %add_add_fusion.18.in_sums.sums4, ...), custom_call_target="tpu_custom_call" | custom-call | flops 1644167168 | bytes 20908032 | tf_op jit(solution)/shard_map/back_middle/pallas_call | solution.py:74
  523.7 13.4 %back_entry_expand.1 = (bf16[7,7,16,2048]{3,2,1,0:T(8,128)(2,1)}, bf16[7,7,16,2048]{3,2,1,0:T(8,128)(2,1)}, f32[7,7,16,512]{3,2,1,0:T(8,128)}, f32[8,512]{1,0:T(8,128)}) custom-call(bf16[7,7,16,2048]{3,2,1,0:T(8,128)(2,1)} %get-tuple-element.86.du3, bf16[7,7,16,2048]{3,2,1,0:T(8,128)(2,1)} %get-tuple-element.65.z3, ...), custom_call_target="tpu_custom_call" | custom-call | flops 1644167168 | bytes 13850624 | tf_op jit(solution)/shard_map/back_entry_expand/pallas_call | solution.py:74
  559.5 8.6 %back_strided.1.strided = f32[7,7,16,1024]{3,2,1,0:T(8,128)} custom-call(bf16[7,7,16,2048]{3,2,1,0:T(8,128)(2,1)} %get-tuple-element.94.dzs, bf16[4,1024,512]{2,1,0:T(8,128)(2,1)} %bitcast.254), custom_call_target="tpu_custom_call" | custom-call | flops 3288334336 | bytes 7405568 | tf_op jit(solution)/shard_map/back_strided/pallas_call | solution.py:74
  568.8 12.0 %back_entry_spatial.1 = (bf16[7,7,16,512]{3,2,1,0:T(8,128)(2,1)}, bf16[7,2,7,2,16,512]{5,4,3,2,1,0:T(8,128)(2,1)}, f32[8,512]{1,0:T(8,128)}) custom-call(f32[7,7,16,512]{3,2,1,0:T(8,128)} %get-tuple-element.89.du2, bf16[7,7,16,512]{3,2,1,0:T(8,128)(2,1)} %get-tuple-element.63.z.z2, f32[8,512]{1,0:T(8,128)} %add_add_fusion.20.in_sums.sums2, ...), custom_call_target="tpu_custom_call" | custom-call | flops 3699376128 | bytes 13754368 | tf_op jit(solution)/shard_map/back_entry_spatial/pallas_call | solution.py:74
  593.3 10.4 %entry_spatial_grad.1 = bf16[9,512,512]{2,1,0:T(8,128)(2,1)} custom-call(bf16[2,2,8,8,16,512]{5,4,3,2,1,0:T(8,128)(2,1)} %get-tuple-element.97.planes, bf16[7,7,16,512]{3,2,1,0:T(8,128)(2,1)} %get-tuple-element.98.dz), custom_call_target="tpu_custom_call" | custom-call | flops 3699376128 | bytes 4997120 | tf_op jit(solution)/shard_map/entry_spatial_grad/pallas_call | solution.py:74
  609.5 13.7 %back_first.1 = (bf16[14,14,16,512]{3,2,1,0:T(8,128)(2,1)}, f32[14,14,16,1024]{3,2,1,0:T(8,128)}) custom-call(bf16[14,14,16,512]{3,2,1,0:T(8,128)(2,1)} %bitcast.310, bf16[14,14,16,512]{3,2,1,0:T(8,128)(2,1)} %get-tuple-element.61.z1, f32[8,512]{1,0:T(8,128)} %copy-done.4, f32[8,512]{1,0:T(8,128)} %add_add_fusion.8.back1, f32[6,512]{1,0:T(8,128)} %reshape.335.table.table1, ...), custom_call_target="tpu_custom_call" | custom-call | flops 3288334336 | bytes 10864640 | tf_op jit(solution)/shard_map/back_first/pallas_call | solution.py:74
  623.1 8.6 %fusion = bf16[1024,512]{0,1:T(8,128)(2,1)} fusion(bf16[14,14,16,512]{3,2,1,0:T(8,128)(2,1)} %get-tuple-element.96, bf16[16,14,14,1024]{3,0,2,1:T(8,128)(2,1)} %param.20), kind=kOutput, calls=%fused_computation.10 | convolution fusion | flops 3288858624 | bytes 10682368 | tf_op jit(solution)/shard_map/dot_general | solution.py:56
  634.0 9.7 %pad_maximum_fusion = bf16[32,368,512]{2,1,0:T(8,128)(2,1)} fusion(bf16[32,128,512]{2,1,0:T(8,128)(2,1)} %bitcast.237, bf16[32,64,512]{2,1,0:T(8,128)(2,1)S(1)} %bitcast.240, bf16[32,144,512]{2,1,0:T(8,128)(2,1)} %bitcast.233, bf16[32,32,512]{2,1,0:T(8,128)(2,1)} %bitcast.252), kind=kLoop, calls=%fused_computation | loop fusion | flops 48234496 | bytes 24117248 | tf_op jit(solution)/shard_map/concatenate | solution.py:666
  647.9 150.6 %reduce-scatter.3.cloned.1.call-done = bf16[368,512]{1,0:T(8,128)(2,1)} async-done(((bf16[11776,512]{1,0:T(8,128)(2,1)}), bf16[368,512]{1,0:T(8,128)(2,1)}) %reduce-scatter.3.cloned.1.call-update) | async-done | bytes 376848 | tf_op jit(solution)/shard_map/reduce_scatter | solution.py:667
  804.0 9.1 %all-gather.16.cloned.1.call-done = bf16[1088,512]{1,0:T(8,128)(2,1)} async-done(((bf16[272,512]{1,0:T(8,128)(2,1)}), bf16[1088,512]{1,0:T(8,128)(2,1)}) %all-gather.16.cloned.1.call-update) | async-done | bytes 1114128 | tf_op jit(solution)/shard_map/all_gather | solution.py:668
  818.8 15.0 %all-gather.14.cloned.1.call-done = bf16[1472,512]{1,0:T(8,128)(2,1)} async-done(((bf16[368,512]{1,0:T(8,128)(2,1)}), bf16[1472,512]{1,0:T(8,128)(2,1)}) %all-gather.14.cloned.1.call-update) | async-done | bytes 1507344 | tf_op jit(solution)/shard_map/all_gather | solution.py:668
  (398 shorter events, 302.2 us)
Async XLA Ops:
  7.3 46.2 %all-gather.10.cloned.1.call-start = ((), (), s32[]{:S(2)}) async-start(), calls=%async_computation.2 | async-start | bytes 1179648 | tf_op jit(solution)/shard_map/all_gather | solution.py:690
  8.0 178.6 %all-gather.12.cloned.1.call-start = ((), (), s32[]{:S(2)}) async-start(), calls=%async_computation.5 | async-start | bytes 20545536 | tf_op jit(solution)/shard_map/all_gather | solution.py:651
  12.0 631.9 %reduce-scatter.5.cloned.1.call-start = ((), (), s32[]{:S(2)}) async-start(), calls=%async_computation.4 | async-start | bytes 9191424 | tf_op jit(solution)/shard_map/reduce_scatter | solution.py:667
  216.5 13.5 %collective-permute-start.10 = (f32[8,512]{1,0:T(8,128)S(1)}, f32[8,512]{1,0:T(8,128)S(1)}, u32[]{:S(2)}, u32[]{:S(2)}) collective-permute-start(f32[8,512]{1,0:T(8,128)S(1)} %add.300), channel_id=1, source_target_pairs={{0,6},{1,7},{2,4},{3,5},{4,2},{5,3},{6,0},{7,1},{8,14},{9,15},{10,... | collective-permute-start | bytes 49160 | tf_op jit(solution)/shard_map/ppermute | solution.py:21
  217.9 12.0 %collective-permute-start.9 = (f32[8,512]{1,0:T(8,128)S(1)}, f32[8,512]{1,0:T(8,128)S(1)}, u32[]{:S(2)}, u32[]{:S(2)}) collective-permute-start(f32[8,512]{1,0:T(8,128)S(1)} %add.300), channel_id=1, source_target_pairs={{0,4},{1,5},{2,6},{3,7},{4,0},{5,1},{6,2},{7,3},{8,12},{9,13},{10,... | collective-permute-start | bytes 49160 | tf_op jit(solution)/shard_map/ppermute | solution.py:21
  230.0 14.5 %collective-permute-start.13 = (f32[8,512]{1,0:T(8,128)S(1)}, f32[8,512]{1,0:T(8,128)S(1)}, u32[]{:S(2)}, u32[]{:S(2)}) collective-permute-start(f32[8,512]{1,0:T(8,128)S(1)} %add_add_fusion.21), channel_id=1, source_target_pairs={{0,24},{1,25},{2,26},{3,27},{4,28},{5,29},{6,30},{7,31},{8,16},{9,... | collective-permute-start | bytes 49160 | tf_op jit(solution)/shard_map/ppermute | solution.py:21
  231.4 13.1 %collective-permute-start.12 = (f32[8,512]{1,0:T(8,128)S(1)}, f32[8,512]{1,0:T(8,128)S(1)}, u32[]{:S(2)}, u32[]{:S(2)}) collective-permute-start(f32[8,512]{1,0:T(8,128)S(1)} %add_add_fusion.21), channel_id=1, source_target_pairs={{0,16},{1,17},{2,18},{3,19},{4,20},{5,21},{6,22},{7,23},{8,24},{9,... | collective-permute-start | bytes 49160 | tf_op jit(solution)/shard_map/ppermute | solution.py:21
  231.5 13.0 %collective-permute-start.11 = (f32[8,512]{1,0:T(8,128)S(1)}, f32[8,512]{1,0:T(8,128)S(1)}, u32[]{:S(2)}, u32[]{:S(2)}) collective-permute-start(f32[8,512]{1,0:T(8,128)S(1)} %add_add_fusion.21), channel_id=1, source_target_pairs={{0,8},{1,9},{2,10},{3,11},{4,12},{5,13},{6,14},{7,15},{8,0},{9,1},... | collective-permute-start | bytes 49160 | tf_op jit(solution)/shard_map/ppermute | solution.py:21
  267.0 11.9 %collective-permute-start.19 = (f32[8,4096]{1,0:T(8,128)S(1)}, f32[8,4096]{1,0:T(8,128)S(1)}, u32[]{:S(2)}, u32[]{:S(2)}) collective-permute-start(f32[8,4096]{1,0:T(8,128)S(1)} %add_add_fusion.3), channel_id=1, source_target_pairs={{0,16},{1,17},{2,18},{3,19},{4,20},{5,21},{6,22},{7,23},{8,24},{9,... | collective-permute-start | bytes 393224 | tf_op jit(solution)/shard_map/ppermute | solution.py:21
  267.1 11.8 %collective-permute-start.18 = (f32[8,4096]{1,0:T(8,128)S(1)}, f32[8,4096]{1,0:T(8,128)S(1)}, u32[]{:S(2)}, u32[]{:S(2)}) collective-permute-start(f32[8,4096]{1,0:T(8,128)S(1)} %add_add_fusion.3), channel_id=1, source_target_pairs={{0,8},{1,9},{2,10},{3,11},{4,12},{5,13},{6,14},{7,15},{8,0},{9,1},... | collective-permute-start | bytes 393224 | tf_op jit(solution)/shard_map/ppermute | solution.py:21
  454.1 16.5 %collective-permute-start.62 = (f32[8,512]{1,0:T(8,128)S(1)}, f32[8,512]{1,0:T(8,128)S(1)}, u32[]{:S(2)}, u32[]{:S(2)}) collective-permute-start(f32[8,512]{1,0:T(8,128)S(1)} %add_add_fusion.13), channel_id=1, source_target_pairs={{0,24},{1,25},{2,26},{3,27},{4,28},{5,29},{6,30},{7,31},{8,16},{9,... | collective-permute-start | bytes 49160 | tf_op jit(solution)/shard_map/ppermute | solution.py:21
  456.0 14.6 %collective-permute-start.61 = (f32[8,512]{1,0:T(8,128)S(1)}, f32[8,512]{1,0:T(8,128)S(1)}, u32[]{:S(2)}, u32[]{:S(2)}) collective-permute-start(f32[8,512]{1,0:T(8,128)S(1)} %add_add_fusion.13), channel_id=1, source_target_pairs={{0,16},{1,17},{2,18},{3,19},{4,20},{5,21},{6,22},{7,23},{8,24},{9,... | collective-permute-start | bytes 49160 | tf_op jit(solution)/shard_map/ppermute | solution.py:21
  456.0 14.6 %collective-permute-start.60 = (f32[8,512]{1,0:T(8,128)S(1)}, f32[8,512]{1,0:T(8,128)S(1)}, u32[]{:S(2)}, u32[]{:S(2)}) collective-permute-start(f32[8,512]{1,0:T(8,128)S(1)} %add_add_fusion.13), channel_id=1, source_target_pairs={{0,8},{1,9},{2,10},{3,11},{4,12},{5,13},{6,14},{7,15},{8,0},{9,1},... | collective-permute-start | bytes 49160 | tf_op jit(solution)/shard_map/ppermute | solution.py:21
  492.5 306.0 %reduce-scatter.3.cloned.1.call-start = ((), (), s32[]{:S(2)}) async-start(), calls=%async_computation.3 | async-start | bytes 12435456 | tf_op jit(solution)/shard_map/reduce_scatter | solution.py:667
  497.4 12.4 %collective-permute-start.64 = (f32[16,2048]{1,0:T(8,128)S(1)}, f32[16,2048]{1,0:T(8,128)S(1)}, u32[]{:S(2)}, u32[]{:S(2)}) collective-permute-start(f32[16,2048]{1,0:T(8,128)S(1)} %add.356), channel_id=1, source_target_pairs={{0,2},{1,3},{2,0},{3,1},{4,6},{5,7},{6,4},{7,5},{8,10},{9,11},{10,... | collective-permute-start | bytes 393224 | tf_op jit(solution)/shard_map/ppermute | solution.py:21
  510.4 12.6 %collective-permute-start.68 = (f32[16,2048]{1,0:T(8,128)S(1)}, f32[16,2048]{1,0:T(8,128)S(1)}, u32[]{:S(2)}, u32[]{:S(2)}) collective-permute-start(f32[16,2048]{1,0:T(8,128)S(1)} %add_add_fusion.1), channel_id=1, source_target_pairs={{0,16},{1,17},{2,18},{3,19},{4,20},{5,21},{6,22},{7,23},{8,24},{9,... | collective-permute-start | bytes 393224 | tf_op jit(solution)/shard_map/ppermute | solution.py:21
  510.4 12.6 %collective-permute-start.67 = (f32[16,2048]{1,0:T(8,128)S(1)}, f32[16,2048]{1,0:T(8,128)S(1)}, u32[]{:S(2)}, u32[]{:S(2)}) collective-permute-start(f32[16,2048]{1,0:T(8,128)S(1)} %add_add_fusion.1), channel_id=1, source_target_pairs={{0,8},{1,9},{2,10},{3,11},{4,12},{5,13},{6,14},{7,15},{8,0},{9,1},... | collective-permute-start | bytes 393224 | tf_op jit(solution)/shard_map/ppermute | solution.py:21
  555.1 13.0 %collective-permute-start.76 = (f32[8,512]{1,0:T(8,128)S(1)}, f32[8,512]{1,0:T(8,128)S(1)}, u32[]{:S(2)}, u32[]{:S(2)}) collective-permute-start(f32[8,512]{1,0:T(8,128)S(1)} %add_add_fusion.11), channel_id=1, source_target_pairs={{0,24},{1,25},{2,26},{3,27},{4,28},{5,29},{6,30},{7,31},{8,16},{9,... | collective-permute-start | bytes 49160 | tf_op jit(solution)/shard_map/ppermute | solution.py:21
  556.4 11.7 %collective-permute-start.74 = (f32[8,512]{1,0:T(8,128)S(1)}, f32[8,512]{1,0:T(8,128)S(1)}, u32[]{:S(2)}, u32[]{:S(2)}) collective-permute-start(f32[8,512]{1,0:T(8,128)S(1)} %add_add_fusion.11), channel_id=1, source_target_pairs={{0,8},{1,9},{2,10},{3,11},{4,12},{5,13},{6,14},{7,15},{8,0},{9,1},... | collective-permute-start | bytes 49160 | tf_op jit(solution)/shard_map/ppermute | solution.py:21
  588.9 19.9 %collective-permute-start.83 = (f32[8,512]{1,0:T(8,128)S(1)}, f32[8,512]{1,0:T(8,128)S(1)}, u32[]{:S(2)}, u32[]{:S(2)}) collective-permute-start(f32[8,512]{1,0:T(8,128)S(1)} %add_add_fusion.9), channel_id=1, source_target_pairs={{0,24},{1,25},{2,26},{3,27},{4,28},{5,29},{6,30},{7,31},{8,16},{9,... | collective-permute-start | bytes 49160 | tf_op jit(solution)/shard_map/ppermute | solution.py:21
  590.3 18.6 %collective-permute-start.82 = (f32[8,512]{1,0:T(8,128)S(1)}, f32[8,512]{1,0:T(8,128)S(1)}, u32[]{:S(2)}, u32[]{:S(2)}) collective-permute-start(f32[8,512]{1,0:T(8,128)S(1)} %add_add_fusion.9), channel_id=1, source_target_pairs={{0,16},{1,17},{2,18},{3,19},{4,20},{5,21},{6,22},{7,23},{8,24},{9,... | collective-permute-start | bytes 49160 | tf_op jit(solution)/shard_map/ppermute | solution.py:21
  590.3 18.5 %collective-permute-start.81 = (f32[8,512]{1,0:T(8,128)S(1)}, f32[8,512]{1,0:T(8,128)S(1)}, u32[]{:S(2)}, u32[]{:S(2)}) collective-permute-start(f32[8,512]{1,0:T(8,128)S(1)} %add_add_fusion.9), channel_id=1, source_target_pairs={{0,8},{1,9},{2,10},{3,11},{4,12},{5,13},{6,14},{7,15},{8,0},{9,1},... | collective-permute-start | bytes 49160 | tf_op jit(solution)/shard_map/ppermute | solution.py:21
  643.7 169.4 %all-gather.16.cloned.1.call-start = ((), (), s32[]{:S(2)}) async-start(), calls=%async_computation.7 | async-start | bytes 1392640 | tf_op jit(solution)/shard_map/all_gather | solution.py:668
  644.3 189.5 %all-gather.14.cloned.1.call-start = ((), (), s32[]{:S(2)}) async-start(), calls=%async_computation.6 | async-start | bytes 1884160 | tf_op jit(solution)/shard_map/all_gather | solution.py:668
  (89 other events, 693.6 us)
Sparse Core Ops, SparseCore 0:
  10.3 43.1 all-gather.9
  56.9 129.7 all-gather.11
  492.6 151.1 reduce-scatter.4
  646.1 152.3 reduce-scatter.2
  799.9 13.1 all-gather.15
  814.5 19.2 all-gather.13

commit v2 on v1

--- a/solution.py
+++ b/solution.py
@@ -13,7 +13,7 @@
 F32 = jnp.float32
 GROUPS = 3
 LANES = 512
-VMEM = 56 * 1024 * 1024
+VMEM = 22 * 1024 * 1024
 
 
 def xor_swap(value, distance):
@@ -21,26 +21,222 @@
     return lax.ppermute(value, AXES, [(d, d ^ distance) for d in range(count)])
 
 
-def sum_everywhere(value):
+def own_bit(bit):
+    me = lax.axis_index("dp") * lax.axis_size("rep") + lax.axis_index("rep")
+    return lax.shift_right_logical(me, bit) & 1
+
+
+def index_bits():
     count = lax.axis_size("dp") * lax.axis_size("rep")
-    bits = [1 << b for b in range(count.bit_length() - 1)]
-    stages = [bits[:1]] + [bits[i : i + 2] for i in range(1, len(bits), 2)]
-    for stage in stages:
+    return count.bit_length() - 1
+
+
+def sum_stages(value, bits):
+    for stage in [bits[i : i + 2] for i in range(0, len(bits), 2)]:
         distances = [0]
         for bit in stage:
-            distances = distances + [d | bit for d in distances]
-        parts = [xor_swap(value, d) for d in distances[1:]]
-        for part in parts:
+            distances = distances + [d | (1 << bit) for d in distances]
+        for part in [xor_swap(value, d) for d in distances[1:]]:
             value = value + part
     return value
+
+
+def sum_near(value):
+    if value.size <= 8192:
+        return sum_stages(value + xor_swap(value, 1), [1, 2])
+    width = value.shape[1] // 2
+    own = own_bit(0)
+    kept = lax.dynamic_slice_in_dim(value, own * width, width, 1)
+    sent = lax.dynamic_slice_in_dim(value, (1 - own) * width, width, 1)
+    return sum_stages(kept + xor_swap(sent, 1), [1, 2])
+
+
+def sum_far(value, columns):
+    value = sum_stages(value, list(range(3, index_bits())))
+    if value.shape[1] == columns:
+        return value
+    return pair(value, xor_swap(value, 1), 0, 1)
+
+
+def sum_everywhere(value):
+    return sum_far(sum_near(value), value.shape[1])
+
+
+def after(*values):
+    return lax.optimization_barrier(values)
+
+
+def pair(value, other, bit, axis):
+    own = own_bit(bit)
+    return jnp.concatenate(
+        [jnp.where(own == 0, value, other), jnp.where(own == 0, other, value)], axis=axis
+    )
+
+
+def gather_bit(value, bit, axis):
+    return pair(value, xor_swap(value, 1 << bit), bit, axis)
+
+
+def gather_rows(part, others):
+    count = index_bits()
+    value = part.reshape((1,) * count + part.shape)
+    for bit in list(range(3, count)) + [2, 1, 0]:
+        value = gather_bit(value, bit, count - 1 - bit)
+        if bit == 3:
+            value, *others = after(value, *others)
+    return value.reshape((-1,) + part.shape), others
+
+
+def split_rows(value):
+    total = value.shape[-2]
+    cut = total // 32 * 16 or total // 2
+    return value[..., :cut, :], value[..., cut:, :]
+
+
+def is_line():
+    return lax.axis_size("dp") == 8 and lax.axis_size("rep") == 4
+
+
+def line_place():
+    return lax.axis_index("dp") // 2
+
+
+def line_shift(value, step, among=range(4)):
+    pairs = [
+        (p * 8 + i, (p + step) * 8 + i) for p in among for i in range(8) if 0 <= p + step < 4
+    ]
+    return lax.ppermute(value, AXES, pairs)
+
+
+def line_gather_start(part):
+    if not is_line():
+        return (part,)
+    return part, line_shift(part, 1), line_shift(part, -1)
+
+
+def line_gather_end(parts):
+    part = parts[0]
+    if not is_line():
+        count = index_bits()
+        value = part.reshape((1,) * count + part.shape)
+        for bit in range(3, count):
+            value = gather_bit(value, bit, count - 1 - bit)
+        return value.reshape((-1, 1, 1, 1) + part.shape)
+    right, left = [parts[1]], [parts[2]]
+    for _ in range(2):
+        right.append(line_shift(right[-1], 1))
+        left.append(line_shift(left[-1], -1))
+    row = jnp.stack(right[::-1] + [part] + left)
+    row = lax.dynamic_slice_in_dim(row, 3 - line_place(), 4, 0)
+    return row.reshape((4, 1, 1, 1) + part.shape)
+
+
+def added(parts):
+    total = parts[0].astype(F32)
+    for part in parts[1:]:
+        total = total + part.astype(F32)
+    return total
+
+
+def halves(segments, bit, axis, other):
+    index = own_bit(bit) ^ other
+    return [[lax.dynamic_slice_in_dim(p, index, 1, axis) for p in s] for s in segments]
+
+
+def halve_sent(segments, bit, axis):
+    sent = [added(parts).astype(BF) for parts in halves(segments, bit, axis, 1)]
+    return sent[0] if len(sent) == 1 else jnp.concatenate(sent, axis=-2)
+
+
+def halve_end(segments, sent, bit, axis):
+    got = xor_swap(sent, 1 << bit)
+    result, at = [], 0
+    for parts in halves(segments, bit, axis, 0):
+        count = parts[0].shape[-2]
+        result.append(parts + [lax.slice_in_dim(got, at, at + count, axis=got.ndim - 2)])
+        at += count
+    return result
+
+
+def halve_bit(segments, bit, axis):
+    return halve_end(segments, halve_sent(segments, bit, axis), bit, axis)
+
+
+def cut_rows(segments):
+    total = sum(s[0].shape[-2] for s in segments)
+    cut = total // 32 * 16 or total // 2
+    low, high, at = [], [], 0
+    for s in segments:
+        count = s[0].shape[-2]
+        here = min(max(cut - at, 0), count)
+        if here:
+            low.append([p[..., :here, :] for p in s])
+        if here < count:
+            high.append([p[..., here:, :] for p in s])
+        at += count
+    return low, high
+
+
+def flat_after(*values):
+    leaves, tree = jax.tree.flatten(values)
+    return jax.tree.unflatten(tree, lax.optimization_barrier(leaves))
+
+
+def near_shape(value):
+    return value.reshape((-1, 2, 2, 2) + value.shape[1:])
+
+
+class LineScatter:
+    def __init__(self, segments):
+        self.segments = segments
+        self.right = self.left = None
+
+    def block(self, index):
+        index = jnp.clip(index, 0, 3)
+        parts = [
+            added([lax.dynamic_index_in_dim(p, index, 0, keepdims=False) for p in s])
+            for s in self.segments
+        ]
+        return jnp.concatenate(parts, axis=-2) if len(parts) > 1 else parts[0]
+
+    def step(self, number):
+        if not is_line():
+            return
+        place = line_place()
+        to_right, to_left = self.block(4 - number + place), self.block(number - 4 + place)
+        if self.right is not None:
+            to_right, to_left = added([to_right, self.right]), added([to_left, self.left])
+        self.right = line_shift(to_right.astype(BF), 1, range(number))
+        self.left = line_shift(to_left.astype(BF), -1, range(4 - number, 4))
+
+    def end(self):
+        shape = self.segments[0][0].shape
+        if is_line():
+            result = added([self.block(line_place()), self.right, self.left])
+            return result.reshape((-1, shape[-1])).astype(BF)
+        count = index_bits() - 3
+        values = [[p.reshape((2,) * count + p.shape[-2:]) for p in s] for s in self.segments]
+        for step in range(count):
+            values = halve_bit(values, step + 3, count - 1 - step)
+        values = [added(s).reshape((-1, shape[-1])).astype(BF) for s in values]
+        return jnp.concatenate(values, axis=0)
+
+    def state(self):
+        return [self.segments, self.right, self.left]
+
+    def put(self, state):
+        self.segments, self.right, self.left = state
+
+
+def gather_copy(value, bit):
+    return gather_bit(value, bit, 1 - bit)
 
 
 def gelu_parts(u):
     k = 0.7978845608028654
     square = u * u
-    t = jnp.tanh(k * u * (1.0 + 0.044715 * square))
-    half = 0.5 * (1.0 + t)
-    slope = half + 0.5 * u * (1.0 - t * t) * (k + (3 * 0.044715 * k) * square)
+    half = 0.5 + 0.5 * jnp.tanh(u * (k + (0.044715 * k) * square))
+    slope = half * (1.0 + u * (1.0 - half) * (2 * k + (6 * 0.044715 * k) * square))
     return u * half, slope
 
 
@@ -61,21 +257,97 @@
 
 
 def whole(shape):
-    return pl.BlockSpec(shape, lambda *_: (0,) * len(shape))
+    return pl.BlockSpec(shape, lambda *_: (0,) * len(shape), pipeline_mode=pl.Buffered(1))
 
 
 def along(shape, axis):
     return pl.BlockSpec(shape, lambda s: tuple(s if a == axis else 0 for a in range(len(shape))))
 
 
-def call(kernel, name, steps, ins, outs, scratch=(), flops=0):
-    arrays = [a for a, _ in ins]
+class Weight:
+    def __init__(self, gathered, at, taps, q):
+        if q % 16 == 0:
+            self.array, self.at, self.taps, self.q = gathered, at, taps, q
+        else:
+            devices = gathered.shape[0]
+            field = gathered[:, at : at + taps * q].reshape(devices, taps, q, LANES)
+            field = field.transpose(1, 0, 2, 3).reshape(1, taps * devices * q, LANES)
+            self.array, self.at, self.taps, self.q = field, 0, taps, devices * q
+
+    def held(self):
+        return pltpu.with_memory_space_constraint(self.array, pltpu.HBM)
+
+    def spec(self, rows, index, mode=None):
+        return pl.BlockSpec((self.array.shape[0], rows, LANES), index, pipeline_mode=mode)
+
+    def chunk(self, at, count):
+        rows = count * self.q
+        place = at // rows
+        return (self.held(), self.spec(rows, lambda *_: (0, place, 0), pl.Buffered(1)))
+
+    def every(self):
+        chunks, left, at = [], self.taps, self.at
+        while left:
+            count = left
+            while at % (count * self.q):
+                count -= 1
+            chunks.append(self.chunk(at, count))
+            at += count * self.q
+            left -= count
+        return chunks
+
+    def moving(self):
+        first = self.at // self.q
+        return (self.held(), self.spec(self.q, lambda s: (0, first + s, 0)))
+
+    def moving_all(self):
+        return self.chunk(self.at, self.taps)
+
+    def moving_rows(self, steps):
+        devices = self.array.shape[0]
+        if devices > 1:
+            place = self.at // self.q
+            return (
+                self.held(),
+                pl.BlockSpec((devices // steps, self.q, LANES), lambda s: (s, place, 0)),
+            )
+        return (self.held(), pl.BlockSpec((1, self.q // steps, LANES), lambda s: (0, s, 0)))
+
+
+class Taps:
+    def __init__(self, refs, total):
+        self.refs = refs
+        self.q = sum(r.shape[1] for r in refs) // total
+
+    def __getitem__(self, t):
+        row = t * self.q
+        for ref in self.refs:
+            if row < ref.shape[1]:
+                return flat(ref[:, row : row + self.q])
+            row -= ref.shape[1]
+
+
+def call(kernel, name, steps, ins, outs, scratch=(), flops=0, into=None):
+    groups = [i if isinstance(i, list) else [i] for i in ins]
+    arrays = [a for g in groups for a, _ in g]
     size = sum(a.size * a.dtype.itemsize for a in arrays)
+
+    def body(*refs):
+        params, at = [], 0
+        for i, g in zip(ins, groups):
+            some = refs[at : at + len(g)]
+            params.append(Taps(some, 9) if isinstance(i, list) else some[0])
+            at += len(g)
+        kernel(*params, *refs[at + (into is not None) :])
+
+    given = [] if into is None else [into]
+
     return pl.pallas_call(
-        kernel,
+        body,
         name=name,
         grid=(steps,),
-        in_specs=[s for _, s in ins],
+        in_specs=[s for g in groups for _, s in g] + [pl.BlockSpec(memory_space=pl.ANY)] * len(given),
+        input_output_aliases={len(arrays): 0} if given else {},
         out_specs=[s for _, _, s in outs],
         out_shape=[jax.ShapeDtypeStruct(shape, dtype) for shape, dtype, _ in outs],
         scratch_shapes=list(scratch),
@@ -83,7 +355,7 @@
             vmem_limit_bytes=VMEM, dimension_semantics=("arbitrary",)
         ),
         cost_estimate=pl.CostEstimate(flops=flops, bytes_accessed=size, transcendentals=0),
-    )(*arrays)
+    )(*arrays, *given)
 
 
 def rows3(ref, first):
@@ -160,7 +432,7 @@
         acc[...] = jnp.zeros_like(acc)
 
     rows, cols = x.shape[0], x.shape[1]
-    values = dot(flat(x[...]), w[...]).reshape(rows, cols, x.shape[2], w.shape[1])
+    values = dot(flat(x[...]), flat(w[...])).reshape(rows, cols, x.shape[2], LANES)
     z[...] = values.astype(BF)
     first, second = acc[0], acc[1]
     for r in range(rows):
@@ -181,17 +453,19 @@
     def row(i, carry):
         values = field[i]
         z[i] = values.astype(BF)
+        if limits is None:
+            return carry[0] + jnp.sum(values, axis=0), carry[1] + jnp.sum(values * values, axis=0)
         return add_stats(values, inside(limits[...], i, side), *carry)
 
     first, second = lax.fori_loop(
-        0, side, row, (jnp.zeros(shape, F32), jnp.zeros(shape, F32))
+        0, side, row, (jnp.zeros(shape, F32), jnp.zeros(shape, F32)), unroll=True
     )
     put_rows(sums, group_rows(onehot, first, second))
 
 
 def k_strided(x, w, limits, onehot, z, sums, acc):
     side = z.shape[0]
-    acc[...] = dot(flat(x[:, 0, :, 0]), w[0]).reshape(acc.shape)
+    acc[...] = dot(flat(x[:, 0, :, 0]), flat(w[...])).reshape(acc.shape)
     stats_of(acc, limits, onehot, z, sums)
 
 
@@ -239,10 +513,10 @@
         store(i, jnp.where(mask, act, 0.0).astype(BF), jnp.where(mask, grad, 0.0).astype(BF))
         return carry
 
-    lax.fori_loop(0, side, row, 0)
-
-
-def k_expand(z, in_sums, table, counts, keeps, limits, onehot, w, a, slope, z_out, sums, acc):
+    lax.fori_loop(0, side, row, 0, unroll=True)
+
+
+def k_expand(z, in_sums, table, counts, keeps, onehot, w, a, slope, z_out, sums, acc):
     @pl.when(pl.program_id(0) == 0)
     def _():
         def store(i, act, grad):
@@ -251,8 +525,8 @@
 
         activate(z, forward_coefs(in_sums, table, counts, onehot), keeps, store)
 
-    acc[...] = dot(flat(a[...]), w[0]).reshape(acc.shape)
-    stats_of(acc, limits, onehot, z_out, sums)
+    acc[...] = dot(flat(a[...]), flat(w[...])).reshape(acc.shape)
+    stats_of(acc, None, onehot, z_out, sums)
 
 
 def k_middle(
@@ -272,8 +546,8 @@
         slope[i] = jnp.where(mask, grad, 0.0).astype(BF)
         return carry
 
-    lax.fori_loop(0, side, row, 0)
-    part = dot(flat(middle[...]), w[...]).reshape(acc.shape)
+    lax.fori_loop(0, side, row, 0, unroll=True)
+    part = dot(flat(middle[...]), flat(w[...])).reshape(acc.shape)
 
     @pl.when(step == 0)
     def _():
@@ -285,7 +559,7 @@
 
     @pl.when(step == pl.num_programs(0) - 1)
     def _():
-        stats_of(acc, limits, onehot, z4, sums)
+        stats_of(acc, None, onehot, z4, sums)
 
 
 def clear_edges(padded):
@@ -335,7 +609,7 @@
         du6[i] = du.astype(BF)
         return plain + jnp.sum(du, axis=0), with_z + jnp.sum(du * z, axis=0)
 
-    plain, with_z = lax.fori_loop(0, side, row, (zero, zero))
+    plain, with_z = lax.fori_loop(0, side, row, (zero, zero), unroll=True)
     put_rows(
         sums,
         gain_rows(in_sums, counts, onehot, with_z, plain) + group_rows(onehot, plain),
@@ -351,7 +625,7 @@
         du_out[i] = du.astype(du_out.dtype)
         return plain + jnp.sum(du, axis=0), with_z + jnp.sum(du * z[i].astype(F32), axis=0)
 
-    plain, with_z = lax.fori_loop(0, slope.shape[0], row, (zero, zero))
+    plain, with_z = lax.fori_loop(0, slope.shape[0], row, (zero, zero), unroll=True)
     put_rows(
         sums,
         gain_rows(in_sums, counts, onehot, with_z, plain) + group_rows(onehot, plain),
@@ -367,7 +641,7 @@
         store(i, jnp.where(inside(limits[...], i, side), dz, 0.0).astype(BF))
         return carry
 
-    lax.fori_loop(0, side, row, 0)
+    lax.fori_loop(0, side, row, 0, unroll=True)
 
 
 def k_back_expand(
@@ -380,7 +654,7 @@
         dz6[i] = dz
 
     norm_back(du6, z6, backward_coefs(sums6, back6, table6, counts, onehot), limits, store)
-    part = dot_nt(flat(dz6[...]), w[0]).reshape(acc.shape)
+    part = dot_nt(flat(dz6[...]), flat(w[...])).reshape(acc.shape)
 
     @pl.when(step == 0)
     def _():
@@ -431,7 +705,7 @@
 
         norm_back(du4, z4, backward_coefs(sums4, back4, table4, counts, onehot), limits, store)
 
-    acc[...] = dot_nt(flat(dz4[...]), w[...]).reshape(acc.shape)
+    acc[...] = dot_nt(flat(dz4[...]), flat(w[...])).reshape(acc.shape)
     shut = 1.0 - gate[...]
     zero = jnp.zeros(shut.shape, F32)
 
@@ -446,7 +720,7 @@
             with_zs + jnp.sum(du * zs[i].astype(F32), axis=0),
         )
 
-    plain, with_z3, with_zs = lax.fori_loop(0, side, row, (zero, zero, zero))
+    plain, with_z3, with_zs = lax.fori_loop(0, side, row, (zero, zero, zero), unroll=True)
     put_rows(
         sums,
         gain_rows(sums3, counts, onehot, with_z3, plain)
@@ -475,8 +749,8 @@
         dzs[i] = jnp.where(mask, dz, 0.0).astype(BF)
         return carry
 
-    lax.fori_loop(0, side, row, 0)
-    part = dot_nt(flat(dz3[...]), w[0]).reshape(acc.shape)
+    lax.fori_loop(0, side, row, 0, unroll=True)
+    part = dot_nt(flat(dz3[...]), flat(w[...])).reshape(acc.shape)
 
     @pl.when(step == 0)
     def _():
@@ -492,7 +766,7 @@
 
 
 def k_back_strided(dzs, w, out):
-    part = dot_nt(flat(dzs[...]), w[0]).reshape(out.shape)
+    part = dot_nt(flat(dzs[...]), flat(w[...])).reshape(out.shape)
 
     @pl.when(pl.program_id(0) == 0)
     def _():
@@ -545,7 +819,7 @@
         z = z1[i, 0, :, 0].astype(F32)
         return plain + jnp.sum(du, axis=0), with_z + jnp.sum(du * z, axis=0)
 
-    plain, with_z = lax.fori_loop(0, side, row, (total[0], total[1]))
+    plain, with_z = lax.fori_loop(0, side, row, (total[0], total[1]), unroll=True)
     total[0] = plain
     total[1] = with_z
 
@@ -557,7 +831,7 @@
         )
 
 
-def k_back_first(du1, z1, sums1, back1, table1, counts, limits, onehot, w, strided, dz1, dx):
+def k_back_first(du1, z1, sums1, back1, table1, counts, limits, onehot, x, dz1, grad, acc):
     step = pl.program_id(0)
     rows, cols = du1.shape[0], du1.shape[1]
     factor, on_z, on_one = backward_coefs(sums1, back1, table1, counts, onehot)
@@ -565,11 +839,44 @@
         dz = du1[r].astype(F32) * factor + z1[r].astype(F32) * on_z + on_one
         mask = inside(limits[...], rows * step + r, cols)
         dz1[r] = jnp.where(mask, dz, 0.0).astype(BF)
+    part = dot_tn(flat(x[...]), flat(dz1[...]))
+
+    @pl.when(step == 0)
+    def _():
+        acc[...] = part
+
+    @pl.when(step > 0)
+    def _():
+        acc[...] += part
+
+    @pl.when(step == pl.num_programs(0) - 1)
+    def _():
+        grad[...] = acc[...].astype(BF).reshape(grad.shape)
+
+
+def k_input_grad(dz1, w, strided, dx):
+    rows, cols = dz1.shape[0], dz1.shape[1]
+    weights = flat(w[...])
     for r in range(rows):
-        part = dot_nt(flat(dz1[r]), w[...]).reshape(dx.shape[1:])
-        dx[r] = part
+        dx[r] = dot_nt(flat(dz1[r]), weights).reshape(dx.shape[1:])
     for j in range(cols // 2):
         dx[0, 2 * j] += strided[0, j]
+
+
+def k_grad(source, dz, out):
+    out[...] = dot_tn(flat(source[...]), flat(dz[...])).astype(BF).reshape(out.shape)
+
+
+def k_grad_columns(source, dz, out, turned):
+    @pl.when(pl.program_id(0) == 0)
+    def _():
+        turned[...] = flat(source[...]).T
+
+    out[...] = dot(turned[...], flat(dz[...])).astype(BF).reshape(out.shape)
+
+
+def k_grad_strided(x, dz, out, turned):
+    k_grad_columns(x.at[:, 0, :, 0], dz, out, turned)
 
 
 def k_taps(field, dz, out):
@@ -577,7 +884,7 @@
     v, h = t // 3, t % 3
     side = dz.shape[0]
     rows = field[pl.ds(v, side), pl.ds(h, side)]
-    out[0] = dot_tn(flat(rows), flat(dz[...])).astype(BF)
+    out[...] = dot_tn(flat(rows), flat(dz[...])).astype(BF).reshape(out.shape)
 
 
 def k_taps_strided(planes, dz, out):
@@ -585,7 +892,7 @@
     v, h = t // 3, t % 3
     side = dz.shape[0]
     rows = planes[(v + 1) % 2, (h + 1) % 2, pl.ds(v // 2, side), pl.ds(h // 2, side)]
-    out[0] = dot_tn(flat(rows), flat(dz[...])).astype(BF)
+    out[...] = dot_tn(flat(rows), flat(dz[...])).astype(BF).reshape(out.shape)
 
 
 def body(
@@ -641,42 +948,89 @@
         rows = weights.shape[-2] // copies
         part = lax.dynamic_slice_in_dim(weights, copy * rows, rows, weights.ndim - 2)
         part = part.reshape((-1,) + part.shape[-2:])
-        return jnp.concatenate(
-            [part[..., i : i + LANES] for i in range(0, part.shape[-1], LANES)], axis=0
+        return flat(
+            jnp.concatenate(
+                [part[..., i : i + LANES] for i in range(0, part.shape[-1], LANES)], axis=0
+            )
         )
 
-    def gather_weights(weights):
+    def layout(weights):
+        taps = weights.shape[0] if weights.ndim == 3 else weights.shape[1] // LANES
+        return taps, weights.shape[-2] // copies
+
+    def joined(weights):
         parts = [quarter(w) for w in weights]
-        rows = jnp.concatenate([flat(p) for p in parts], axis=0)
-        gathered = lax.all_gather(rows, AXES, axis=0, tiled=False)
+        return parts[0] if len(parts) == 1 else jnp.concatenate(parts, axis=0)
+
+    def views(gathered, weights):
         result, at = [], 0
-        for p in parts:
-            size = p.shape[0] * p.shape[1]
-            field = gathered[:, at : at + size].reshape((devices,) + p.shape)
-            result.append(field.transpose(1, 0, 2, 3).reshape(p.shape[0], -1, LANES))
-            at += size
+        for w in weights:
+            taps, q = layout(w)
+            result.append(Weight(gathered, at, taps, q))
+            at += taps * q
         return result
 
-    def scatter_grads(grads, shapes):
-        parts = []
-        for g in grads:
-            q = g.shape[1] // devices
-            field = g.reshape(g.shape[0], devices, q, LANES).transpose(1, 0, 2, 3)
-            parts.append(field.reshape(devices, -1, LANES))
-        rows = jnp.concatenate(parts, axis=1).reshape(-1, LANES)
-        own = lax.psum_scatter(rows, AXES, scatter_dimension=0, tiled=True)
-        gathered = lax.all_gather(own, "rep", axis=0, tiled=False)
+    def everywhere(weights):
+        return views(lax.all_gather(joined(weights), AXES, axis=0, tiled=False), weights)
+
+    def shares(own, weights):
+        gathered = own.reshape((copies,) + own.shape[-2:])
         result, at = [], 0
-        for g, shape in zip(grads, shapes):
-            t, q = g.shape[0], g.shape[1] // devices
-            field = gathered[:, at : at + t * q].reshape(copies, t, q, LANES)
-            if len(shape) == 3:
+        for w in weights:
+            taps, q = layout(w)
+            field = gathered[:, at : at + taps * q].reshape(copies, taps, q, LANES)
+            if w.ndim == 3:
                 field = field.transpose(1, 0, 2, 3)
             else:
                 field = field.transpose(0, 2, 1, 3)
-            result.append(field.reshape(shape).astype(F32))
-            at += t * q
+            result.append(field.reshape(w.shape).astype(F32))
+            at += taps * q
         return result
+
+    def packs(weights):
+        return all(layout(w)[1] % 16 == 0 for w in weights)
+
+    def grad_out(weights, steps, at=0, total=None):
+        taps, q = layout(weights)
+        if q % 16:
+            shape = (taps * devices * q, LANES)
+            return (shape, BF, pl.BlockSpec((shape[0] // steps, LANES), lambda s: (s, 0)))
+        shape = (devices, total or taps * q, LANES)
+        first = at // q
+        if taps > 1:
+            return (shape, BF, pl.BlockSpec((devices, q, LANES), lambda s: (0, first + s, 0)))
+        return (shape, BF, pl.BlockSpec((devices // steps, q, LANES), lambda s: (s, first, 0)))
+
+    def grad_rows(grad, weights):
+        taps, q = layout(weights)
+        if q % 16 == 0:
+            return grad
+        field = grad.reshape(taps, devices, q, LANES).transpose(1, 0, 2, 3)
+        return field.reshape(devices, taps * q, LANES)
+
+    def grads_into(weights):
+        total = sum(layout(w)[0] * layout(w)[1] for w in weights)
+        results = {}
+
+        def run(index, kernel, name, steps, ins, flops, scratch=()):
+            w = weights[index]
+            at = sum(layout(v)[0] * layout(v)[1] for v in weights[:index])
+            if packs(weights):
+                (results["all"],) = call(
+                    kernel, name, steps, ins, [grad_out(w, steps, at, total)], scratch, flops,
+                    into=results.get("all"),
+                )
+            else:
+                (results[index],) = call(kernel, name, steps, ins, [grad_out(w, steps)], scratch, flops)
+
+        def whole_rows():
+            if "all" in results:
+                return results["all"]
+            return jnp.concatenate(
+                [grad_rows(results[i], w) for i, w in enumerate(weights)], axis=1
+            )
+
+        return run, whole_rows
 
     tables_all = (
         entry_norm_reduce,
@@ -687,19 +1041,30 @@
         inner_norm_spatial,
         inner_norm_expand,
     )
-    w_reduce = lax.all_gather(entry_reduce, "dp", axis=0, tiled=True)
-    tables_flat = jnp.concatenate([t.reshape(2 * GROUPS, -1) for t in tables_all], axis=1)
-    tables_flat = lax.all_gather(tables_flat, "dp", axis=0, tiled=False)
+    w_spatial, w_expand = everywhere([entry_spatial, entry_expand])
+    table_cells = jnp.concatenate([t.reshape(2 * GROUPS, -1) for t in tables_all], axis=1)
+    table_rows = -(-table_cells.size // (copies * LANES))
+    table_part = jnp.pad(
+        table_cells.reshape(-1), (0, copies * table_rows * LANES - table_cells.size)
+    ).reshape(copies, table_rows, LANES)
+    table_part = lax.dynamic_index_in_dim(table_part, copy, 0, keepdims=False)
+    middle_weights = [entry_project, inner_reduce]
+    last_weights = [inner_spatial, inner_expand]
+    first_array, others = gather_rows(
+        jnp.concatenate([quarter(entry_reduce), table_part], axis=0), middle_weights + last_weights
+    )
+    w_ispatial, w_iexpand = everywhere(others[2:])
+    first_array, part = after(first_array, joined(others[:2]))
+    (w_reduce,) = views(first_array, [entry_reduce])
+    line = line_gather_start(part)
+    tables_flat = first_array[:, -table_rows:].reshape(shards, -1)[:, : table_cells.size]
+    tables_flat = tables_flat.reshape((shards,) + table_cells.shape)
     tables, at = [], 0
     for t in tables_all:
         width = t.shape[2]
         field = tables_flat[:, :, at : at + width].transpose(1, 0, 2)
         tables.append(field.reshape(2 * GROUPS, shards * width).astype(F32))
         at += width
-    w_spatial, w_expand, w_project, w_ireduce, w_ispatial, w_iexpand = gather_weights(
-        [entry_spatial, entry_expand, entry_project, inner_reduce, inner_spatial, inner_expand]
-    )
-    w_ireduce = w_ireduce[0]
 
     x = inputs.transpose(1, 2, 0, 3)
     x_split = x.reshape(half, 2, half, 2, images, wide)
@@ -717,9 +1082,6 @@
 
     def column(array):
         return (array, along(array.shape[:-1] + (LANES,), array.ndim - 1))
-
-    def tap(array):
-        return (array, along((1,) + array.shape[1:], 0))
 
     small_out = (small, BF, whole(small))
     large_out = (large, BF, along(small, 3))
@@ -737,12 +1099,18 @@
     )
     z1, sums1 = call(
         k_first, "first", half,
-        [(x, along((2, full, images, wide), 0)), fixed(w_reduce), fixed(limits_in), fixed(onehot),
+        [(x, along((2, full, images, wide), 0)), w_reduce.moving_all(), fixed(limits_in), fixed(onehot),
          fixed(count_row)],
         [((full, full, images, mid), BF, along((2, full, images, mid), 0)), sums_out],
         [pltpu.VMEM((2, images, mid), F32)], flops=2 * rows_in * wide * mid,
     )
-    sums1 = sum_everywhere(sums1)
+    sums1, z1, *line = after(sums1, z1, *line)
+    sums1, *line = after(sum_everywhere(sums1), *line)
+    low, high = split_rows(line_gather_end(line))
+    low, high = gather_bit(low, 2, 1), gather_bit(high, 1, 2)
+    low, high, w_spatial.array, z1 = after(low, high, w_spatial.array, z1)
+    w_expand.array = w_spatial.array if w_expand.at else w_expand.array
+    low, high = gather_bit(low, 1, 2), gather_bit(high, 2, 1)
     totals = sums1[2 * GROUPS, 0 : 128 * GROUPS : 128]
     side_real = group_side.astype(F32)
     half_real = (group_side // 2).astype(F32)
@@ -753,32 +1121,36 @@
     limits_in, limits_out = fixed(limits_in), fixed(limits_out)
     keeps_in, keeps_out = fixed(keeps_in), fixed(keeps_out)
 
-    zs, sums_s = call(
-        k_strided, "strided", blocks,
-        [(x_split, whole((half, 1, half, 1, images, wide))), tap(w_project), limits_out, onehot],
-        [large_out, sums_wide], [acc], flops=2 * rows_out * wide * out,
-    )
     z1_split = z1.reshape(split)
     row_split = (1, 2, half, 2, images, LANES)
     planes_shape = (2, 2, half + 1, half + 1, images, mid)
     planes, slope1, z2, sums2 = call(
         k_entry_spatial, "entry_spatial", half,
         [(z1_split, along(row_split, 0)), fixed(sums1), fixed(tables[0]), counts_in, counts,
-         keeps_in, limits_out, onehot, fixed(w_spatial)],
+         keeps_in, limits_out, onehot, w_spatial.every()],
         [(planes_shape, BF, whole(planes_shape)), (split, BF, along(row_split, 0)), small_out,
          sums_out],
         [acc], flops=18 * rows_out * mid * mid,
     )
+    sums2, low, high = after(sums2, low, high)
+    values = [gather_bit(v, 0, 3) for v in (low, high)]
+    gathered = jnp.concatenate(values, axis=4).reshape(devices, -1, LANES)
+    w_project, w_ireduce = views(gathered, middle_weights)
     sums2 = sum_everywhere(sums2)
+    zs, sums_s = call(
+        k_strided, "strided", blocks,
+        [(x_split, whole((half, 1, half, 1, images, wide))), w_project.moving(), limits_out, onehot],
+        [large_out, sums_wide], [acc], flops=2 * rows_out * wide * out,
+    )
     a2, slope2, z3, sums3 = call(
         k_expand, "expand", blocks,
-        [fixed(z2), fixed(sums2), fixed(tables[1]), counts, keeps_out, limits_out, onehot,
-         tap(w_expand)],
+        [fixed(z2), fixed(sums2), fixed(tables[1]), counts, keeps_out, onehot,
+         w_expand.moving()],
         [small_out, small_out, large_out, sums_wide], [acc], flops=2 * rows_out * mid * out,
     )
     joined = sum_everywhere(jnp.concatenate([sums3, sums_s], axis=1))
     sums3, sums_s = joined[:, :out], joined[:, out:]
-    w_rows = (w_ireduce, along((LANES, mid), 0))
+    w_rows = w_ireduce.moving_rows(blocks)
     middle, slope3, z4, sums4 = call(
         k_middle, "middle", blocks,
         [column(z3), column(zs), column(sums3), column(sums_s), column(tables[2]),
@@ -790,15 +1162,15 @@
     padded4, slope4, z5, sums5 = call(
         k_inner_spatial, "inner_spatial", 1,
         [fixed(z4), fixed(sums4), fixed(tables[4]), counts, keeps_out, limits_out, onehot,
-         fixed(w_ispatial)],
+         w_ispatial.every()],
         [(padded_shape, BF, whole(padded_shape)), small_out, small_out, sums_out], [acc],
         flops=18 * rows_out * mid * mid,
     )
     sums5 = sum_everywhere(sums5)
     a5, slope5, z6, sums6 = call(
         k_expand, "inner_expand", blocks,
-        [fixed(z5), fixed(sums5), fixed(tables[5]), counts, keeps_out, limits_out, onehot,
-         tap(w_iexpand)],
+        [fixed(z5), fixed(sums5), fixed(tables[5]), counts, keeps_out, onehot,
+         w_iexpand.moving()],
         [small_out, small_out, large_out, sums_wide], [acc], flops=2 * rows_out * mid * out,
     )
     sums6 = sum_everywhere(sums6)
@@ -812,25 +1184,30 @@
     dz6, du5, back5 = call(
         k_back_expand, "back_inner_expand", blocks,
         [column(du6), column(z6), column(sums6), column(back6), column(tables[6]), counts,
-         limits_out, onehot, tap(w_iexpand), fixed(slope5), fixed(z5), fixed(sums5)],
+         limits_out, onehot, w_iexpand.moving(), fixed(slope5), fixed(z5), fixed(sums5)],
         [large_out, (small, F32, whole(small)), sums_out], [acc],
         flops=2 * rows_out * mid * out,
     )
-    back5 = sum_everywhere(back5)
-    g_iexpand = weight_blocks(a5, dz6)
+    near, dz6 = after(sum_near(back5), dz6)
+    back5 = sum_far(near, LANES)
+    inner_grad, inner_rows = grads_into([inner_spatial, inner_expand])
+    inner_grad(
+        1, k_grad_columns, "inner_expand_grad", blocks, [fixed(a5), column(dz6)],
+        2 * rows_out * mid * out, [pltpu.VMEM((mid, rows_out), BF)],
+    )
     dz5, du4, back4 = call(
         k_back_inner_spatial, "back_inner_spatial", 1,
         [fixed(du5), fixed(z5), fixed(sums5), fixed(back5), fixed(tables[5]), counts, limits_out,
-         onehot, fixed(w_ispatial), fixed(slope4), fixed(z4), fixed(sums4)],
+         onehot, w_ispatial.every(), fixed(slope4), fixed(z4), fixed(sums4)],
         [small_out, (small, F32, whole(small)), sums_out],
         [pltpu.VMEM(padded_shape, BF), acc], flops=18 * rows_out * mid * mid,
     )
-    back4 = sum_everywhere(back4)
-    taps_out = ((9, mid, mid), BF, along((1, mid, mid), 0))
-    (g_ispatial,) = call(
-        k_taps, "inner_spatial_grad", 9, [fixed(padded4), fixed(dz5)], [taps_out],
-        flops=18 * rows_out * mid * mid,
-    )
+    near, dz5 = after(sum_near(back4), dz5)
+    inner_grad(
+        0, k_taps, "inner_spatial_grad", 9, [fixed(padded4), fixed(dz5)], 18 * rows_out * mid * mid
+    )
+    late_rows, back4 = after(inner_rows().reshape(-1, LANES), sum_far(near, LANES))
+    inner_own = lax.psum_scatter(late_rows, AXES, scatter_dimension=0, tiled=True)
     dz4, du3, back3 = call(
         k_back_middle, "back_middle", blocks,
         [fixed(du4), fixed(z4), fixed(sums4), fixed(back4), fixed(tables[4]), counts, limits_out,
@@ -839,28 +1216,37 @@
         [small_out, large_out, ((16, out), F32, along((16, LANES), 1))], [acc],
         flops=2 * rows_out * mid * out,
     )
-    back3 = sum_everywhere(back3)
-    g_ireduce = dot_tn(flat(middle), flat(dz4)).astype(BF)[None]
-    inner_grads = scatter_grads(
-        (g_ireduce, g_ispatial, g_iexpand),
-        (inner_reduce.shape, inner_spatial.shape, inner_expand.shape),
+    near, dz4 = after(sum_near(back3), dz4)
+    back3 = sum_far(near, out)
+    middle_grads = [entry_project, inner_reduce, entry_expand]
+    middle_grad, middle_rows = grads_into(middle_grads)
+    middle_grad(
+        1, k_grad, "inner_reduce_grad", blocks, [column(middle), fixed(dz4)],
+        2 * rows_out * mid * out,
     )
     dz3, dzs, du2, back2 = call(
         k_back_entry_expand, "back_entry_expand", blocks,
         [column(du3), column(z3), column(zs), column(sums3), column(sums_s), column(back3),
-         column(tables[2]), column(tables[3]), counts, limits_out, onehot, tap(w_expand),
+         column(tables[2]), column(tables[3]), counts, limits_out, onehot, w_expand.moving(),
          fixed(slope2), fixed(z2), fixed(sums2)],
         [large_out, large_out, (small, F32, whole(small)), sums_out], [acc],
         flops=2 * rows_out * mid * out,
     )
-    back2 = sum_everywhere(back2)
+    near, dz3, dzs = after(sum_near(back2), dz3, dzs)
+    back2 = sum_far(near, LANES)
+    middle_grad(
+        2, k_grad_columns, "expand_grad", blocks, [fixed(a2), column(dz3)],
+        2 * rows_out * mid * out, [pltpu.VMEM((mid, rows_out), BF)],
+    )
+    middle_grad(
+        0, k_grad_strided, "project_grad", blocks,
+        [(x_split, whole((half, 1, half, 1, images, wide))), column(dzs)],
+        2 * rows_out * wide * out, [pltpu.VMEM((wide, rows_out), BF)],
+    )
+    low, high = cut_rows(halve_bit([[near_shape(middle_rows())]], 0, 3))
+    low_sent, high_sent, back2 = after(halve_sent(low, 1, 2), halve_sent(high, 2, 1), back2)
+    low, high = halve_end(low, low_sent, 1, 2), halve_end(high, high_sent, 2, 1)
     strided_shape = (half, half, images, wide)
-    (d_strided,) = call(
-        k_back_strided, "back_strided", blocks, [column(dzs), tap(w_project)],
-        [(strided_shape, F32, whole(strided_shape))], flops=2 * rows_out * wide * out,
-    )
-    g_expand = weight_blocks(a2, dz3)
-    g_project = weight_blocks(x_split[:, 0, :, 0], dzs)
     plane = (half, 1, half, 1, images, LANES)
 
     def parity(array):
@@ -869,31 +1255,92 @@
     dz2, du1, back1 = call(
         k_back_entry_spatial, "back_entry_spatial", 4,
         [fixed(du2), fixed(z2), fixed(sums2), fixed(back2), fixed(tables[1]), counts, counts_in,
-         limits_out, onehot, fixed(w_spatial), parity(slope1), parity(z1_split), fixed(sums1)],
+         limits_out, onehot, w_spatial.every(), parity(slope1), parity(z1_split), fixed(sums1)],
         [small_out, (split, BF, parity(z1_split)[1]), sums_out],
         [pltpu.VMEM((half + 1, half + 1, images, mid), BF), pltpu.VMEM((2, images, mid), F32), acc],
         flops=18 * rows_out * mid * mid,
     )
-    back1 = sum_everywhere(back1)
     (g_spatial,) = call(
-        k_taps_strided, "entry_spatial_grad", 9, [fixed(planes), fixed(dz2)], [taps_out],
+        k_taps_strided, "entry_spatial_grad", 9, [fixed(planes), fixed(dz2)],
+        [grad_out(entry_spatial, 9)],
         flops=18 * rows_out * mid * mid,
     )
+    spatial_rows = [[near_shape(grad_rows(g_spatial, entry_spatial))]]
+    spatial_sent = halve_sent(spatial_rows, 0, 3)
+    back1, low_sent, high_sent, spatial_sent = after(
+        back1, halve_sent(low, 2, 1), halve_sent(high, 1, 2), spatial_sent
+    )
+    near, low_sent, high_sent = after(sum_near(back1), low_sent, high_sent)
+    low, high = halve_end(low, low_sent, 2, 1), halve_end(high, high_sent, 1, 2)
+    back1 = sum_far(near, LANES)
+    spatial_rows = halve_end(spatial_rows, spatial_sent, 0, 3)
     two = (2, full, images, mid)
-    dz1, d_inputs = call(
+    taps, q = layout(entry_reduce)
+    flat_shape = (devices, q, LANES) if q % 16 == 0 else (devices * q, LANES)
+    dz1, g_reduce = call(
         k_back_first, "back_first", half,
         [(du1.reshape(z1.shape), along(two, 0)), (z1, along(two, 0)), fixed(sums1), fixed(back1),
-         fixed(tables[0]), counts_in, limits_in, onehot, fixed(w_reduce),
+         fixed(tables[0]), counts_in, limits_in, onehot, (x, along((2, full, images, wide), 0))],
+        [(z1.shape, BF, along(two, 0)), (flat_shape, BF, whole(flat_shape))],
+        [pltpu.VMEM((wide, mid), F32)], flops=2 * rows_in * wide * mid,
+    )
+    first_rows = [[added(v).astype(BF)] for v in low + high]
+    first_rows, g_reduce, dz1, dzs, inner_own = flat_after(
+        first_rows, g_reduce, dz1, dzs, inner_own
+    )
+    reduce_rows = halve_bit([[near_shape(grad_rows(g_reduce, entry_reduce))]], 0, 3)
+    low, high = cut_rows(spatial_rows + reduce_rows)
+    first_rows, low_sent, high_sent, dz1, dzs = flat_after(
+        first_rows, halve_sent(low, 1, 2), halve_sent(high, 2, 1), dz1, dzs
+    )
+    first_line = LineScatter(first_rows)
+    first_line.step(1)
+    low, high = halve_end(low, low_sent, 1, 2), halve_end(high, high_sent, 2, 1)
+    inner_own = gather_copy(inner_own.reshape(1, 1, -1, LANES), 1)
+    (d_strided,) = call(
+        k_back_strided, "back_strided", blocks, [column(dzs), w_project.moving()],
+        [(strided_shape, F32, whole(strided_shape))], flops=2 * rows_out * wide * out,
+    )
+    first_state, low_sent, high_sent, d_strided, inner_own = flat_after(
+        first_line.state(), halve_sent(low, 2, 1), halve_sent(high, 1, 2), d_strided, inner_own
+    )
+    first_line.put(first_state)
+    first_line.step(2)
+    low, high = halve_end(low, low_sent, 2, 1), halve_end(high, high_sent, 1, 2)
+    inner_own = gather_copy(inner_own, 0)
+    (d_inputs,) = call(
+        k_input_grad, "input_grad", half,
+        [(dz1, along(two, 0)), w_reduce.moving_all(),
          (d_strided, along((1, half, images, wide), 0))],
-        [(z1.shape, BF, along(two, 0)),
-         ((full, full, images, wide), F32, along((2, full, images, wide), 0))],
+        [((full, full, images, wide), F32, along((2, full, images, wide), 0))],
         flops=2 * rows_in * wide * mid,
     )
-    g_reduce = dot_tn(flat(x), flat(dz1)).astype(BF)[None]
-    entry_grads = scatter_grads(
-        (g_reduce, g_spatial, g_expand, g_project),
-        (entry_reduce.shape, entry_spatial.shape, entry_expand.shape, entry_project.shape),
-    )
+    last_rows = [[added(v).astype(BF)] for v in low + high]
+    first_state, last_rows, d_inputs, inner_own = flat_after(
+        first_line.state(), last_rows, d_inputs, inner_own
+    )
+    first_line.put(first_state)
+    first_line.step(3)
+    last_line = LineScatter(last_rows)
+    last_line.step(1)
+    g_ispatial, g_iexpand = shares(inner_own, [inner_spatial, inner_expand])
+    first_state, last_state, g_ispatial, g_iexpand = flat_after(
+        first_line.state(), last_line.state(), g_ispatial, g_iexpand
+    )
+    first_line.put(first_state)
+    last_line.put(last_state)
+    last_line.step(2)
+    entry_own = gather_copy(first_line.end().reshape(1, 1, -1, LANES), 1)
+    entry_own, last_state = flat_after(entry_own, last_line.state())
+    last_line.put(last_state)
+    last_line.step(3)
+    entry_own = gather_copy(entry_own, 0)
+    entry_own, last_state = flat_after(entry_own, last_line.state())
+    last_line.put(last_state)
+    last_own = gather_copy(last_line.end().reshape(1, 1, -1, LANES), 1)
+    g_project, g_ireduce, g_expand = shares(entry_own, middle_grads)
+    last_own, g_project, g_ireduce, g_expand = after(last_own, g_project, g_ireduce, g_expand)
+    g_spatial, g_reduce = shares(gather_copy(last_own, 0), [entry_spatial, entry_reduce])
 
     def own_share(back, gain_at=0):
         width = back.shape[1] // shards
@@ -903,21 +1350,21 @@
     return (
         result.transpose(2, 0, 1, 3),
         d_inputs.transpose(2, 0, 1, 3),
-        *entry_grads,
+        g_reduce,
+        g_spatial,
+        g_expand,
+        g_project,
         own_share(back1),
         own_share(back2),
         own_share(back3),
         own_share(back3, 2 * GROUPS),
-        *inner_grads,
+        g_ireduce,
+        g_ispatial,
+        g_iexpand,
         own_share(back4),
         own_share(back5),
         own_share(back6),
     )
-
-
-def weight_blocks(source, dz):
-    grad = dot_tn(flat(source), flat(dz)).astype(BF)
-    return jnp.stack([grad[:, i : i + LANES] for i in range(0, grad.shape[1], LANES)])
 
 
 def solution(mesh):

time: 856 us -> 664 us (0.78)
  waiting for transfers between devices: 368 us -> 184 us
  starting transfers between devices: 96.9 us -> 168 us
  Pallas kernels: 200 us -> 154 us
  blocking collectives: 32.6 us -> 0 us
  matrix products: 26.6 us -> 0 us
  local copies, waits for them, and re-layouts: 75.8 us -> 94.8 us
    reduce_scatter x2 -> x1, waiting for transfers between devices: 151 us -> 0.02 us  [body(): lax.psum_scatter(late_rows, AXES, scatter_dimension=0, tiled=True)]
    all_gather x4 -> x2, waiting for transfers between devices: 135 us -> 0.04 us  [everywhere(): lax.all_gather(joined(weights), AXES, axis=0, tiled=False)]
    ppermute x84 -> x116, waiting for transfers between devices: 81.6 us -> 160 us  [xor_swap(): return lax.ppermute(value, AXES, [(d, d ^ distance) for d in range(count)])]
    unnamed x69 -> x214, local copies, waits for them, and re-layouts: 11.3 us -> 76.1 us
    pallas_call x17 -> x22, Pallas kernels: 200 us -> 154 us  [call(): pl.pallas_call(body, name=name, grid=(steps,), in_specs=[s for g in group...]
    ppermute x0 -> x18, starting transfers between devices: none -> 40.7 us  [line_shift(): return lax.ppermute(value, AXES, pairs)]
    all_gather x1 -> x0, blocking collectives: 32.6 us -> none  [body(): tables_flat = lax.all_gather(tables_flat, 'dp', axis=0, tiled=False)]
    ppermute x84 -> x116, starting transfers between devices: 96.7 us -> 127 us  [xor_swap(): return lax.ppermute(value, AXES, [(d, d ^ distance) for d in range(count)])]
  transfers between devices with their start and end apart: 90 -> 137, of which waited for: 59 -> 88; matrix products, arithmetic and copies ran while one was open for 11% -> 9% of each run, Pallas kernels for 10% -> 18%
where the time goes in v2:
time: 664 us; the launch traced here: 656 us
  waiting for transfers between devices  184 us (28%)
  starting transfers between devices  168 us (25%)
  Pallas kernels  154 us (23%)
  local copies, waits for them, and re-layouts  94.8 us (14%)
  other arithmetic  37.3 us (6%)
  between operations  18.7 us (3%)
    ppermute x116, waiting for transfers between devices, xor_swap(): return lax.ppermute(value, AXES, [(d, d ^ distance) for d in range(count)])  160 us
    pallas_call x22, Pallas kernels, call(): pl.pallas_call(body, name=name, grid=(steps,), in_specs=[s for g in group...  154 us
    ppermute x116, starting transfers between devices, xor_swap(): return lax.ppermute(value, AXES, [(d, d ^ distance) for d in range(count)])  127 us
    unnamed x214, local copies, waits for them, and re-layouts  76.1 us
    ppermute x18, starting transfers between devices, line_shift(): return lax.ppermute(value, AXES, pairs)  40.7 us
    ppermute x18, waiting for transfers between devices, line_shift(): return lax.ppermute(value, AXES, pairs)  23 us
  transfers between devices with their start and end apart: 137, of which 88 were waited for; matrix products, arithmetic and copies ran while one was open for 9% of the time, Pallas kernels for 18%

profile of v2, /device:TPU:0, one launch (start us, length us, event | category | flops | bytes accessed | tf_op | source)
XLA Modules:
  0.0 655.9 jit_solution(2558131323887689882)
XLA Ops:
  41.6 10.8 %collective-permute-done.3 = bf16[2,2,2,1,1,35,512]{6,5,4,3,2,1,0:T(8,128)(2,1)} collective-permute-done((bf16[2,2,2,1,1,35,512]{6,5,4,3,2,1,0:T(8,128)(2,1)S(1)}, bf16[2,2,2,1,1,35,512]{6,5,4,3,2,1,0:T(8,128)(2,1)}, u32[]{:S(2)}, u32[]{:S(2)}) %collective-permute-start.3) | collective-permute-done | bytes 286752 | tf_op jit(solution)/shard_map/ppermute | solution.py:21
  60.2 6.4 first.1
  72.3 6.1 collective-permute-start.10
  103.0 5.8 collective-permute-done.17
  112.1 7.3 %collective-permute-done.18 = bf16[4,1,1,1,96,512]{5,4,3,2,1,0:T(8,128)(2,1)S(1)} collective-permute-done((bf16[4,1,1,1,96,512]{5,4,3,2,1,0:T(8,128)(2,1)S(1)}, bf16[4,1,1,1,96,512]{5,4,3,2,1,0:T(8,128)(2,1)S(1)}, u32[]{:S(2)}, u32[]{:S(2)}) %collective-permute-start.18) | collective-permute-done | bytes 393248 | tf_op jit(solution)/shard_map/ppermute | solution.py:21
  125.7 12.2 %entry_spatial.1 = (bf16[2,2,8,8,16,512]{5,4,3,2,1,0:T(8,128)(2,1)S(1)}, bf16[7,2,7,2,16,512]{5,4,3,2,1,0:T(8,128)(2,1)S(1)}, bf16[7,7,16,512]{3,2,1,0:T(8,128)(2,1)S(1)}, f32[8,512]{1,0:T(8,128)S(1)}) custom-call(bf16[7,2,7,2,16,512]{5,4,3,2,1,0:T(8,128)(2,1)S(1)} %bitcast.236, f32[8,512]{1,0:T(8,128)S(1)} %add_add_fusion.22.refs_1_.refs_12_.refs_2_, ...), custom_call_target="tpu_custom_call" | custom-call | flops 3699376128 | bytes 10231808 | tf_op jit(solution)/shard_map/entry_spatial/pallas_call | solution.py:345
  164.6 5.7 expand.1
  181.5 6.3 strided.1
  211.0 9.4 %middle.1 = (bf16[7,7,16,2048]{3,2,1,0:T(8,128)(2,1)S(1)}, bf16[7,7,16,2048]{3,2,1,0:T(8,128)(2,1)S(1)}, bf16[7,7,16,512]{3,2,1,0:T(8,128)(2,1)S(1)}, f32[8,512]{1,0:T(8,128)S(1)}) custom-call(bf16[7,7,16,2048]{3,2,1,0:T(8,128)(2,1)S(1)} %copy-done.6, bf16[7,7,16,2048]{3,2,1,0:T(8,128)(2,1)S(1)} %copy-done.9, ...), custom_call_target="tpu_custom_call" | custom-call | flops 1644167168 | bytes 13080576 | tf_op jit(solution)/shard_map/middle/pallas_call | solution.py:345
  242.7 7.0 %inner_spatial.1 = (bf16[9,9,16,512]{3,2,1,0:T(8,128)(2,1)S(1)}, bf16[7,7,16,512]{3,2,1,0:T(8,128)(2,1)S(1)}, bf16[7,7,16,512]{3,2,1,0:T(8,128)(2,1)S(1)}, f32[8,512]{1,0:T(8,128)S(1)}) custom-call(bf16[7,7,16,512]{3,2,1,0:T(8,128)(2,1)S(1)} %copy-done.49, f32[8,512]{1,0:T(8,128)S(1)} %add_add_fusion.18.refs_1_.refs_11_.refs_2_, ...), custom_call_target="tpu_custom_call" | custom-call | flops 3699376128 | bytes 7817216 | tf_op jit(solution)/shard_map/inner_spatial/pallas_call | solution.py:345
  299.8 9.2 %close.1 = (bf16[7,7,16,2048]{3,2,1,0:T(8,128)(2,1)}, bf16[7,7,16,2048]{3,2,1,0:T(8,128)(2,1)S(1)}, f32[8,2048]{1,0:T(8,128)S(1)}) custom-call(bf16[7,7,16,2048]{3,2,1,0:T(8,128)(2,1)S(1)} %copy-done.23, f32[8,2048]{1,0:T(8,128)S(1)} %pad_maximum_fusion.29.refs_1_.refs_2_, f32[6,2048]{1,0:T(8,128)S(1)} %bitcast.254, ...), custom_call_target="tpu_custom_call" | custom-call | bytes 9918464 | tf_op jit(solution)/shard_map/close/pallas_call | solution.py:345
  326.5 6.3 back_inner_expand.1
  349.8 6.6 %back_inner_spatial.1 = (bf16[7,7,16,512]{3,2,1,0:T(8,128)(2,1)S(1)}, f32[7,7,16,512]{3,2,1,0:T(8,128)S(1)}, f32[8,512]{1,0:T(8,128)S(1)}) custom-call(f32[7,7,16,512]{3,2,1,0:T(8,128)S(1)} %get-tuple-element.203.refs_0_, bf16[7,7,16,512]{3,2,1,0:T(8,128)(2,1)S(1)} %get-tuple-element.194.refs_0_.refs_10_.refs_1_, ...), custom_call_target="tpu_custom_call" | custom-call | flops 3699376128 | bytes 11028480 | tf_op jit(solution)/shard_map/back_inner_spatial/pallas_call | solution.py:345
  370.3 7.0 %inner_spatial_grad.1 = bf16[32,208,512]{2,1,0:T(8,128)(2,1)S(1)} custom-call(bf16[9,9,16,512]{3,2,1,0:T(8,128)(2,1)S(1)} %get-tuple-element.209.refs_0_, bf16[7,7,16,512]{3,2,1,0:T(8,128)(2,1)S(1)} %get-tuple-element.212.refs_1_, bf16[32,208,512]{2,1,0:T(8,128)(2,1)S(1)} %inner_expand_grad.1.refs_2_), custom_call_target="tpu_custom_call", output_to_operand_aliasing={{}: (2, {})} | custom-call | flops 3699376128 | bytes 2129920 | tf_op jit(solution)/shard_map/inner_spatial_grad/pallas_call | solution.py:345
  393.2 7.4 %back_middle.1 = (bf16[7,7,16,512]{3,2,1,0:T(8,128)(2,1)S(1)}, bf16[7,7,16,2048]{3,2,1,0:T(8,128)(2,1)S(1)}, f32[16,2048]{1,0:T(8,128)S(1)}) custom-call(f32[7,7,16,512]{3,2,1,0:T(8,128)S(1)} %copy-done.37, bf16[7,7,16,512]{3,2,1,0:T(8,128)(2,1)S(1)} %copy-done.51, f32[8,512]{1,0:T(8,128)S(1)} %copy-done.72, f32[8,512]{1,0:T(8,128)S(1)} %add_add_fusion.12.refs_3_, ...), custom_call_target="tpu_custom_call" | custom-call | flops 1644167168 | bytes 25102336 | tf_op jit(solution)/shard_map/back_middle/pallas_call | solution.py:345
  423.9 7.3 %back_entry_expand.1 = (bf16[7,7,16,2048]{3,2,1,0:T(8,128)(2,1)S(1)}, bf16[7,7,16,2048]{3,2,1,0:T(8,128)(2,1)S(1)}, f32[7,7,16,512]{3,2,1,0:T(8,128)S(1)}, f32[8,512]{1,0:T(8,128)S(1)}) custom-call(bf16[7,7,16,2048]{3,2,1,0:T(8,128)(2,1)S(1)} %get-tuple-element.218.refs_0_, bf16[7,7,16,2048]{3,2,1,0:T(8,128)(2,1)S(1)} %copy-done.7, ...), custom_call_target="tpu_custom_call" | custom-call | flops 1644167168 | bytes 18569216 | tf_op jit(solution)/shard_map/back_entry_expand/pallas_call | solution.py:345
  449.4 6.4 project_grad.1
  478.2 9.4 %back_entry_spatial.1 = (bf16[7,7,16,512]{3,2,1,0:T(8,128)(2,1)S(1)}, bf16[7,2,7,2,16,512]{5,4,3,2,1,0:T(8,128)(2,1)S(1)}, f32[8,512]{1,0:T(8,128)S(1)}) custom-call(f32[7,7,16,512]{3,2,1,0:T(8,128)S(1)} %copy-done.39, bf16[7,7,16,512]{3,2,1,0:T(8,128)(2,1)S(1)} %get-tuple-element.179.refs_0_.refs_13_.refs_1_, ...), custom_call_target="tpu_custom_call" | custom-call | flops 3699376128 | bytes 15851520 | tf_op jit(solution)/shard_map/back_entry_spatial/pallas_call | solution.py:345
  487.6 7.1 %entry_spatial_grad.1 = bf16[32,144,512]{2,1,0:T(8,128)(2,1)S(1)} custom-call(bf16[2,2,8,8,16,512]{5,4,3,2,1,0:T(8,128)(2,1)S(1)} %copy-done.76, bf16[7,7,16,512]{3,2,1,0:T(8,128)(2,1)S(1)} %get-tuple-element.238.refs_1_), custom_call_target="tpu_custom_call" | custom-call | flops 3699376128 | bytes 4997120 | tf_op jit(solution)/shard_map/entry_spatial_grad/pallas_call | solution.py:345
  496.9 10.3 %collective-permute-done.100 = bf16[4,1,2,1,128,512]{5,4,3,2,1,0:T(8,128)(2,1)} collective-permute-done((bf16[4,1,2,1,128,512]{5,4,3,2,1,0:T(8,128)(2,1)S(1)}, bf16[4,1,2,1,128,512]{5,4,3,2,1,0:T(8,128)(2,1)}, u32[]{:S(2)}, u32[]{:S(2)}) %collective-permute-start.100) | collective-permute-done | bytes 1048608 | tf_op jit(solution)/shard_map/ppermute | solution.py:21
  507.2 13.3 %collective-permute-done.99 = bf16[4,2,1,1,128,512]{5,4,3,2,1,0:T(8,128)(2,1)} collective-permute-done((bf16[4,2,1,1,128,512]{5,4,3,2,1,0:T(8,128)(2,1)S(1)}, bf16[4,2,1,1,128,512]{5,4,3,2,1,0:T(8,128)(2,1)}, u32[]{:S(2)}, u32[]{:S(2)}) %collective-permute-start.99) | collective-permute-done | bytes 1048608 | tf_op jit(solution)/shard_map/ppermute | solution.py:21
  540.6 8.1 %back_first.1 = (bf16[14,14,16,512]{3,2,1,0:T(8,128)(2,1)S(1)}, bf16[32,32,512]{2,1,0:T(8,128)(2,1)S(1)}) custom-call(bf16[14,14,16,512]{3,2,1,0:T(8,128)(2,1)S(1)} %bitcast.245, bf16[14,14,16,512]{3,2,1,0:T(8,128)(2,1)S(1)} %copy-done.21, f32[8,512]{1,0:T(8,128)S(1)} %copy-done.62, f32[8,512]{1,0:T(8,128)S(1)} %add_add_fusion.8.refs_3_, ...), custom_call_target="tpu_custom_call" | custom-call | flops 3288334336 | bytes 13027328 | tf_op jit(solution)/shard_map/back_first/pallas_call | solution.py:345
  565.0 6.6 %back_strided.1.refs_2_ = f32[7,7,16,1024]{3,2,1,0:T(8,128)S(1)} custom-call(bf16[7,7,16,2048]{3,2,1,0:T(8,128)(2,1)S(1)} %copy-done.13, bf16[32,192,512]{2,1,0:T(8,128)(2,1)} %bitcast.259), custom_call_target="tpu_custom_call" | custom-call | flops 3288334336 | bytes 9502720 | tf_op jit(solution)/shard_map/back_strided/pallas_call | solution.py:345
  584.3 9.3 %input_grad.1 = f32[14,14,16,1024]{3,2,1,0:T(8,128)} custom-call(bf16[14,14,16,512]{3,2,1,0:T(8,128)(2,1)S(1)} %copy-done.29, bf16[32,35,512]{2,1,0:T(8,128)(2,1)} %bitcast.271, f32[7,7,16,1024]{3,2,1,0:T(8,128)S(1)} %back_strided.1.refs_2_), custom_call_target="tpu_custom_call" | custom-call | flops 3288334336 | bytes 7569408 | tf_op jit(solution)/shard_map/input_grad/pallas_call | solution.py:345
  (730 shorter events, 446.0 us)
Async XLA Ops:
  7.2 112.5 %all-gather.5.cloned.1.call-start = ((), (), s32[]{:S(2)}) async-start(), calls=%async_computation.2 | async-start | bytes 7028736 | tf_op jit(solution)/shard_map/all_gather | solution.py:974
  9.0 232.5 %all-gather.7.cloned.1.call-start = ((), (), s32[]{:S(2)}) async-start(), calls=%async_computation.3 | async-start | bytes 7028736 | tf_op jit(solution)/shard_map/all_gather | solution.py:974
  37.8 14.6 %collective-permute-start.3 = (bf16[2,2,2,1,1,35,512]{6,5,4,3,2,1,0:T(8,128)(2,1)S(1)}, bf16[2,2,2,1,1,35,512]{6,5,4,3,2,1,0:T(8,128)(2,1)}, u32[]{:S(2)}, u32[]{:S(2)}) collective-permute-start(bf16[2,2,2,1,1,35,512]{6,5,4,3,2,1,0:T(8,128)(2,1)S(1)} %pad_maximum_fusion.14), channel_id=1, source_target_pairs={{0,2},{1,3},{2,0},{3,1},{4,6},{5,7},{6,4},{7,5},{8,10},{9,11},{10,... | collective-permute-start | bytes 860168 | tf_op jit(solution)/shard_map/ppermute | solution.py:21
  40.6 513.5 %reduce-scatter.2.cloned.1.call-start = ((), (), s32[]{:S(2)}) async-start(), calls=%async_computation.1 | async-start | bytes 7028736 | tf_op jit(solution)/shard_map/reduce_scatter | solution.py:1210
  119.7 20.2 %collective-permute-start.21 = (bf16[4,1,2,1,96,512]{5,4,3,2,1,0:T(8,128)(2,1)S(1)}, bf16[4,1,2,1,96,512]{5,4,3,2,1,0:T(8,128)(2,1)}, u32[]{:S(2)}, u32[]{:S(2)}) collective-permute-start(bf16[4,1,2,1,96,512]{5,4,3,2,1,0:T(8,128)(2,1)S(1)} %pad_maximum_fusion.6), channel_id=1, source_target_pairs={{0,4},{1,5},{2,6},{3,7},{4,0},{5,1},{6,2},{7,3},{8,12},{9,13},{10,... | collective-permute-start | bytes 2359304 | tf_op jit(solution)/shard_map/ppermute | solution.py:21
  122.0 19.7 %collective-permute-start.20 = (bf16[4,2,1,1,96,512]{5,4,3,2,1,0:T(8,128)(2,1)S(1)}, bf16[4,2,1,1,96,512]{5,4,3,2,1,0:T(8,128)(2,1)S(1)}, u32[]{:S(2)}, u32[]{:S(2)}) collective-permute-start(bf16[4,2,1,1,96,512]{5,4,3,2,1,0:T(8,128)(2,1)S(1)} %pad_maximum_fusion.5), channel_id=1, source_target_pairs={{0,2},{1,3},{2,0},{3,1},{4,6},{5,7},{6,4},{7,5},{8,10},{9,11},{10,... | collective-permute-start | bytes 2359304 | tf_op jit(solution)/shard_map/ppermute | solution.py:21
  143.9 28.0 %collective-permute-start.29 = (bf16[4,2,2,1,96,512]{5,4,3,2,1,0:T(8,128)(2,1)}, bf16[4,2,2,1,96,512]{5,4,3,2,1,0:T(8,128)(2,1)}, u32[]{:S(2)}, u32[]{:S(2)}) collective-permute-start(bf16[4,2,2,1,96,512]{5,4,3,2,1,0:T(8,128)(2,1)} %get-tuple-element.185), channel_id=1, source_target_pairs={{0,1},{1,0},{2,3},{3,2},{4,5},{5,4},{6,7},{7,6},{8,9},{9,8},{10,11... | collective-permute-start | bytes 4718600 | tf_op jit(solution)/shard_map/ppermute | solution.py:21
  143.9 30.7 %collective-permute-start.30 = (bf16[4,2,2,1,96,512]{5,4,3,2,1,0:T(8,128)(2,1)}, bf16[4,2,2,1,96,512]{5,4,3,2,1,0:T(8,128)(2,1)S(1)}, u32[]{:S(2)}, u32[]{:S(2)}) collective-permute-start(bf16[4,2,2,1,96,512]{5,4,3,2,1,0:T(8,128)(2,1)} %get-tuple-element.186), channel_id=1, source_target_pairs={{0,1},{1,0},{2,3},{3,2},{4,5},{5,4},{6,7},{7,6},{8,9},{9,8},{10,11... | collective-permute-start | bytes 4718600 | tf_op jit(solution)/shard_map/ppermute | solution.py:21
  365.8 14.2 %collective-permute-start.80 = (f32[8,512]{1,0:T(8,128)S(1)}, f32[8,512]{1,0:T(8,128)S(1)}, u32[]{:S(2)}, u32[]{:S(2)}) collective-permute-start(f32[8,512]{1,0:T(8,128)S(1)} %add_add_fusion.13), channel_id=1, source_target_pairs={{0,8},{1,9},{2,10},{3,11},{4,12},{5,13},{6,14},{7,15},{8,0},{9,1},... | collective-permute-start | bytes 49160 | tf_op jit(solution)/shard_map/ppermute | solution.py:21
  365.9 14.2 %collective-permute-start.81 = (f32[8,512]{1,0:T(8,128)S(1)}, f32[8,512]{1,0:T(8,128)S(1)}, u32[]{:S(2)}, u32[]{:S(2)}) collective-permute-start(f32[8,512]{1,0:T(8,128)S(1)} %add_add_fusion.13), channel_id=1, source_target_pairs={{0,16},{1,17},{2,18},{3,19},{4,20},{5,21},{6,22},{7,23},{8,24},{9,... | collective-permute-start | bytes 49160 | tf_op jit(solution)/shard_map/ppermute | solution.py:21
  474.5 32.8 %collective-permute-start.100 = (bf16[4,1,2,1,128,512]{5,4,3,2,1,0:T(8,128)(2,1)S(1)}, bf16[4,1,2,1,128,512]{5,4,3,2,1,0:T(8,128)(2,1)}, u32[]{:S(2)}, u32[]{:S(2)}) collective-permute-start(bf16[4,1,2,1,128,512]{5,4,3,2,1,0:T(8,128)(2,1)S(1)} %add_convert_fusion), channel_id=1, source_target_pairs={{0,4},{1,5},{2,6},{3,7},{4,0},{5,1},{6,2},{7,3},{8,12},{9,13},{10,... | collective-permute-start | bytes 3145736 | tf_op jit(solution)/shard_map/ppermute | solution.py:21
  474.5 46.0 %collective-permute-start.99 = (bf16[4,2,1,1,128,512]{5,4,3,2,1,0:T(8,128)(2,1)S(1)}, bf16[4,2,1,1,128,512]{5,4,3,2,1,0:T(8,128)(2,1)}, u32[]{:S(2)}, u32[]{:S(2)}) collective-permute-start(bf16[4,2,1,1,128,512]{5,4,3,2,1,0:T(8,128)(2,1)S(1)} %add_convert_fusion.1), channel_id=1, source_target_pairs={{0,2},{1,3},{2,0},{3,1},{4,6},{5,7},{6,4},{7,5},{8,10},{9,11},{10,... | collective-permute-start | bytes 3145736 | tf_op jit(solution)/shard_map/ppermute | solution.py:21
  522.2 30.3 %collective-permute-start.110 = (bf16[4,2,2,1,144,512]{5,4,3,2,1,0:T(8,128)(2,1)S(1)}, bf16[4,2,2,1,144,512]{5,4,3,2,1,0:T(8,128)(2,1)S(1)}, u32[]{:S(2)}, u32[]{:S(2)}) collective-permute-start(bf16[4,2,2,1,144,512]{5,4,3,2,1,0:T(8,128)(2,1)S(1)} %constant_dynamic-slice_fusion.3), channel_id=1, source_target_pairs={{0,1},{1,0},{2,3},{3,2},{4,5},{5,4},{6,7},{7,6},{8,9},{9,8},{10,11... | collective-permute-start | bytes 7077896 | tf_op jit(solution)/shard_map/ppermute | solution.py:21
  560.5 18.4 %collective-permute-start.115 = (bf16[4,1,2,1,96,512]{5,4,3,2,1,0:T(8,128)(2,1)S(1)}, bf16[4,1,2,1,96,512]{5,4,3,2,1,0:T(8,128)(2,1)S(1)}, u32[]{:S(2)}, u32[]{:S(2)}) collective-permute-start(bf16[4,1,2,1,96,512]{5,4,3,2,1,0:T(8,128)(2,1)S(1)} %pad_maximum_fusion.7), channel_id=1, source_target_pairs={{0,4},{1,5},{2,6},{3,7},{4,0},{5,1},{6,2},{7,3},{8,12},{9,13},{10,... | collective-permute-start | bytes 2359304 | tf_op jit(solution)/shard_map/ppermute | solution.py:21
  561.2 15.0 %collective-permute-start.114 = (bf16[4,2,1,1,80,512]{5,4,3,2,1,0:T(8,128)(2,1)S(1)}, bf16[4,2,1,1,80,512]{5,4,3,2,1,0:T(8,128)(2,1)S(1)}, u32[]{:S(2)}, u32[]{:S(2)}) collective-permute-start(bf16[4,2,1,1,80,512]{5,4,3,2,1,0:T(8,128)(2,1)S(1)} %add_convert_fusion.2), channel_id=1, source_target_pairs={{0,2},{1,3},{2,0},{3,1},{4,6},{5,7},{6,4},{7,5},{8,10},{9,11},{10,... | collective-permute-start | bytes 1966088 | tf_op jit(solution)/shard_map/ppermute | solution.py:21
  562.6 17.7 %collective-permute-start.113 = (bf16[1,1,1,256,512]{4,3,2,1,0:T(8,128)(2,1)S(1)}, bf16[1,1,1,256,512]{4,3,2,1,0:T(8,128)(2,1)S(1)}, u32[]{:S(2)}, u32[]{:S(2)}) collective-permute-start(bf16[1,1,1,256,512]{4,3,2,1,0:T(8,128)(2,1)S(1)} %pad_maximum_fusion.16), channel_id=1, source_target_pairs={{24,16},{25,17},{26,18},{27,19},{28,20},{29,21},{30,22},{31,23}} | collective-permute-start | bytes 786440 | tf_op jit(solution)/shard_map/ppermute | solution.py:108
  563.4 17.0 %collective-permute-start.112 = (bf16[1,1,1,256,512]{4,3,2,1,0:T(8,128)(2,1)S(1)}, bf16[1,1,1,256,512]{4,3,2,1,0:T(8,128)(2,1)S(1)}, u32[]{:S(2)}, u32[]{:S(2)}) collective-permute-start(bf16[1,1,1,256,512]{4,3,2,1,0:T(8,128)(2,1)S(1)} %pad_maximum_fusion.15), channel_id=1, source_target_pairs={{0,8},{1,9},{2,10},{3,11},{4,12},{5,13},{6,14},{7,15}} | collective-permute-start | bytes 786440 | tf_op jit(solution)/shard_map/ppermute | solution.py:108
  580.3 15.7 %collective-permute-start.121 = (bf16[2,1,208,512]{3,2,1,0:T(8,128)(2,1)S(1)}, bf16[2,1,208,512]{3,2,1,0:T(8,128)(2,1)S(1)}, u32[]{:S(2)}, u32[]{:S(2)}) collective-permute-start(bf16[2,1,208,512]{3,2,1,0:T(8,128)(2,1)S(1)} %pad_maximum_fusion.11), channel_id=1, source_target_pairs={{0,1},{1,0},{2,3},{3,2},{4,5},{5,4},{6,7},{7,6},{8,9},{9,8},{10,11... | collective-permute-start | bytes 1277960 | tf_op jit(solution)/shard_map/ppermute | solution.py:21
  580.4 14.4 %collective-permute-start.120 = (bf16[4,1,1,1,96,512]{5,4,3,2,1,0:T(8,128)(2,1)S(1)}, bf16[4,1,1,1,96,512]{5,4,3,2,1,0:T(8,128)(2,1)S(1)}, u32[]{:S(2)}, u32[]{:S(2)}) collective-permute-start(bf16[4,1,1,1,96,512]{5,4,3,2,1,0:T(8,128)(2,1)S(1)} %pad_maximum_fusion.12), channel_id=1, source_target_pairs={{0,2},{1,3},{2,0},{3,1},{4,6},{5,7},{6,4},{7,5},{8,10},{9,11},{10,... | collective-permute-start | bytes 1179656 | tf_op jit(solution)/shard_map/ppermute | solution.py:21
  580.8 12.9 %collective-permute-start.119 = (bf16[4,1,1,1,80,512]{5,4,3,2,1,0:T(8,128)(2,1)S(1)}, bf16[4,1,1,1,80,512]{5,4,3,2,1,0:T(8,128)(2,1)S(1)}, u32[]{:S(2)}, u32[]{:S(2)}) collective-permute-start(bf16[4,1,1,1,80,512]{5,4,3,2,1,0:T(8,128)(2,1)S(1)} %add_convert_fusion.9), channel_id=1, source_target_pairs={{0,4},{1,5},{2,6},{3,7},{4,0},{5,1},{6,2},{7,3},{8,12},{9,13},{10,... | collective-permute-start | bytes 983048 | tf_op jit(solution)/shard_map/ppermute | solution.py:21
  581.6 14.6 %collective-permute-start.118 = (bf16[1,1,1,256,512]{4,3,2,1,0:T(8,128)(2,1)S(1)}, bf16[1,1,1,256,512]{4,3,2,1,0:T(8,128)(2,1)S(1)}, u32[]{:S(2)}, u32[]{:S(2)}) collective-permute-start(bf16[1,1,1,256,512]{4,3,2,1,0:T(8,128)(2,1)S(1)} %add_convert_fusion.14), channel_id=1, source_target_pairs={{16,8},{17,9},{18,10},{19,11},{20,12},{21,13},{22,14},{23,15},{24,... | collective-permute-start | bytes 786440 | tf_op jit(solution)/shard_map/ppermute | solution.py:108
  582.3 13.9 %collective-permute-start.117 = (bf16[1,1,1,256,512]{4,3,2,1,0:T(8,128)(2,1)S(1)}, bf16[1,1,1,256,512]{4,3,2,1,0:T(8,128)(2,1)S(1)}, u32[]{:S(2)}, u32[]{:S(2)}) collective-permute-start(bf16[1,1,1,256,512]{4,3,2,1,0:T(8,128)(2,1)S(1)} %add_convert_fusion.15), channel_id=1, source_target_pairs={{0,8},{1,9},{2,10},{3,11},{4,12},{5,13},{6,14},{7,15},{8,16},{9,17... | collective-permute-start | bytes 786440 | tf_op jit(solution)/shard_map/ppermute | solution.py:108
  598.5 15.4 %collective-permute-start.123 = (bf16[1,1,1,256,512]{4,3,2,1,0:T(8,128)(2,1)S(1)}, bf16[1,1,1,256,512]{4,3,2,1,0:T(8,128)(2,1)S(1)}, u32[]{:S(2)}, u32[]{:S(2)}) collective-permute-start(bf16[1,1,1,256,512]{4,3,2,1,0:T(8,128)(2,1)S(1)} %add_convert_fusion.11), channel_id=1, source_target_pairs={{8,0},{9,1},{10,2},{11,3},{12,4},{13,5},{14,6},{15,7},{16,8},{17,9... | collective-permute-start | bytes 786440 | tf_op jit(solution)/shard_map/ppermute | solution.py:108
  599.9 14.1 %collective-permute-start.122 = (bf16[1,1,1,256,512]{4,3,2,1,0:T(8,128)(2,1)S(1)}, bf16[1,1,1,256,512]{4,3,2,1,0:T(8,128)(2,1)S(1)}, u32[]{:S(2)}, u32[]{:S(2)}) collective-permute-start(bf16[1,1,1,256,512]{4,3,2,1,0:T(8,128)(2,1)S(1)} %add_convert_fusion.12), channel_id=1, source_target_pairs={{0,8},{1,9},{2,10},{3,11},{4,12},{5,13},{6,14},{7,15},{8,16},{9,17... | collective-permute-start | bytes 786440 | tf_op jit(solution)/shard_map/ppermute | solution.py:108
  (208 other events, 1683.6 us)
Sparse Core Ops, SparseCore 0:
  11.5 81.2 all-gather.4
  96.2 75.6 all-gather.6
  380.2 144.9 reduce-scatter.1

commit v3 on v2

--- a/solution.py
+++ b/solution.py
@@ -13,7 +13,9 @@
 F32 = jnp.float32
 GROUPS = 3
 LANES = 512
-VMEM = 22 * 1024 * 1024
+VMEM = 24 * 1024 * 1024
+LARGE = 1700 * 1000
+NEAR = ("first",)
 
 
 def xor_swap(value, distance):
@@ -186,46 +188,27 @@
     return value.reshape((-1, 2, 2, 2) + value.shape[1:])
 
 
-class LineScatter:
-    def __init__(self, segments):
-        self.segments = segments
-        self.right = self.left = None
-
-    def block(self, index):
-        index = jnp.clip(index, 0, 3)
+def far_scatter(segments):
+    if not is_line():
+        count = index_bits() - 3
+        values = [[p.reshape((2,) * count + p.shape[-2:]) for p in s] for s in segments]
+        for step in range(count):
+            values = halve_bit(values, step + 3, count - 1 - step)
+        values = [added(s).reshape((-1, LANES)).astype(BF) for s in values]
+        return jnp.concatenate(values, axis=0)
+
+    def block(index):
         parts = [
             added([lax.dynamic_index_in_dim(p, index, 0, keepdims=False) for p in s])
-            for s in self.segments
+            for s in segments
         ]
         return jnp.concatenate(parts, axis=-2) if len(parts) > 1 else parts[0]
 
-    def step(self, number):
-        if not is_line():
-            return
-        place = line_place()
-        to_right, to_left = self.block(4 - number + place), self.block(number - 4 + place)
-        if self.right is not None:
-            to_right, to_left = added([to_right, self.right]), added([to_left, self.left])
-        self.right = line_shift(to_right.astype(BF), 1, range(number))
-        self.left = line_shift(to_left.astype(BF), -1, range(4 - number, 4))
-
-    def end(self):
-        shape = self.segments[0][0].shape
-        if is_line():
-            result = added([self.block(line_place()), self.right, self.left])
-            return result.reshape((-1, shape[-1])).astype(BF)
-        count = index_bits() - 3
-        values = [[p.reshape((2,) * count + p.shape[-2:]) for p in s] for s in self.segments]
-        for step in range(count):
-            values = halve_bit(values, step + 3, count - 1 - step)
-        values = [added(s).reshape((-1, shape[-1])).astype(BF) for s in values]
-        return jnp.concatenate(values, axis=0)
-
-    def state(self):
-        return [self.segments, self.right, self.left]
-
-    def put(self, state):
-        self.segments, self.right, self.left = state
+    place = line_place()
+    parts = [block(place)]
+    for k in (1, 2, 3):
+        parts.append(xor_swap(block(place ^ k).astype(BF), k << 3))
+    return added(parts).reshape((-1, LANES)).astype(BF)
 
 
 def gather_copy(value, bit):
@@ -341,6 +324,17 @@
         kernel(*params, *refs[at + (into is not None) :])
 
     given = [] if into is None else [into]
+    arrays = [
+        pltpu.with_memory_space_constraint(a, pltpu.HBM) if a.nbytes > LARGE and name not in NEAR else a
+        for a in arrays
+    ]
+
+    def result(shape, dtype):
+        size = dtype.dtype.itemsize
+        for extent in shape:
+            size *= extent
+        return (pltpu.HBM if size > LARGE else jax.ShapeDtypeStruct)(shape, dtype)
+
 
     return pl.pallas_call(
         body,
@@ -349,7 +343,7 @@
         in_specs=[s for g in groups for _, s in g] + [pl.BlockSpec(memory_space=pl.ANY)] * len(given),
         input_output_aliases={len(arrays): 0} if given else {},
         out_specs=[s for _, _, s in outs],
-        out_shape=[jax.ShapeDtypeStruct(shape, dtype) for shape, dtype, _ in outs],
+        out_shape=[result(shape, dtype) for shape, dtype, _ in outs],
         scratch_shapes=list(scratch),
         compiler_params=pltpu.CompilerParams(
             vmem_limit_bytes=VMEM, dimension_semantics=("arbitrary",)
@@ -1041,7 +1035,6 @@
         inner_norm_spatial,
         inner_norm_expand,
     )
-    w_spatial, w_expand = everywhere([entry_spatial, entry_expand])
     table_cells = jnp.concatenate([t.reshape(2 * GROUPS, -1) for t in tables_all], axis=1)
     table_rows = -(-table_cells.size // (copies * LANES))
     table_part = jnp.pad(
@@ -1050,14 +1043,61 @@
     table_part = lax.dynamic_index_in_dim(table_part, copy, 0, keepdims=False)
     middle_weights = [entry_project, inner_reduce]
     last_weights = [inner_spatial, inner_expand]
-    first_array, others = gather_rows(
-        jnp.concatenate([quarter(entry_reduce), table_part], axis=0), middle_weights + last_weights
-    )
+    first_weights = [entry_spatial, entry_expand]
+    early_array = lax.all_gather(
+        jnp.concatenate([joined(first_weights), table_part], axis=0), AXES, axis=0, tiled=False
+    )
+    w_spatial, w_expand = views(early_array, first_weights)
+    first_array, others = gather_rows(quarter(entry_reduce), middle_weights + last_weights)
     w_ispatial, w_iexpand = everywhere(others[2:])
     first_array, part = after(first_array, joined(others[:2]))
     (w_reduce,) = views(first_array, [entry_reduce])
     line = line_gather_start(part)
-    tables_flat = first_array[:, -table_rows:].reshape(shards, -1)[:, : table_cells.size]
+    x = inputs.transpose(1, 2, 0, 3)
+    x_split = x.reshape(half, 2, half, 2, images, wide)
+    cot = cotangent.transpose(1, 2, 0, 3)
+
+    small = (half, half, images, LANES)
+    large = (half, half, images, out)
+    split = (half, 2, half, 2, images, LANES)
+    rows_out, rows_in = half * half * images, full * full * images
+    six = (2 * GROUPS, LANES)
+    sums_block = (8, LANES)
+
+    def fixed(array):
+        return (array, whole(array.shape))
+
+    def column(array):
+        return (array, along(array.shape[:-1] + (LANES,), array.ndim - 1))
+
+    small_out = (small, BF, whole(small))
+    large_out = (large, BF, along(small, 3))
+    sums_out = ((8, LANES), F32, whole((8, LANES)))
+    sums_wide = ((8, out), F32, along((8, LANES), 1))
+    acc = pltpu.VMEM(small, F32)
+
+    count_row = jnp.concatenate(
+        [
+            jnp.broadcast_to(jnp.sum(onehot_int[g]).astype(F32), (1, 128))
+            for g in range(GROUPS)
+        ]
+        + [jnp.zeros((1, LANES - 128 * GROUPS), F32)],
+        axis=1,
+    )
+    z1, sums1 = call(
+        k_first, "first", half,
+        [(x, along((2, full, images, wide), 0)), w_reduce.moving_all(), fixed(limits_in), fixed(onehot),
+         fixed(count_row)],
+        [((full, full, images, mid), BF, along((2, full, images, mid), 0)), sums_out],
+        [pltpu.VMEM((2, images, mid), F32)], flops=2 * rows_in * wide * mid,
+    )
+    sums1, z1, *line = after(sums1, z1, *line)
+    sums1, *line = after(sum_everywhere(sums1), *line)
+    low, high = split_rows(line_gather_end(line))
+    low, high, early_array, z1 = after(low, high, early_array, z1)
+    w_spatial, w_expand = views(early_array, first_weights)
+    low, high = gather_bit(low, 2, 1), gather_bit(high, 1, 2)
+    tables_flat = early_array[:, -table_rows:].reshape(shards, -1)[:, : table_cells.size]
     tables_flat = tables_flat.reshape((shards,) + table_cells.shape)
     tables, at = [], 0
     for t in tables_all:
@@ -1065,52 +1105,6 @@
         field = tables_flat[:, :, at : at + width].transpose(1, 0, 2)
         tables.append(field.reshape(2 * GROUPS, shards * width).astype(F32))
         at += width
-
-    x = inputs.transpose(1, 2, 0, 3)
-    x_split = x.reshape(half, 2, half, 2, images, wide)
-    cot = cotangent.transpose(1, 2, 0, 3)
-
-    small = (half, half, images, LANES)
-    large = (half, half, images, out)
-    split = (half, 2, half, 2, images, LANES)
-    rows_out, rows_in = half * half * images, full * full * images
-    six = (2 * GROUPS, LANES)
-    sums_block = (8, LANES)
-
-    def fixed(array):
-        return (array, whole(array.shape))
-
-    def column(array):
-        return (array, along(array.shape[:-1] + (LANES,), array.ndim - 1))
-
-    small_out = (small, BF, whole(small))
-    large_out = (large, BF, along(small, 3))
-    sums_out = ((8, LANES), F32, whole((8, LANES)))
-    sums_wide = ((8, out), F32, along((8, LANES), 1))
-    acc = pltpu.VMEM(small, F32)
-
-    count_row = jnp.concatenate(
-        [
-            jnp.broadcast_to(jnp.sum(onehot_int[g]).astype(F32), (1, 128))
-            for g in range(GROUPS)
-        ]
-        + [jnp.zeros((1, LANES - 128 * GROUPS), F32)],
-        axis=1,
-    )
-    z1, sums1 = call(
-        k_first, "first", half,
-        [(x, along((2, full, images, wide), 0)), w_reduce.moving_all(), fixed(limits_in), fixed(onehot),
-         fixed(count_row)],
-        [((full, full, images, mid), BF, along((2, full, images, mid), 0)), sums_out],
-        [pltpu.VMEM((2, images, mid), F32)], flops=2 * rows_in * wide * mid,
-    )
-    sums1, z1, *line = after(sums1, z1, *line)
-    sums1, *line = after(sum_everywhere(sums1), *line)
-    low, high = split_rows(line_gather_end(line))
-    low, high = gather_bit(low, 2, 1), gather_bit(high, 1, 2)
-    low, high, w_spatial.array, z1 = after(low, high, w_spatial.array, z1)
-    w_expand.array = w_spatial.array if w_expand.at else w_expand.array
-    low, high = gather_bit(low, 1, 2), gather_bit(high, 2, 1)
     totals = sums1[2 * GROUPS, 0 : 128 * GROUPS : 128]
     side_real = group_side.astype(F32)
     half_real = (group_side // 2).astype(F32)
@@ -1133,20 +1127,24 @@
         [acc], flops=18 * rows_out * mid * mid,
     )
     sums2, low, high = after(sums2, low, high)
-    values = [gather_bit(v, 0, 3) for v in (low, high)]
-    gathered = jnp.concatenate(values, axis=4).reshape(devices, -1, LANES)
-    w_project, w_ireduce = views(gathered, middle_weights)
-    sums2 = sum_everywhere(sums2)
-    zs, sums_s = call(
-        k_strided, "strided", blocks,
-        [(x_split, whole((half, 1, half, 1, images, wide))), w_project.moving(), limits_out, onehot],
-        [large_out, sums_wide], [acc], flops=2 * rows_out * wide * out,
-    )
+    near, low, high = after(sum_near(sums2), low, high)
+    low_other, high_other = xor_swap(low, 1 << 1), xor_swap(high, 1 << 2)
+    sums2 = sum_far(near, LANES)
     a2, slope2, z3, sums3 = call(
         k_expand, "expand", blocks,
         [fixed(z2), fixed(sums2), fixed(tables[1]), counts, keeps_out, onehot,
          w_expand.moving()],
         [small_out, small_out, large_out, sums_wide], [acc], flops=2 * rows_out * mid * out,
+    )
+    z3, sums3, low_other, high_other = after(z3, sums3, low_other, high_other)
+    low, high = pair(low, low_other, 1, 2), pair(high, high_other, 2, 1)
+    values = [gather_bit(v, 0, 3) for v in (low, high)]
+    gathered = jnp.concatenate(values, axis=4).reshape(devices, -1, LANES)
+    w_project, w_ireduce = views(gathered, middle_weights)
+    zs, sums_s = call(
+        k_strided, "strided", blocks,
+        [(x_split, whole((half, 1, half, 1, images, wide))), w_project.moving(), limits_out, onehot],
+        [large_out, sums_wide], [acc], flops=2 * rows_out * wide * out,
     )
     joined = sum_everywhere(jnp.concatenate([sums3, sums_s], axis=1))
     sums3, sums_s = joined[:, :out], joined[:, out:]
@@ -1247,6 +1245,10 @@
     low_sent, high_sent, back2 = after(halve_sent(low, 1, 2), halve_sent(high, 2, 1), back2)
     low, high = halve_end(low, low_sent, 1, 2), halve_end(high, high_sent, 2, 1)
     strided_shape = (half, half, images, wide)
+    (d_strided,) = call(
+        k_back_strided, "back_strided", blocks, [column(dzs), w_project.moving()],
+        [(strided_shape, F32, whole(strided_shape))], flops=2 * rows_out * wide * out,
+    )
     plane = (half, 1, half, 1, images, LANES)
 
     def parity(array):
@@ -1267,8 +1269,8 @@
     )
     spatial_rows = [[near_shape(grad_rows(g_spatial, entry_spatial))]]
     spatial_sent = halve_sent(spatial_rows, 0, 3)
-    back1, low_sent, high_sent, spatial_sent = after(
-        back1, halve_sent(low, 2, 1), halve_sent(high, 1, 2), spatial_sent
+    back1, low_sent, high_sent, spatial_sent, d_strided = after(
+        back1, halve_sent(low, 2, 1), halve_sent(high, 1, 2), spatial_sent, d_strided
     )
     near, low_sent, high_sent = after(sum_near(back1), low_sent, high_sent)
     low, high = halve_end(low, low_sent, 2, 1), halve_end(high, high_sent, 1, 2)
@@ -1285,29 +1287,14 @@
         [pltpu.VMEM((wide, mid), F32)], flops=2 * rows_in * wide * mid,
     )
     first_rows = [[added(v).astype(BF)] for v in low + high]
-    first_rows, g_reduce, dz1, dzs, inner_own = flat_after(
-        first_rows, g_reduce, dz1, dzs, inner_own
-    )
+    first_rows, g_reduce, dz1, inner_own = flat_after(first_rows, g_reduce, dz1, inner_own)
     reduce_rows = halve_bit([[near_shape(grad_rows(g_reduce, entry_reduce))]], 0, 3)
     low, high = cut_rows(spatial_rows + reduce_rows)
-    first_rows, low_sent, high_sent, dz1, dzs = flat_after(
-        first_rows, halve_sent(low, 1, 2), halve_sent(high, 2, 1), dz1, dzs
-    )
-    first_line = LineScatter(first_rows)
-    first_line.step(1)
+    first_rows, low_sent, high_sent, dz1 = flat_after(
+        first_rows, halve_sent(low, 1, 2), halve_sent(high, 2, 1), dz1
+    )
     low, high = halve_end(low, low_sent, 1, 2), halve_end(high, high_sent, 2, 1)
-    inner_own = gather_copy(inner_own.reshape(1, 1, -1, LANES), 1)
-    (d_strided,) = call(
-        k_back_strided, "back_strided", blocks, [column(dzs), w_project.moving()],
-        [(strided_shape, F32, whole(strided_shape))], flops=2 * rows_out * wide * out,
-    )
-    first_state, low_sent, high_sent, d_strided, inner_own = flat_after(
-        first_line.state(), halve_sent(low, 2, 1), halve_sent(high, 1, 2), d_strided, inner_own
-    )
-    first_line.put(first_state)
-    first_line.step(2)
-    low, high = halve_end(low, low_sent, 2, 1), halve_end(high, high_sent, 1, 2)
-    inner_own = gather_copy(inner_own, 0)
+    entry_own = far_scatter(first_rows)
     (d_inputs,) = call(
         k_input_grad, "input_grad", half,
         [(dz1, along(two, 0)), w_reduce.moving_all(),
@@ -1315,31 +1302,20 @@
         [((full, full, images, wide), F32, along((2, full, images, wide), 0))],
         flops=2 * rows_in * wide * mid,
     )
+    entry_own, low_sent, high_sent, d_inputs, inner_own = after(
+        entry_own, halve_sent(low, 2, 1), halve_sent(high, 1, 2), d_inputs, inner_own
+    )
+    low, high = halve_end(low, low_sent, 2, 1), halve_end(high, high_sent, 1, 2)
+    early_own = jnp.concatenate([entry_own, inner_own], axis=0).reshape(1, 1, -1, LANES)
+    early_own = gather_copy(early_own, 1)
     last_rows = [[added(v).astype(BF)] for v in low + high]
-    first_state, last_rows, d_inputs, inner_own = flat_after(
-        first_line.state(), last_rows, d_inputs, inner_own
-    )
-    first_line.put(first_state)
-    first_line.step(3)
-    last_line = LineScatter(last_rows)
-    last_line.step(1)
-    g_ispatial, g_iexpand = shares(inner_own, [inner_spatial, inner_expand])
-    first_state, last_state, g_ispatial, g_iexpand = flat_after(
-        first_line.state(), last_line.state(), g_ispatial, g_iexpand
-    )
-    first_line.put(first_state)
-    last_line.put(last_state)
-    last_line.step(2)
-    entry_own = gather_copy(first_line.end().reshape(1, 1, -1, LANES), 1)
-    entry_own, last_state = flat_after(entry_own, last_line.state())
-    last_line.put(last_state)
-    last_line.step(3)
-    entry_own = gather_copy(entry_own, 0)
-    entry_own, last_state = flat_after(entry_own, last_line.state())
-    last_line.put(last_state)
-    last_own = gather_copy(last_line.end().reshape(1, 1, -1, LANES), 1)
-    g_project, g_ireduce, g_expand = shares(entry_own, middle_grads)
-    last_own, g_project, g_ireduce, g_expand = after(last_own, g_project, g_ireduce, g_expand)
+    early_own, last_rows = flat_after(early_own, last_rows)
+    last_own = far_scatter(last_rows)
+    g_project, g_ireduce, g_expand, g_ispatial, g_iexpand = shares(
+        gather_copy(early_own, 0), middle_grads + [inner_spatial, inner_expand]
+    )
+    last_own, g_project, g_ispatial = after(last_own, g_project, g_ispatial)
+    last_own = gather_copy(last_own.reshape(1, 1, -1, LANES), 1)
     g_spatial, g_reduce = shares(gather_copy(last_own, 0), [entry_spatial, entry_reduce])
 
     def own_share(back, gain_at=0):

time: 664 us -> 645 us (0.971)
  Pallas kernels: 154 us -> 195 us
  local copies, waits for them, and re-layouts: 94.8 us -> 53.9 us
  starting transfers between devices: 168 us -> 152 us
    unnamed x214 -> x154, local copies, waits for them, and re-layouts: 76.1 us -> 25.5 us
    pallas_call x22, Pallas kernels: 154 us -> 195 us  [call(): pl.pallas_call(body, name=name, grid=(steps,), in_specs=[s for g in group...]
    ppermute x18 -> x6, starting transfers between devices: 40.7 us -> 16.7 us  [line_shift(): return lax.ppermute(value, AXES, pairs)]
    ppermute x116 -> x120, starting transfers between devices: 127 us -> 136 us  [xor_swap(): return lax.ppermute(value, AXES, [(d, d ^ distance) for d in range(count)])]
    ppermute x18 -> x6, waiting for transfers between devices: 23 us -> 17.2 us  [line_shift(): return lax.ppermute(value, AXES, pairs)]
    ppermute x116 -> x120, waiting for transfers between devices: 160 us -> 163 us  [xor_swap(): return lax.ppermute(value, AXES, [(d, d ^ distance) for d in range(count)])]
  transfers between devices with their start and end apart: 137 -> 129, of which waited for: 88 -> 85; matrix products, arithmetic and copies ran while one was open for 9% -> 10% of each run, Pallas kernels for 18% -> 24%
where the time goes in v3:
time: 645 us; the launch traced here: 636 us
  Pallas kernels  195 us (30%)
  waiting for transfers between devices  181 us (28%)
  starting transfers between devices  152 us (24%)
  local copies, waits for them, and re-layouts  53.9 us (8%)
  other arithmetic  37.2 us (6%)
  between operations  17.7 us (3%)
    pallas_call x22, Pallas kernels, call(): pl.pallas_call(body, name=name, grid=(steps,), in_specs=[s for g in group...  195 us
    ppermute x120, waiting for transfers between devices, xor_swap(): return lax.ppermute(value, AXES, [(d, d ^ distance) for d in range(count)])  163 us
    ppermute x120, starting transfers between devices, xor_swap(): return lax.ppermute(value, AXES, [(d, d ^ distance) for d in range(count)])  136 us
    unnamed x154, local copies, waits for them, and re-layouts  25.5 us
    ppermute x6, waiting for transfers between devices, line_shift(): return lax.ppermute(value, AXES, pairs)  17.2 us
    ppermute x6, starting transfers between devices, line_shift(): return lax.ppermute(value, AXES, pairs)  16.7 us
  transfers between devices with their start and end apart: 129, of which 85 were waited for; matrix products, arithmetic and copies ran while one was open for 10% of the time, Pallas kernels for 24%

profile of v3, /device:TPU:0, one launch (start us, length us, event | category | flops | bytes accessed | tf_op | source)
XLA Modules:
  0.0 636.3 jit_solution(14850890196406649447)
XLA Ops:
  49.1 7.3 %first.1 = (bf16[14,14,16,512]{3,2,1,0:T(8,128)(2,1)}, f32[8,512]{1,0:T(8,128)S(1)}) custom-call(bf16[14,14,16,1024]{3,2,1,0:T(8,128)(2,1)S(1)} %bitcast.195, bf16[32,32,512]{2,1,0:T(8,128)(2,1)} %bitcast.235, s32[16,512]{1,0:T(8,128)S(1)} %broadcast_in_dim.24.refs_2_.refs_6_, ...), custom_call_target="tpu_custom_call" | custom-call | flops 3288334336 | bytes 7604224 | tf_op jit(solution)/shard_map/first/pallas_call | solution.py:339
  87.4 7.2 %collective-permute-start.15 = (bf16[192,512]{1,0:T(8,128)(2,1)S(1)}, bf16[192,512]{1,0:T(8,128)(2,1)S(1)}, u32[]{:S(2)}, u32[]{:S(2)}) collective-permute-start(bf16[192,512]{1,0:T(8,128)(2,1)S(1)} %collective-permute-done.14), channel_id=1, source_target_pairs={{0,8},{1,9},{2,10},{3,11},{4,12},{5,13},{6,14},{7,15},{8,16},{9,17... | collective-permute-start | bytes 589832 | tf_op jit(solution)/shard_map/ppermute | solution.py:110
  107.8 16.0 %entry_spatial.1 = (bf16[2,2,8,8,16,512]{5,4,3,2,1,0:T(8,128)(2,1)}, bf16[7,2,7,2,16,512]{5,4,3,2,1,0:T(8,128)(2,1)}, bf16[7,7,16,512]{3,2,1,0:T(8,128)(2,1)S(1)}, f32[8,512]{1,0:T(8,128)S(1)}) custom-call(bf16[7,2,7,2,16,512]{5,4,3,2,1,0:T(8,128)(2,1)} %bitcast.223, f32[8,512]{1,0:T(8,128)S(1)} %add_add_fusion.22.refs_1_.refs_12_.refs_2_, ...), custom_call_target="tpu_custom_call" | custom-call | flops 3699376128 | bytes 10330112 | tf_op jit(solution)/shard_map/entry_spatial/pallas_call | solution.py:339
  143.1 6.5 %expand.1 = (bf16[7,7,16,512]{3,2,1,0:T(8,128)(2,1)S(1)}, bf16[7,7,16,512]{3,2,1,0:T(8,128)(2,1)S(1)}, bf16[7,7,16,2048]{3,2,1,0:T(8,128)(2,1)}, f32[8,2048]{1,0:T(8,128)S(1)}) custom-call(bf16[7,7,16,512]{3,2,1,0:T(8,128)(2,1)S(1)} %get-tuple-element.153.refs_0_.refs_13_.refs_1_, f32[8,512]{1,0:T(8,128)S(1)} %add_add_fusion.20.refs_1_.refs_14_.refs_2_, ...), custom_call_target="tpu_custom_call" | custom-call | flops 1644167168 | bytes 7882752 | tf_op jit(solution)/shard_map/expand/pallas_call | solution.py:339
  149.7 7.6 %collective-permute-done.27 = bf16[4,2,1,1,96,512]{5,4,3,2,1,0:T(8,128)(2,1)} collective-permute-done((bf16[4,2,1,1,96,512]{5,4,3,2,1,0:T(8,128)(2,1)S(1)}, bf16[4,2,1,1,96,512]{5,4,3,2,1,0:T(8,128)(2,1)}, u32[]{:S(2)}, u32[]{:S(2)}) %collective-permute-start.27) | collective-permute-done | bytes 786464 | tf_op jit(solution)/shard_map/ppermute | solution.py:23
  176.2 7.9 %strided.1 = (bf16[7,7,16,2048]{3,2,1,0:T(8,128)(2,1)}, f32[8,2048]{1,0:T(8,128)S(1)}) custom-call(bf16[7,2,7,2,16,1024]{5,4,3,2,1,0:T(8,128)(2,1)} %bitcast.192, bf16[32,192,512]{2,1,0:T(8,128)(2,1)} %bitcast.206, s32[16,512]{1,0:T(8,128)S(1)} %broadcast_in_dim.34.refs_6_.refs_2_.refs_7_.refs_5_.refs_4_.refs_9_, ...), custom_call_target="tpu_custom_call" | custom-call | flops 3288334336 | bytes 12845056 | tf_op jit(solution)/shard_map/strided/pallas_call | solution.py:339
  206.3 10.5 %middle.1 = (bf16[7,7,16,2048]{3,2,1,0:T(8,128)(2,1)}, bf16[7,7,16,2048]{3,2,1,0:T(8,128)(2,1)}, bf16[7,7,16,512]{3,2,1,0:T(8,128)(2,1)S(1)}, f32[8,512]{1,0:T(8,128)S(1)}) custom-call(bf16[7,7,16,2048]{3,2,1,0:T(8,128)(2,1)} %get-tuple-element.165.refs_0_.refs_13_.refs_1_, bf16[7,7,16,2048]{3,2,1,0:T(8,128)(2,1)} %get-tuple-element.168.refs_1_.refs_14_.refs_2_, ...), custom_call_target="tpu_custom_call" | custom-call | flops 1644167168 | bytes 13080576 | tf_op jit(solution)/shard_map/middle/pallas_call | solution.py:339
  232.9 7.0 %inner_spatial.1 = (bf16[9,9,16,512]{3,2,1,0:T(8,128)(2,1)S(1)}, bf16[7,7,16,512]{3,2,1,0:T(8,128)(2,1)S(1)}, bf16[7,7,16,512]{3,2,1,0:T(8,128)(2,1)S(1)}, f32[8,512]{1,0:T(8,128)S(1)}) custom-call(bf16[7,7,16,512]{3,2,1,0:T(8,128)(2,1)S(1)} %get-tuple-element.171.refs_0_.refs_10_.refs_1_, f32[8,512]{1,0:T(8,128)S(1)} %add_add_fusion.18.refs_1_.refs_11_.refs_2_, ...), custom_call_target="tpu_custom_call" | custom-call | flops 3699376128 | bytes 7817216 | tf_op jit(solution)/shard_map/inner_spatial/pallas_call | solution.py:339
  257.8 6.6 %inner_expand.1 = (bf16[7,7,16,512]{3,2,1,0:T(8,128)(2,1)S(1)}, bf16[7,7,16,512]{3,2,1,0:T(8,128)(2,1)S(1)}, bf16[7,7,16,2048]{3,2,1,0:T(8,128)(2,1)}, f32[8,2048]{1,0:T(8,128)S(1)}) custom-call(bf16[7,7,16,512]{3,2,1,0:T(8,128)(2,1)S(1)} %get-tuple-element.175.refs_0_.refs_10_.refs_1_, f32[8,512]{1,0:T(8,128)S(1)} %add_add_fusion.16.refs_1_.refs_11_.refs_2_, ...), custom_call_target="tpu_custom_call" | custom-call | flops 1644167168 | bytes 7784448 | tf_op jit(solution)/shard_map/inner_expand/pallas_call | solution.py:339
  283.0 10.8 %close.1 = (bf16[7,7,16,2048]{3,2,1,0:T(8,128)(2,1)}, bf16[7,7,16,2048]{3,2,1,0:T(8,128)(2,1)}, f32[8,2048]{1,0:T(8,128)S(1)}) custom-call(bf16[7,7,16,2048]{3,2,1,0:T(8,128)(2,1)} %get-tuple-element.177.refs_0_.refs_1_, f32[8,2048]{1,0:T(8,128)S(1)} %pad_maximum_fusion.28.refs_1_.refs_2_, f32[6,2048]{1,0:T(8,128)S(1)} %bitcast.204, ...), custom_call_target="tpu_custom_call" | custom-call | bytes 9918464 | tf_op jit(solution)/shard_map/close/pallas_call | solution.py:339
  311.6 8.0 %back_inner_expand.1 = (bf16[7,7,16,2048]{3,2,1,0:T(8,128)(2,1)}, f32[7,7,16,512]{3,2,1,0:T(8,128)S(1)}, f32[8,512]{1,0:T(8,128)S(1)}) custom-call(bf16[7,7,16,2048]{3,2,1,0:T(8,128)(2,1)} %get-tuple-element.181.refs_0_.refs_11_, bf16[7,7,16,2048]{3,2,1,0:T(8,128)(2,1)} %get-tuple-element.177.refs_0_.refs_1_, ...), custom_call_target="tpu_custom_call" | custom-call | flops 1644167168 | bytes 15177728 | tf_op jit(solution)/shard_map/back_inner_expand/pallas_call | solution.py:339
  336.3 6.7 %back_inner_spatial.1 = (bf16[7,7,16,512]{3,2,1,0:T(8,128)(2,1)S(1)}, f32[7,7,16,512]{3,2,1,0:T(8,128)S(1)}, f32[8,512]{1,0:T(8,128)S(1)}) custom-call(f32[7,7,16,512]{3,2,1,0:T(8,128)S(1)} %get-tuple-element.184.refs_0_, bf16[7,7,16,512]{3,2,1,0:T(8,128)(2,1)S(1)} %get-tuple-element.175.refs_0_.refs_10_.refs_1_, f32[8,512]{1,0:T(8,128)S(1)} %copy-done.26, ...), custom_call_target="tpu_custom_call" | custom-call | flops 3699376128 | bytes 11028480 | tf_op jit(solution)/shard_map/back_inner_spatial/pallas_call | solution.py:339
  358.2 7.9 %inner_spatial_grad.1 = bf16[32,208,512]{2,1,0:T(8,128)(2,1)} custom-call(bf16[9,9,16,512]{3,2,1,0:T(8,128)(2,1)S(1)} %copy-done.4, bf16[7,7,16,512]{3,2,1,0:T(8,128)(2,1)S(1)} %get-tuple-element.193.refs_1_, bf16[32,208,512]{2,1,0:T(8,128)(2,1)} %inner_expand_grad.1.refs_2_), custom_call_target="tpu_custom_call", output_to_operand_aliasing={{}: (2, {})} | custom-call | flops 3699376128 | bytes 2129920 | tf_op jit(solution)/shard_map/inner_spatial_grad/pallas_call | solution.py:339
  370.7 10.6 %back_middle.1 = (bf16[7,7,16,512]{3,2,1,0:T(8,128)(2,1)S(1)}, bf16[7,7,16,2048]{3,2,1,0:T(8,128)(2,1)}, f32[16,2048]{1,0:T(8,128)S(1)}) custom-call(f32[7,7,16,512]{3,2,1,0:T(8,128)S(1)} %get-tuple-element.189.refs_0_, bf16[7,7,16,512]{3,2,1,0:T(8,128)(2,1)S(1)} %copy-done.13, f32[8,512]{1,0:T(8,128)S(1)} %copy-done.38, f32[8,512]{1,0:T(8,128)S(1)} %copy-done.31, ...), custom_call_target="tpu_custom_call" | custom-call | flops 1644167168 | bytes 25102336 | tf_op jit(solution)/shard_map/back_middle/pallas_call | solution.py:339
  404.0 9.9 %back_entry_expand.1 = (bf16[7,7,16,2048]{3,2,1,0:T(8,128)(2,1)}, bf16[7,7,16,2048]{3,2,1,0:T(8,128)(2,1)}, f32[7,7,16,512]{3,2,1,0:T(8,128)S(1)}, f32[8,512]{1,0:T(8,128)}) custom-call(bf16[7,7,16,2048]{3,2,1,0:T(8,128)(2,1)} %get-tuple-element.199.refs_0_, bf16[7,7,16,2048]{3,2,1,0:T(8,128)(2,1)} %get-tuple-element.165.refs_0_.refs_13_.refs_1_, ...), custom_call_target="tpu_custom_call" | custom-call | flops 1644167168 | bytes 18667520 | tf_op jit(solution)/shard_map/back_entry_expand/pallas_call | solution.py:339
  432.3 9.0 %project_grad.1 = bf16[32,256,512]{2,1,0:T(8,128)(2,1)} custom-call(bf16[7,2,7,2,16,1024]{5,4,3,2,1,0:T(8,128)(2,1)} %bitcast.193, bf16[7,7,16,2048]{3,2,1,0:T(8,128)(2,1)} %get-tuple-element.207.refs_1_.refs_0_, bf16[32,256,512]{2,1,0:T(8,128)(2,1)} %expand_grad.1.refs_2_), custom_call_target="tpu_custom_call", output_to_operand_aliasing={{}: (2, {})} | custom-call | flops 3288334336 | bytes 9633792 | tf_op jit(solution)/shard_map/project_grad/pallas_call | solution.py:339
  462.3 8.6 %back_strided.1.refs_2_ = f32[7,7,16,1024]{3,2,1,0:T(8,128)} custom-call(bf16[7,7,16,2048]{3,2,1,0:T(8,128)(2,1)} %get-tuple-element.207.refs_1_.refs_0_, bf16[32,192,512]{2,1,0:T(8,128)(2,1)} %bitcast.209), custom_call_target="tpu_custom_call" | custom-call | flops 3288334336 | bytes 9502720 | tf_op jit(solution)/shard_map/back_strided/pallas_call | solution.py:339
  470.9 10.4 %back_entry_spatial.1 = (bf16[7,7,16,512]{3,2,1,0:T(8,128)(2,1)S(1)}, bf16[7,2,7,2,16,512]{5,4,3,2,1,0:T(8,128)(2,1)}, f32[8,512]{1,0:T(8,128)S(1)}) custom-call(f32[7,7,16,512]{3,2,1,0:T(8,128)S(1)} %get-tuple-element.213.refs_0_, bf16[7,7,16,512]{3,2,1,0:T(8,128)(2,1)S(1)} %get-tuple-element.153.refs_0_.refs_13_.refs_1_, f32[8,512]{1,0:T(8,128)S(1)} %copy-done.22, ...), custom_call_target="tpu_custom_call" | custom-call | flops 3699376128 | bytes 15949824 | tf_op jit(solution)/shard_map/back_entry_spatial/pallas_call | solution.py:339
  481.3 10.2 %entry_spatial_grad.1 = bf16[32,144,512]{2,1,0:T(8,128)(2,1)} custom-call(bf16[2,2,8,8,16,512]{5,4,3,2,1,0:T(8,128)(2,1)} %get-tuple-element.218.refs_0_, bf16[7,7,16,512]{3,2,1,0:T(8,128)(2,1)S(1)} %get-tuple-element.219.refs_1_), custom_call_target="tpu_custom_call" | custom-call | flops 3699376128 | bytes 4997120 | tf_op jit(solution)/shard_map/entry_spatial_grad/pallas_call | solution.py:339
  494.8 12.4 %collective-permute-done.99 = bf16[4,2,1,1,128,512]{5,4,3,2,1,0:T(8,128)(2,1)S(1)} collective-permute-done((bf16[4,2,1,1,128,512]{5,4,3,2,1,0:T(8,128)(2,1)S(1)}, bf16[4,2,1,1,128,512]{5,4,3,2,1,0:T(8,128)(2,1)S(1)}, u32[]{:S(2)}, u32[]{:S(2)}) %collective-permute-start.99) | collective-permute-done | bytes 1048608 | tf_op jit(solution)/shard_map/ppermute | solution.py:23
  526.7 11.8 %back_first.1 = (bf16[14,14,16,512]{3,2,1,0:T(8,128)(2,1)}, bf16[32,32,512]{2,1,0:T(8,128)(2,1)S(1)}) custom-call(bf16[14,14,16,512]{3,2,1,0:T(8,128)(2,1)} %bitcast.238, bf16[14,14,16,512]{3,2,1,0:T(8,128)(2,1)} %get-tuple-element.150.refs_1_, f32[8,512]{1,0:T(8,128)S(1)} %copy-done.24, f32[8,512]{1,0:T(8,128)S(1)} %add_add_fusion.8.refs_3_, ...), custom_call_target="tpu_custom_call" | custom-call | flops 3288334336 | bytes 13027328 | tf_op jit(solution)/shard_map/back_first/pallas_call | solution.py:339
  551.1 11.6 %input_grad.1 = f32[14,14,16,1024]{3,2,1,0:T(8,128)} custom-call(bf16[14,14,16,512]{3,2,1,0:T(8,128)(2,1)} %get-tuple-element.239.refs_0_, bf16[32,32,512]{2,1,0:T(8,128)(2,1)} %bitcast.236, f32[7,7,16,1024]{3,2,1,0:T(8,128)} %back_strided.1.refs_2_), custom_call_target="tpu_custom_call" | custom-call | flops 3288334336 | bytes 7471104 | tf_op jit(solution)/shard_map/input_grad/pallas_call | solution.py:339
  591.6 6.3 collective-permute-start.120
  606.5 7.6 %collective-permute-done.121 = bf16[1,1,1,176,512]{4,3,2,1,0:T(8,128)(2,1)S(1)} collective-permute-done((bf16[1,1,1,176,512]{4,3,2,1,0:T(8,128)(2,1)S(1)}, bf16[1,1,1,176,512]{4,3,2,1,0:T(8,128)(2,1)S(1)}, u32[]{:S(2)}, u32[]{:S(2)}) %collective-permute-start.121) | collective-permute-done | bytes 180256 | tf_op jit(solution)/shard_map/ppermute | solution.py:23
  (626 shorter events, 400.4 us)
Async XLA Ops:
  7.2 95.6 %all-gather.8.cloned.1.call-start = ((), (), s32[]{:S(2)}) async-start(), calls=%async_computation.3 | async-start | bytes 7299072 | tf_op jit(solution)/shard_map/all_gather | solution.py:1047
  14.1 218.8 %all-gather.6.cloned.1.call-start = ((), (), s32[]{:S(2)}) async-start(), calls=%async_computation.2 | async-start | bytes 7028736 | tf_op jit(solution)/shard_map/all_gather | solution.py:968
  36.8 502.3 %reduce-scatter.2.cloned.1.call-start = ((), (), s32[]{:S(2)}) async-start(), calls=%async_computation.1 | async-start | bytes 7028736 | tf_op jit(solution)/shard_map/reduce_scatter | solution.py:1208
  47.6 13.3 %collective-permute-start.6 = (bf16[192,512]{1,0:T(8,128)(2,1)S(1)}, bf16[192,512]{1,0:T(8,128)(2,1)S(1)}, u32[]{:S(2)}, u32[]{:S(2)}) collective-permute-start(bf16[192,512]{1,0:T(8,128)(2,1)S(1)} %pad_maximum_fusion.17), channel_id=1, source_target_pairs={{8,0},{9,1},{10,2},{11,3},{12,4},{13,5},{14,6},{15,7},{16,8},{17,9... | collective-permute-start | bytes 589832 | tf_op jit(solution)/shard_map/ppermute | solution.py:110
  80.0 14.6 %collective-permute-start.16 = (bf16[192,512]{1,0:T(8,128)(2,1)S(1)}, bf16[192,512]{1,0:T(8,128)(2,1)S(1)}, u32[]{:S(2)}, u32[]{:S(2)}) collective-permute-start(bf16[192,512]{1,0:T(8,128)(2,1)S(1)} %collective-permute-done.6), channel_id=1, source_target_pairs={{8,0},{9,1},{10,2},{11,3},{12,4},{13,5},{14,6},{15,7},{16,8},{17,9... | collective-permute-start | bytes 589832 | tf_op jit(solution)/shard_map/ppermute | solution.py:110
  102.8 20.9 %collective-permute-start.19 = (bf16[4,1,1,1,96,512]{5,4,3,2,1,0:T(8,128)(2,1)S(1)}, bf16[4,1,1,1,96,512]{5,4,3,2,1,0:T(8,128)(2,1)S(1)}, u32[]{:S(2)}, u32[]{:S(2)}) collective-permute-start(bf16[4,1,1,1,96,512]{5,4,3,2,1,0:T(8,128)(2,1)S(1)} %get-tuple-element.156), channel_id=1, source_target_pairs={{0,2},{1,3},{2,0},{3,1},{4,6},{5,7},{6,4},{7,5},{8,10},{9,11},{10,... | collective-permute-start | bytes 1179656 | tf_op jit(solution)/shard_map/ppermute | solution.py:23
  104.1 19.9 %collective-permute-start.18 = (bf16[4,1,1,1,96,512]{5,4,3,2,1,0:T(8,128)(2,1)S(1)}, bf16[4,1,1,1,96,512]{5,4,3,2,1,0:T(8,128)(2,1)}, u32[]{:S(2)}, u32[]{:S(2)}) collective-permute-start(bf16[4,1,1,1,96,512]{5,4,3,2,1,0:T(8,128)(2,1)S(1)} %get-tuple-element.155), channel_id=1, source_target_pairs={{0,4},{1,5},{2,6},{3,7},{4,0},{5,1},{6,2},{7,3},{8,12},{9,13},{10,... | collective-permute-start | bytes 1179656 | tf_op jit(solution)/shard_map/ppermute | solution.py:23
  133.0 24.3 %collective-permute-start.27 = (bf16[4,2,1,1,96,512]{5,4,3,2,1,0:T(8,128)(2,1)S(1)}, bf16[4,2,1,1,96,512]{5,4,3,2,1,0:T(8,128)(2,1)}, u32[]{:S(2)}, u32[]{:S(2)}) collective-permute-start(bf16[4,2,1,1,96,512]{5,4,3,2,1,0:T(8,128)(2,1)S(1)} %pad_maximum_fusion.5), channel_id=1, source_target_pairs={{0,2},{1,3},{2,0},{3,1},{4,6},{5,7},{6,4},{7,5},{8,10},{9,11},{10,... | collective-permute-start | bytes 2359304 | tf_op jit(solution)/shard_map/ppermute | solution.py:23
  134.1 25.1 %collective-permute-start.28 = (bf16[4,1,2,1,96,512]{5,4,3,2,1,0:T(8,128)(2,1)S(1)}, bf16[4,1,2,1,96,512]{5,4,3,2,1,0:T(8,128)(2,1)}, u32[]{:S(2)}, u32[]{:S(2)}) collective-permute-start(bf16[4,1,2,1,96,512]{5,4,3,2,1,0:T(8,128)(2,1)S(1)} %pad_maximum_fusion.6), channel_id=1, source_target_pairs={{0,4},{1,5},{2,6},{3,7},{4,0},{5,1},{6,2},{7,3},{8,12},{9,13},{10,... | collective-permute-start | bytes 2359304 | tf_op jit(solution)/shard_map/ppermute | solution.py:23
  461.7 33.1 %collective-permute-start.100 = (bf16[4,1,2,1,128,512]{5,4,3,2,1,0:T(8,128)(2,1)S(1)}, bf16[4,1,2,1,128,512]{5,4,3,2,1,0:T(8,128)(2,1)S(1)}, u32[]{:S(2)}, u32[]{:S(2)}) collective-permute-start(bf16[4,1,2,1,128,512]{5,4,3,2,1,0:T(8,128)(2,1)S(1)} %add_convert_fusion), channel_id=1, source_target_pairs={{0,4},{1,5},{2,6},{3,7},{4,0},{5,1},{6,2},{7,3},{8,12},{9,13},{10,... | collective-permute-start | bytes 3145736 | tf_op jit(solution)/shard_map/ppermute | solution.py:23
  461.8 45.4 %collective-permute-start.99 = (bf16[4,2,1,1,128,512]{5,4,3,2,1,0:T(8,128)(2,1)S(1)}, bf16[4,2,1,1,128,512]{5,4,3,2,1,0:T(8,128)(2,1)S(1)}, u32[]{:S(2)}, u32[]{:S(2)}) collective-permute-start(bf16[4,2,1,1,128,512]{5,4,3,2,1,0:T(8,128)(2,1)S(1)} %add_convert_fusion.1), channel_id=1, source_target_pairs={{0,2},{1,3},{2,0},{3,1},{4,6},{5,7},{6,4},{7,5},{8,10},{9,11},{10,... | collective-permute-start | bytes 3145736 | tf_op jit(solution)/shard_map/ppermute | solution.py:23
  507.7 31.6 %collective-permute-start.110 = (bf16[4,2,2,1,144,512]{5,4,3,2,1,0:T(8,128)(2,1)}, bf16[4,2,2,1,144,512]{5,4,3,2,1,0:T(8,128)(2,1)}, u32[]{:S(2)}, u32[]{:S(2)}) collective-permute-start(bf16[4,2,2,1,144,512]{5,4,3,2,1,0:T(8,128)(2,1)} %constant_dynamic-slice_fusion.3), channel_id=1, source_target_pairs={{0,1},{1,0},{2,3},{3,2},{4,5},{5,4},{6,7},{7,6},{8,9},{9,8},{10,11... | collective-permute-start | bytes 7077896 | tf_op jit(solution)/shard_map/ppermute | solution.py:23
  524.2 14.3 %collective-permute-start.105 = (bf16[4,1,1,1,128,512]{5,4,3,2,1,0:T(8,128)(2,1)S(1)}, bf16[4,1,1,1,128,512]{5,4,3,2,1,0:T(8,128)(2,1)S(1)}, u32[]{:S(2)}, u32[]{:S(2)}) collective-permute-start(bf16[4,1,1,1,128,512]{5,4,3,2,1,0:T(8,128)(2,1)S(1)} %get-tuple-element.223), channel_id=1, source_target_pairs={{0,4},{1,5},{2,6},{3,7},{4,0},{5,1},{6,2},{7,3},{8,12},{9,13},{10,... | collective-permute-start | bytes 1572872 | tf_op jit(solution)/shard_map/ppermute | solution.py:23
  524.7 13.8 %collective-permute-start.106 = (bf16[4,1,1,1,128,512]{5,4,3,2,1,0:T(8,128)(2,1)S(1)}, bf16[4,1,1,1,128,512]{5,4,3,2,1,0:T(8,128)(2,1)S(1)}, u32[]{:S(2)}, u32[]{:S(2)}) collective-permute-start(bf16[4,1,1,1,128,512]{5,4,3,2,1,0:T(8,128)(2,1)S(1)} %get-tuple-element.224), channel_id=1, source_target_pairs={{0,2},{1,3},{2,0},{3,1},{4,6},{5,7},{6,4},{7,5},{8,10},{9,11},{10,... | collective-permute-start | bytes 1572872 | tf_op jit(solution)/shard_map/ppermute | solution.py:23
  544.7 24.9 %collective-permute-start.116 = (bf16[4,1,2,1,96,512]{5,4,3,2,1,0:T(8,128)(2,1)S(1)}, bf16[4,1,2,1,96,512]{5,4,3,2,1,0:T(8,128)(2,1)S(1)}, u32[]{:S(2)}, u32[]{:S(2)}) collective-permute-start(bf16[4,1,2,1,96,512]{5,4,3,2,1,0:T(8,128)(2,1)S(1)} %pad_maximum_fusion.7), channel_id=1, source_target_pairs={{0,4},{1,5},{2,6},{3,7},{4,0},{5,1},{6,2},{7,3},{8,12},{9,13},{10,... | collective-permute-start | bytes 2359304 | tf_op jit(solution)/shard_map/ppermute | solution.py:23
  545.4 23.0 %collective-permute-start.115 = (bf16[4,2,1,1,80,512]{5,4,3,2,1,0:T(8,128)(2,1)S(1)}, bf16[4,2,1,1,80,512]{5,4,3,2,1,0:T(8,128)(2,1)S(1)}, u32[]{:S(2)}, u32[]{:S(2)}) collective-permute-start(bf16[4,2,1,1,80,512]{5,4,3,2,1,0:T(8,128)(2,1)S(1)} %add_convert_fusion.2), channel_id=1, source_target_pairs={{0,2},{1,3},{2,0},{3,1},{4,6},{5,7},{6,4},{7,5},{8,10},{9,11},{10,... | collective-permute-start | bytes 1966088 | tf_op jit(solution)/shard_map/ppermute | solution.py:23
  546.5 16.3 %collective-permute-start.112 = (bf16[1,1,1,256,512]{4,3,2,1,0:T(8,128)(2,1)S(1)}, bf16[1,1,1,256,512]{4,3,2,1,0:T(8,128)(2,1)S(1)}, u32[]{:S(2)}, u32[]{:S(2)}) collective-permute-start(bf16[1,1,1,256,512]{4,3,2,1,0:T(8,128)(2,1)S(1)} %pad_maximum_fusion.13), channel_id=1, source_target_pairs={{0,8},{1,9},{2,10},{3,11},{4,12},{5,13},{6,14},{7,15},{8,0},{9,1},... | collective-permute-start | bytes 786440 | tf_op jit(solution)/shard_map/ppermute | solution.py:23
  546.6 21.7 %collective-permute-start.113 = (bf16[1,1,1,256,512]{4,3,2,1,0:T(8,128)(2,1)S(1)}, bf16[1,1,1,256,512]{4,3,2,1,0:T(8,128)(2,1)S(1)}, u32[]{:S(2)}, u32[]{:S(2)}) collective-permute-start(bf16[1,1,1,256,512]{4,3,2,1,0:T(8,128)(2,1)S(1)} %pad_maximum_fusion.14), channel_id=1, source_target_pairs={{0,16},{1,17},{2,18},{3,19},{4,20},{5,21},{6,22},{7,23},{8,24},{9,... | collective-permute-start | bytes 786440 | tf_op jit(solution)/shard_map/ppermute | solution.py:23
  549.9 18.4 %collective-permute-start.114 = (bf16[1,1,1,256,512]{4,3,2,1,0:T(8,128)(2,1)S(1)}, bf16[1,1,1,256,512]{4,3,2,1,0:T(8,128)(2,1)S(1)}, u32[]{:S(2)}, u32[]{:S(2)}) collective-permute-start(bf16[1,1,1,256,512]{4,3,2,1,0:T(8,128)(2,1)S(1)} %pad_maximum_fusion.15), channel_id=1, source_target_pairs={{0,24},{1,25},{2,26},{3,27},{4,28},{5,29},{6,30},{7,31},{8,16},{9,... | collective-permute-start | bytes 786440 | tf_op jit(solution)/shard_map/ppermute | solution.py:23
  573.8 17.4 %collective-permute-start.117 = (bf16[1,1,464,512]{3,2,1,0:T(8,128)(2,1)S(1)}, bf16[1,1,464,512]{3,2,1,0:T(8,128)(2,1)S(1)}, u32[]{:S(2)}, u32[]{:S(2)}) collective-permute-start(bf16[1,1,464,512]{3,2,1,0:T(8,128)(2,1)S(1)} %maximum_bitcast_fusion), channel_id=1, source_target_pairs={{0,2},{1,3},{2,0},{3,1},{4,6},{5,7},{6,4},{7,5},{8,10},{9,11},{10,... | collective-permute-start | bytes 1425416 | tf_op jit(solution)/shard_map/ppermute | solution.py:23
  591.4 22.8 %collective-permute-start.123 = (bf16[2,1,464,512]{3,2,1,0:T(8,128)(2,1)S(1)}, bf16[2,1,464,512]{3,2,1,0:T(8,128)(2,1)S(1)}, u32[]{:S(2)}, u32[]{:S(2)}) collective-permute-start(bf16[2,1,464,512]{3,2,1,0:T(8,128)(2,1)S(1)} %pad_maximum_fusion.4), channel_id=1, source_target_pairs={{0,1},{1,0},{2,3},{3,2},{4,5},{5,4},{6,7},{7,6},{8,9},{9,8},{10,11... | collective-permute-start | bytes 2850824 | tf_op jit(solution)/shard_map/ppermute | solution.py:23
  591.6 14.9 %collective-permute-start.120 = (bf16[1,1,1,176,512]{4,3,2,1,0:T(8,128)(2,1)S(1)}, bf16[1,1,1,176,512]{4,3,2,1,0:T(8,128)(2,1)S(1)}, u32[]{:S(2)}, u32[]{:S(2)}) collective-permute-start(bf16[1,1,1,176,512]{4,3,2,1,0:T(8,128)(2,1)S(1)} %pad_maximum_fusion.18), channel_id=1, source_target_pairs={{0,8},{1,9},{2,10},{3,11},{4,12},{5,13},{6,14},{7,15},{8,0},{9,1},... | collective-permute-start | bytes 540680 | tf_op jit(solution)/shard_map/ppermute | solution.py:23
  598.0 16.1 %collective-permute-start.121 = (bf16[1,1,1,176,512]{4,3,2,1,0:T(8,128)(2,1)S(1)}, bf16[1,1,1,176,512]{4,3,2,1,0:T(8,128)(2,1)S(1)}, u32[]{:S(2)}, u32[]{:S(2)}) collective-permute-start(bf16[1,1,1,176,512]{4,3,2,1,0:T(8,128)(2,1)S(1)} %pad_maximum_fusion.19), channel_id=1, source_target_pairs={{0,16},{1,17},{2,18},{3,19},{4,20},{5,21},{6,22},{7,23},{8,24},{9,... | collective-permute-start | bytes 540680 | tf_op jit(solution)/shard_map/ppermute | solution.py:23
  599.0 15.1 %collective-permute-start.122 = (bf16[1,1,1,176,512]{4,3,2,1,0:T(8,128)(2,1)S(1)}, bf16[1,1,1,176,512]{4,3,2,1,0:T(8,128)(2,1)S(1)}, u32[]{:S(2)}, u32[]{:S(2)}) collective-permute-start(bf16[1,1,1,176,512]{4,3,2,1,0:T(8,128)(2,1)S(1)} %pad_maximum_fusion.20), channel_id=1, source_target_pairs={{0,24},{1,25},{2,26},{3,27},{4,28},{5,29},{6,30},{7,31},{8,16},{9,... | collective-permute-start | bytes 540680 | tf_op jit(solution)/shard_map/ppermute | solution.py:23
  (170 other events, 1408.0 us)
Sparse Core Ops, SparseCore 0:
  14.2 80.5 all-gather.7
  98.3 77.4 all-gather.5
  366.8 146.4 reduce-scatter.1

commit v4 on v3

--- a/solution.py
+++ b/solution.py
@@ -1035,7 +1035,7 @@
         inner_norm_spatial,
         inner_norm_expand,
     )
-    table_cells = jnp.concatenate([t.reshape(2 * GROUPS, -1) for t in tables_all], axis=1)
+    table_cells = jnp.concatenate(tables_all, axis=2).reshape(2 * GROUPS, -1)
     table_rows = -(-table_cells.size // (copies * LANES))
     table_part = jnp.pad(
         table_cells.reshape(-1), (0, copies * table_rows * LANES - table_cells.size)
@@ -1314,7 +1314,9 @@
     g_project, g_ireduce, g_expand, g_ispatial, g_iexpand = shares(
         gather_copy(early_own, 0), middle_grads + [inner_spatial, inner_expand]
     )
-    last_own, g_project, g_ispatial = after(last_own, g_project, g_ispatial)
+    last_own, g_project, g_ireduce, g_expand, g_ispatial, g_iexpand = after(
+        last_own, g_project, g_ireduce, g_expand, g_ispatial, g_iexpand
+    )
     last_own = gather_copy(last_own.reshape(1, 1, -1, LANES), 1)
     g_spatial, g_reduce = shares(gather_copy(last_own, 0), [entry_spatial, entry_reduce])
 

time: 645 us -> 641 us (level)
    unnamed x154 -> x151, local copies, waits for them, and re-layouts: 25.5 us -> 20.7 us
  transfers between devices with their start and end apart: 129 -> 129, of which waited for: 85 -> 86; matrix products, arithmetic and copies ran while one was open for 10% -> 10% of each run, Pallas kernels for 24% -> 25%
where the time goes in v4:
time: 641 us; the launch traced here: 634 us
  Pallas kernels  194 us (30%)
  waiting for transfers between devices  183 us (29%)
  starting transfers between devices  151 us (24%)
  local copies, waits for them, and re-layouts  49.8 us (8%)
  other arithmetic  38.1 us (6%)
  between operations  17.7 us (3%)
    pallas_call x22, Pallas kernels, call(): pl.pallas_call(body, name=name, grid=(steps,), in_specs=[s for g in group...  194 us
    ppermute x120, waiting for transfers between devices, xor_swap(): return lax.ppermute(value, AXES, [(d, d ^ distance) for d in range(count)])  164 us
    ppermute x120, starting transfers between devices, xor_swap(): return lax.ppermute(value, AXES, [(d, d ^ distance) for d in range(count)])  136 us
    unnamed x151, local copies, waits for them, and re-layouts  20.7 us
    ppermute x6, waiting for transfers between devices, line_shift(): return lax.ppermute(value, AXES, pairs)  19 us
    ppermute x6, starting transfers between devices, line_shift(): return lax.ppermute(value, AXES, pairs)  15 us
  transfers between devices with their start and end apart: 129, of which 86 were waited for; matrix products, arithmetic and copies ran while one was open for 10% of the time, Pallas kernels for 25%

profile of v4, /device:TPU:0, one launch (start us, length us, event | category | flops | bytes accessed | tf_op | source)
XLA Modules:
  0.0 633.7 jit_solution(6638963254314265540)
XLA Ops:
  44.1 7.3 %first.1 = (bf16[14,14,16,512]{3,2,1,0:T(8,128)(2,1)}, f32[8,512]{1,0:T(8,128)S(1)}) custom-call(bf16[14,14,16,1024]{3,2,1,0:T(8,128)(2,1)S(1)} %bitcast.195, bf16[32,32,512]{2,1,0:T(8,128)(2,1)} %bitcast.235, s32[16,512]{1,0:T(8,128)S(1)} %broadcast_in_dim.24.refs_2_.refs_6_, ...), custom_call_target="tpu_custom_call" | custom-call | flops 3288334336 | bytes 7604224 | tf_op jit(solution)/shard_map/first/pallas_call | solution.py:339
  83.3 6.4 %collective-permute-start.15 = (bf16[192,512]{1,0:T(8,128)(2,1)S(1)}, bf16[192,512]{1,0:T(8,128)(2,1)S(1)}, u32[]{:S(2)}, u32[]{:S(2)}) collective-permute-start(bf16[192,512]{1,0:T(8,128)(2,1)S(1)} %collective-permute-done.14), channel_id=1, source_target_pairs={{0,8},{1,9},{2,10},{3,11},{4,12},{5,13},{6,14},{7,15},{8,16},{9,17... | collective-permute-start | bytes 589832 | tf_op jit(solution)/shard_map/ppermute | solution.py:110
  103.5 15.9 %entry_spatial.1 = (bf16[2,2,8,8,16,512]{5,4,3,2,1,0:T(8,128)(2,1)}, bf16[7,2,7,2,16,512]{5,4,3,2,1,0:T(8,128)(2,1)}, bf16[7,7,16,512]{3,2,1,0:T(8,128)(2,1)S(1)}, f32[8,512]{1,0:T(8,128)S(1)}) custom-call(bf16[7,2,7,2,16,512]{5,4,3,2,1,0:T(8,128)(2,1)} %bitcast.223, f32[8,512]{1,0:T(8,128)S(1)} %add_add_fusion.22.refs_1_.refs_12_.refs_2_, ...), custom_call_target="tpu_custom_call" | custom-call | flops 3699376128 | bytes 10330112 | tf_op jit(solution)/shard_map/entry_spatial/pallas_call | solution.py:339
  139.0 6.5 %expand.1 = (bf16[7,7,16,512]{3,2,1,0:T(8,128)(2,1)S(1)}, bf16[7,7,16,512]{3,2,1,0:T(8,128)(2,1)S(1)}, bf16[7,7,16,2048]{3,2,1,0:T(8,128)(2,1)}, f32[8,2048]{1,0:T(8,128)S(1)}) custom-call(bf16[7,7,16,512]{3,2,1,0:T(8,128)(2,1)S(1)} %get-tuple-element.156.refs_0_.refs_13_.refs_1_, f32[8,512]{1,0:T(8,128)S(1)} %add_add_fusion.20.refs_1_.refs_14_.refs_2_, ...), custom_call_target="tpu_custom_call" | custom-call | flops 1644167168 | bytes 7882752 | tf_op jit(solution)/shard_map/expand/pallas_call | solution.py:339
  145.5 7.2 %collective-permute-done.27 = bf16[4,2,1,1,96,512]{5,4,3,2,1,0:T(8,128)(2,1)} collective-permute-done((bf16[4,2,1,1,96,512]{5,4,3,2,1,0:T(8,128)(2,1)S(1)}, bf16[4,2,1,1,96,512]{5,4,3,2,1,0:T(8,128)(2,1)}, u32[]{:S(2)}, u32[]{:S(2)}) %collective-permute-start.27) | collective-permute-done | bytes 786464 | tf_op jit(solution)/shard_map/ppermute | solution.py:23
  172.2 7.9 %strided.1 = (bf16[7,7,16,2048]{3,2,1,0:T(8,128)(2,1)}, f32[8,2048]{1,0:T(8,128)S(1)}) custom-call(bf16[7,2,7,2,16,1024]{5,4,3,2,1,0:T(8,128)(2,1)} %bitcast.192, bf16[32,192,512]{2,1,0:T(8,128)(2,1)} %bitcast.206, s32[16,512]{1,0:T(8,128)S(1)} %broadcast_in_dim.34.refs_6_.refs_2_.refs_7_.refs_5_.refs_4_.refs_9_, ...), custom_call_target="tpu_custom_call" | custom-call | flops 3288334336 | bytes 12845056 | tf_op jit(solution)/shard_map/strided/pallas_call | solution.py:339
  202.3 10.5 %middle.1 = (bf16[7,7,16,2048]{3,2,1,0:T(8,128)(2,1)}, bf16[7,7,16,2048]{3,2,1,0:T(8,128)(2,1)}, bf16[7,7,16,512]{3,2,1,0:T(8,128)(2,1)S(1)}, f32[8,512]{1,0:T(8,128)S(1)}) custom-call(bf16[7,7,16,2048]{3,2,1,0:T(8,128)(2,1)} %get-tuple-element.168.refs_0_.refs_13_.refs_1_, bf16[7,7,16,2048]{3,2,1,0:T(8,128)(2,1)} %get-tuple-element.171.refs_1_.refs_14_.refs_2_, ...), custom_call_target="tpu_custom_call" | custom-call | flops 1644167168 | bytes 13080576 | tf_op jit(solution)/shard_map/middle/pallas_call | solution.py:339
  229.1 7.0 %inner_spatial.1 = (bf16[9,9,16,512]{3,2,1,0:T(8,128)(2,1)S(1)}, bf16[7,7,16,512]{3,2,1,0:T(8,128)(2,1)S(1)}, bf16[7,7,16,512]{3,2,1,0:T(8,128)(2,1)S(1)}, f32[8,512]{1,0:T(8,128)S(1)}) custom-call(bf16[7,7,16,512]{3,2,1,0:T(8,128)(2,1)S(1)} %get-tuple-element.174.refs_0_.refs_10_.refs_1_, f32[8,512]{1,0:T(8,128)S(1)} %add_add_fusion.18.refs_1_.refs_11_.refs_2_, ...), custom_call_target="tpu_custom_call" | custom-call | flops 3699376128 | bytes 7817216 | tf_op jit(solution)/shard_map/inner_spatial/pallas_call | solution.py:339
  253.7 6.6 %inner_expand.1 = (bf16[7,7,16,512]{3,2,1,0:T(8,128)(2,1)S(1)}, bf16[7,7,16,512]{3,2,1,0:T(8,128)(2,1)S(1)}, bf16[7,7,16,2048]{3,2,1,0:T(8,128)(2,1)}, f32[8,2048]{1,0:T(8,128)S(1)}) custom-call(bf16[7,7,16,512]{3,2,1,0:T(8,128)(2,1)S(1)} %get-tuple-element.178.refs_0_.refs_10_.refs_1_, f32[8,512]{1,0:T(8,128)S(1)} %add_add_fusion.16.refs_1_.refs_11_.refs_2_, ...), custom_call_target="tpu_custom_call" | custom-call | flops 1644167168 | bytes 7784448 | tf_op jit(solution)/shard_map/inner_expand/pallas_call | solution.py:339
  279.2 10.8 %close.1 = (bf16[7,7,16,2048]{3,2,1,0:T(8,128)(2,1)}, bf16[7,7,16,2048]{3,2,1,0:T(8,128)(2,1)}, f32[8,2048]{1,0:T(8,128)S(1)}) custom-call(bf16[7,7,16,2048]{3,2,1,0:T(8,128)(2,1)} %get-tuple-element.180.refs_0_.refs_1_, f32[8,2048]{1,0:T(8,128)S(1)} %pad_maximum_fusion.28.refs_1_.refs_2_, f32[6,2048]{1,0:T(8,128)S(1)} %bitcast.204, ...), custom_call_target="tpu_custom_call" | custom-call | bytes 9918464 | tf_op jit(solution)/shard_map/close/pallas_call | solution.py:339
  307.5 8.0 %back_inner_expand.1 = (bf16[7,7,16,2048]{3,2,1,0:T(8,128)(2,1)}, f32[7,7,16,512]{3,2,1,0:T(8,128)S(1)}, f32[8,512]{1,0:T(8,128)S(1)}) custom-call(bf16[7,7,16,2048]{3,2,1,0:T(8,128)(2,1)} %get-tuple-element.184.refs_0_.refs_11_, bf16[7,7,16,2048]{3,2,1,0:T(8,128)(2,1)} %get-tuple-element.180.refs_0_.refs_1_, ...), custom_call_target="tpu_custom_call" | custom-call | flops 1644167168 | bytes 15177728 | tf_op jit(solution)/shard_map/back_inner_expand/pallas_call | solution.py:339
  332.5 6.7 %back_inner_spatial.1 = (bf16[7,7,16,512]{3,2,1,0:T(8,128)(2,1)S(1)}, f32[7,7,16,512]{3,2,1,0:T(8,128)S(1)}, f32[8,512]{1,0:T(8,128)S(1)}) custom-call(f32[7,7,16,512]{3,2,1,0:T(8,128)S(1)} %get-tuple-element.187.refs_0_, bf16[7,7,16,512]{3,2,1,0:T(8,128)(2,1)S(1)} %get-tuple-element.178.refs_0_.refs_10_.refs_1_, f32[8,512]{1,0:T(8,128)S(1)} %copy-done.26, ...), custom_call_target="tpu_custom_call" | custom-call | flops 3699376128 | bytes 11028480 | tf_op jit(solution)/shard_map/back_inner_spatial/pallas_call | solution.py:339
  354.4 7.9 %inner_spatial_grad.1 = bf16[32,208,512]{2,1,0:T(8,128)(2,1)} custom-call(bf16[9,9,16,512]{3,2,1,0:T(8,128)(2,1)S(1)} %copy-done.4, bf16[7,7,16,512]{3,2,1,0:T(8,128)(2,1)S(1)} %get-tuple-element.196.refs_1_, bf16[32,208,512]{2,1,0:T(8,128)(2,1)} %inner_expand_grad.1.refs_2_), custom_call_target="tpu_custom_call", output_to_operand_aliasing={{}: (2, {})} | custom-call | flops 3699376128 | bytes 2129920 | tf_op jit(solution)/shard_map/inner_spatial_grad/pallas_call | solution.py:339
  366.9 10.6 %back_middle.1 = (bf16[7,7,16,512]{3,2,1,0:T(8,128)(2,1)S(1)}, bf16[7,7,16,2048]{3,2,1,0:T(8,128)(2,1)}, f32[16,2048]{1,0:T(8,128)S(1)}) custom-call(f32[7,7,16,512]{3,2,1,0:T(8,128)S(1)} %get-tuple-element.192.refs_0_, bf16[7,7,16,512]{3,2,1,0:T(8,128)(2,1)S(1)} %copy-done.13, f32[8,512]{1,0:T(8,128)S(1)} %copy-done.38, f32[8,512]{1,0:T(8,128)S(1)} %copy-done.31, ...), custom_call_target="tpu_custom_call" | custom-call | flops 1644167168 | bytes 25102336 | tf_op jit(solution)/shard_map/back_middle/pallas_call | solution.py:339
  400.3 10.0 %back_entry_expand.1 = (bf16[7,7,16,2048]{3,2,1,0:T(8,128)(2,1)}, bf16[7,7,16,2048]{3,2,1,0:T(8,128)(2,1)}, f32[7,7,16,512]{3,2,1,0:T(8,128)S(1)}, f32[8,512]{1,0:T(8,128)}) custom-call(bf16[7,7,16,2048]{3,2,1,0:T(8,128)(2,1)} %get-tuple-element.202.refs_0_, bf16[7,7,16,2048]{3,2,1,0:T(8,128)(2,1)} %get-tuple-element.168.refs_0_.refs_13_.refs_1_, ...), custom_call_target="tpu_custom_call" | custom-call | flops 1644167168 | bytes 18667520 | tf_op jit(solution)/shard_map/back_entry_expand/pallas_call | solution.py:339
  428.6 9.0 %project_grad.1 = bf16[32,256,512]{2,1,0:T(8,128)(2,1)} custom-call(bf16[7,2,7,2,16,1024]{5,4,3,2,1,0:T(8,128)(2,1)} %bitcast.193, bf16[7,7,16,2048]{3,2,1,0:T(8,128)(2,1)} %get-tuple-element.210.refs_1_.refs_0_, bf16[32,256,512]{2,1,0:T(8,128)(2,1)} %expand_grad.1.refs_2_), custom_call_target="tpu_custom_call", output_to_operand_aliasing={{}: (2, {})} | custom-call | flops 3288334336 | bytes 9633792 | tf_op jit(solution)/shard_map/project_grad/pallas_call | solution.py:339
  457.1 8.5 %back_strided.1.refs_2_ = f32[7,7,16,1024]{3,2,1,0:T(8,128)} custom-call(bf16[7,7,16,2048]{3,2,1,0:T(8,128)(2,1)} %get-tuple-element.210.refs_1_.refs_0_, bf16[32,192,512]{2,1,0:T(8,128)(2,1)} %bitcast.209), custom_call_target="tpu_custom_call" | custom-call | flops 3288334336 | bytes 9502720 | tf_op jit(solution)/shard_map/back_strided/pallas_call | solution.py:339
  465.6 10.3 %back_entry_spatial.1 = (bf16[7,7,16,512]{3,2,1,0:T(8,128)(2,1)S(1)}, bf16[7,2,7,2,16,512]{5,4,3,2,1,0:T(8,128)(2,1)}, f32[8,512]{1,0:T(8,128)S(1)}) custom-call(f32[7,7,16,512]{3,2,1,0:T(8,128)S(1)} %get-tuple-element.216.refs_0_, bf16[7,7,16,512]{3,2,1,0:T(8,128)(2,1)S(1)} %get-tuple-element.156.refs_0_.refs_13_.refs_1_, f32[8,512]{1,0:T(8,128)S(1)} %copy-done.22, ...), custom_call_target="tpu_custom_call" | custom-call | flops 3699376128 | bytes 15949824 | tf_op jit(solution)/shard_map/back_entry_spatial/pallas_call | solution.py:339
  476.0 10.3 %entry_spatial_grad.1 = bf16[32,144,512]{2,1,0:T(8,128)(2,1)} custom-call(bf16[2,2,8,8,16,512]{5,4,3,2,1,0:T(8,128)(2,1)} %get-tuple-element.221.refs_0_, bf16[7,7,16,512]{3,2,1,0:T(8,128)(2,1)S(1)} %get-tuple-element.222.refs_1_), custom_call_target="tpu_custom_call" | custom-call | flops 3699376128 | bytes 4997120 | tf_op jit(solution)/shard_map/entry_spatial_grad/pallas_call | solution.py:339
  489.5 12.8 %collective-permute-done.99 = bf16[4,2,1,1,128,512]{5,4,3,2,1,0:T(8,128)(2,1)S(1)} collective-permute-done((bf16[4,2,1,1,128,512]{5,4,3,2,1,0:T(8,128)(2,1)S(1)}, bf16[4,2,1,1,128,512]{5,4,3,2,1,0:T(8,128)(2,1)S(1)}, u32[]{:S(2)}, u32[]{:S(2)}) %collective-permute-start.99) | collective-permute-done | bytes 1048608 | tf_op jit(solution)/shard_map/ppermute | solution.py:23
  522.1 11.7 %back_first.1 = (bf16[14,14,16,512]{3,2,1,0:T(8,128)(2,1)}, bf16[32,32,512]{2,1,0:T(8,128)(2,1)S(1)}) custom-call(bf16[14,14,16,512]{3,2,1,0:T(8,128)(2,1)} %bitcast.238, bf16[14,14,16,512]{3,2,1,0:T(8,128)(2,1)} %get-tuple-element.153.refs_1_, f32[8,512]{1,0:T(8,128)S(1)} %copy-done.24, f32[8,512]{1,0:T(8,128)S(1)} %add_add_fusion.8.refs_3_, ...), custom_call_target="tpu_custom_call" | custom-call | flops 3288334336 | bytes 13027328 | tf_op jit(solution)/shard_map/back_first/pallas_call | solution.py:339
  548.1 11.7 %input_grad.1 = f32[14,14,16,1024]{3,2,1,0:T(8,128)} custom-call(bf16[14,14,16,512]{3,2,1,0:T(8,128)(2,1)} %get-tuple-element.242.refs_0_, bf16[32,32,512]{2,1,0:T(8,128)(2,1)} %bitcast.236, f32[7,7,16,1024]{3,2,1,0:T(8,128)} %back_strided.1.refs_2_), custom_call_target="tpu_custom_call" | custom-call | flops 3288334336 | bytes 7471104 | tf_op jit(solution)/shard_map/input_grad/pallas_call | solution.py:339
  587.3 6.4 %collective-permute-start.120 = (bf16[1,1,1,176,512]{4,3,2,1,0:T(8,128)(2,1)S(1)}, bf16[1,1,1,176,512]{4,3,2,1,0:T(8,128)(2,1)S(1)}, u32[]{:S(2)}, u32[]{:S(2)}) collective-permute-start(bf16[1,1,1,176,512]{4,3,2,1,0:T(8,128)(2,1)S(1)} %pad_maximum_fusion.18), channel_id=1, source_target_pairs={{0,8},{1,9},{2,10},{3,11},{4,12},{5,13},{6,14},{7,15},{8,0},{9,1},... | collective-permute-start | bytes 540680 | tf_op jit(solution)/shard_map/ppermute | solution.py:23
  602.2 7.6 %collective-permute-done.121 = bf16[1,1,1,176,512]{4,3,2,1,0:T(8,128)(2,1)S(1)} collective-permute-done((bf16[1,1,1,176,512]{4,3,2,1,0:T(8,128)(2,1)S(1)}, bf16[1,1,1,176,512]{4,3,2,1,0:T(8,128)(2,1)S(1)}, u32[]{:S(2)}, u32[]{:S(2)}) %collective-permute-start.121) | collective-permute-done | bytes 180256 | tf_op jit(solution)/shard_map/ppermute | solution.py:23
  (617 shorter events, 398.7 us)
Async XLA Ops:
  7.2 91.1 %all-gather.8.cloned.1.call-start = ((), (), s32[]{:S(2)}) async-start(), calls=%async_computation.3 | async-start | bytes 7299072 | tf_op jit(solution)/shard_map/all_gather | solution.py:1047
  10.0 219.1 %all-gather.6.cloned.1.call-start = ((), (), s32[]{:S(2)}) async-start(), calls=%async_computation.2 | async-start | bytes 7028736 | tf_op jit(solution)/shard_map/all_gather | solution.py:968
  32.6 502.9 %reduce-scatter.2.cloned.1.call-start = ((), (), s32[]{:S(2)}) async-start(), calls=%async_computation.1 | async-start | bytes 7028736 | tf_op jit(solution)/shard_map/reduce_scatter | solution.py:1208
  42.6 14.8 %collective-permute-start.6 = (bf16[192,512]{1,0:T(8,128)(2,1)S(1)}, bf16[192,512]{1,0:T(8,128)(2,1)S(1)}, u32[]{:S(2)}, u32[]{:S(2)}) collective-permute-start(bf16[192,512]{1,0:T(8,128)(2,1)S(1)} %pad_maximum_fusion.17), channel_id=1, source_target_pairs={{8,0},{9,1},{10,2},{11,3},{12,4},{13,5},{14,6},{15,7},{16,8},{17,9... | collective-permute-start | bytes 589832 | tf_op jit(solution)/shard_map/ppermute | solution.py:110
  75.9 13.9 %collective-permute-start.16 = (bf16[192,512]{1,0:T(8,128)(2,1)S(1)}, bf16[192,512]{1,0:T(8,128)(2,1)S(1)}, u32[]{:S(2)}, u32[]{:S(2)}) collective-permute-start(bf16[192,512]{1,0:T(8,128)(2,1)S(1)} %collective-permute-done.6), channel_id=1, source_target_pairs={{8,0},{9,1},{10,2},{11,3},{12,4},{13,5},{14,6},{15,7},{16,8},{17,9... | collective-permute-start | bytes 589832 | tf_op jit(solution)/shard_map/ppermute | solution.py:110
  98.3 21.2 %collective-permute-start.19 = (bf16[4,1,1,1,96,512]{5,4,3,2,1,0:T(8,128)(2,1)S(1)}, bf16[4,1,1,1,96,512]{5,4,3,2,1,0:T(8,128)(2,1)S(1)}, u32[]{:S(2)}, u32[]{:S(2)}) collective-permute-start(bf16[4,1,1,1,96,512]{5,4,3,2,1,0:T(8,128)(2,1)S(1)} %get-tuple-element.159), channel_id=1, source_target_pairs={{0,2},{1,3},{2,0},{3,1},{4,6},{5,7},{6,4},{7,5},{8,10},{9,11},{10,... | collective-permute-start | bytes 1179656 | tf_op jit(solution)/shard_map/ppermute | solution.py:23
  100.2 19.5 %collective-permute-start.18 = (bf16[4,1,1,1,96,512]{5,4,3,2,1,0:T(8,128)(2,1)S(1)}, bf16[4,1,1,1,96,512]{5,4,3,2,1,0:T(8,128)(2,1)}, u32[]{:S(2)}, u32[]{:S(2)}) collective-permute-start(bf16[4,1,1,1,96,512]{5,4,3,2,1,0:T(8,128)(2,1)S(1)} %get-tuple-element.158), channel_id=1, source_target_pairs={{0,4},{1,5},{2,6},{3,7},{4,0},{5,1},{6,2},{7,3},{8,12},{9,13},{10,... | collective-permute-start | bytes 1179656 | tf_op jit(solution)/shard_map/ppermute | solution.py:23
  128.4 24.3 %collective-permute-start.27 = (bf16[4,2,1,1,96,512]{5,4,3,2,1,0:T(8,128)(2,1)S(1)}, bf16[4,2,1,1,96,512]{5,4,3,2,1,0:T(8,128)(2,1)}, u32[]{:S(2)}, u32[]{:S(2)}) collective-permute-start(bf16[4,2,1,1,96,512]{5,4,3,2,1,0:T(8,128)(2,1)S(1)} %pad_maximum_fusion.5), channel_id=1, source_target_pairs={{0,2},{1,3},{2,0},{3,1},{4,6},{5,7},{6,4},{7,5},{8,10},{9,11},{10,... | collective-permute-start | bytes 2359304 | tf_op jit(solution)/shard_map/ppermute | solution.py:23
  130.2 25.1 %collective-permute-start.28 = (bf16[4,1,2,1,96,512]{5,4,3,2,1,0:T(8,128)(2,1)S(1)}, bf16[4,1,2,1,96,512]{5,4,3,2,1,0:T(8,128)(2,1)}, u32[]{:S(2)}, u32[]{:S(2)}) collective-permute-start(bf16[4,1,2,1,96,512]{5,4,3,2,1,0:T(8,128)(2,1)S(1)} %pad_maximum_fusion.6), channel_id=1, source_target_pairs={{0,4},{1,5},{2,6},{3,7},{4,0},{5,1},{6,2},{7,3},{8,12},{9,13},{10,... | collective-permute-start | bytes 2359304 | tf_op jit(solution)/shard_map/ppermute | solution.py:23
  456.5 33.0 %collective-permute-start.100 = (bf16[4,1,2,1,128,512]{5,4,3,2,1,0:T(8,128)(2,1)S(1)}, bf16[4,1,2,1,128,512]{5,4,3,2,1,0:T(8,128)(2,1)S(1)}, u32[]{:S(2)}, u32[]{:S(2)}) collective-permute-start(bf16[4,1,2,1,128,512]{5,4,3,2,1,0:T(8,128)(2,1)S(1)} %add_convert_fusion), channel_id=1, source_target_pairs={{0,4},{1,5},{2,6},{3,7},{4,0},{5,1},{6,2},{7,3},{8,12},{9,13},{10,... | collective-permute-start | bytes 3145736 | tf_op jit(solution)/shard_map/ppermute | solution.py:23
  456.6 45.7 %collective-permute-start.99 = (bf16[4,2,1,1,128,512]{5,4,3,2,1,0:T(8,128)(2,1)S(1)}, bf16[4,2,1,1,128,512]{5,4,3,2,1,0:T(8,128)(2,1)S(1)}, u32[]{:S(2)}, u32[]{:S(2)}) collective-permute-start(bf16[4,2,1,1,128,512]{5,4,3,2,1,0:T(8,128)(2,1)S(1)} %add_convert_fusion.1), channel_id=1, source_target_pairs={{0,2},{1,3},{2,0},{3,1},{4,6},{5,7},{6,4},{7,5},{8,10},{9,11},{10,... | collective-permute-start | bytes 3145736 | tf_op jit(solution)/shard_map/ppermute | solution.py:23
  502.8 33.4 %collective-permute-start.110 = (bf16[4,2,2,1,144,512]{5,4,3,2,1,0:T(8,128)(2,1)}, bf16[4,2,2,1,144,512]{5,4,3,2,1,0:T(8,128)(2,1)}, u32[]{:S(2)}, u32[]{:S(2)}) collective-permute-start(bf16[4,2,2,1,144,512]{5,4,3,2,1,0:T(8,128)(2,1)} %constant_dynamic-slice_fusion.3), channel_id=1, source_target_pairs={{0,1},{1,0},{2,3},{3,2},{4,5},{5,4},{6,7},{7,6},{8,9},{9,8},{10,11... | collective-permute-start | bytes 7077896 | tf_op jit(solution)/shard_map/ppermute | solution.py:23
  519.1 14.7 %collective-permute-start.105 = (bf16[4,1,1,1,128,512]{5,4,3,2,1,0:T(8,128)(2,1)S(1)}, bf16[4,1,1,1,128,512]{5,4,3,2,1,0:T(8,128)(2,1)S(1)}, u32[]{:S(2)}, u32[]{:S(2)}) collective-permute-start(bf16[4,1,1,1,128,512]{5,4,3,2,1,0:T(8,128)(2,1)S(1)} %get-tuple-element.226), channel_id=1, source_target_pairs={{0,4},{1,5},{2,6},{3,7},{4,0},{5,1},{6,2},{7,3},{8,12},{9,13},{10,... | collective-permute-start | bytes 1572872 | tf_op jit(solution)/shard_map/ppermute | solution.py:23
  519.3 14.6 %collective-permute-start.106 = (bf16[4,1,1,1,128,512]{5,4,3,2,1,0:T(8,128)(2,1)S(1)}, bf16[4,1,1,1,128,512]{5,4,3,2,1,0:T(8,128)(2,1)S(1)}, u32[]{:S(2)}, u32[]{:S(2)}) collective-permute-start(bf16[4,1,1,1,128,512]{5,4,3,2,1,0:T(8,128)(2,1)S(1)} %get-tuple-element.227), channel_id=1, source_target_pairs={{0,2},{1,3},{2,0},{3,1},{4,6},{5,7},{6,4},{7,5},{8,10},{9,11},{10,... | collective-permute-start | bytes 1572872 | tf_op jit(solution)/shard_map/ppermute | solution.py:23
  541.7 24.6 %collective-permute-start.116 = (bf16[4,1,2,1,96,512]{5,4,3,2,1,0:T(8,128)(2,1)S(1)}, bf16[4,1,2,1,96,512]{5,4,3,2,1,0:T(8,128)(2,1)S(1)}, u32[]{:S(2)}, u32[]{:S(2)}) collective-permute-start(bf16[4,1,2,1,96,512]{5,4,3,2,1,0:T(8,128)(2,1)S(1)} %pad_maximum_fusion.7), channel_id=1, source_target_pairs={{0,4},{1,5},{2,6},{3,7},{4,0},{5,1},{6,2},{7,3},{8,12},{9,13},{10,... | collective-permute-start | bytes 2359304 | tf_op jit(solution)/shard_map/ppermute | solution.py:23
  541.8 23.3 %collective-permute-start.115 = (bf16[4,2,1,1,80,512]{5,4,3,2,1,0:T(8,128)(2,1)S(1)}, bf16[4,2,1,1,80,512]{5,4,3,2,1,0:T(8,128)(2,1)S(1)}, u32[]{:S(2)}, u32[]{:S(2)}) collective-permute-start(bf16[4,2,1,1,80,512]{5,4,3,2,1,0:T(8,128)(2,1)S(1)} %add_convert_fusion.2), channel_id=1, source_target_pairs={{0,2},{1,3},{2,0},{3,1},{4,6},{5,7},{6,4},{7,5},{8,10},{9,11},{10,... | collective-permute-start | bytes 1966088 | tf_op jit(solution)/shard_map/ppermute | solution.py:23
  543.5 16.3 %collective-permute-start.112 = (bf16[1,1,1,256,512]{4,3,2,1,0:T(8,128)(2,1)S(1)}, bf16[1,1,1,256,512]{4,3,2,1,0:T(8,128)(2,1)S(1)}, u32[]{:S(2)}, u32[]{:S(2)}) collective-permute-start(bf16[1,1,1,256,512]{4,3,2,1,0:T(8,128)(2,1)S(1)} %pad_maximum_fusion.13), channel_id=1, source_target_pairs={{0,8},{1,9},{2,10},{3,11},{4,12},{5,13},{6,14},{7,15},{8,0},{9,1},... | collective-permute-start | bytes 786440 | tf_op jit(solution)/shard_map/ppermute | solution.py:23
  543.6 21.4 %collective-permute-start.113 = (bf16[1,1,1,256,512]{4,3,2,1,0:T(8,128)(2,1)S(1)}, bf16[1,1,1,256,512]{4,3,2,1,0:T(8,128)(2,1)S(1)}, u32[]{:S(2)}, u32[]{:S(2)}) collective-permute-start(bf16[1,1,1,256,512]{4,3,2,1,0:T(8,128)(2,1)S(1)} %pad_maximum_fusion.14), channel_id=1, source_target_pairs={{0,16},{1,17},{2,18},{3,19},{4,20},{5,21},{6,22},{7,23},{8,24},{9,... | collective-permute-start | bytes 786440 | tf_op jit(solution)/shard_map/ppermute | solution.py:23
  546.6 18.4 %collective-permute-start.114 = (bf16[1,1,1,256,512]{4,3,2,1,0:T(8,128)(2,1)S(1)}, bf16[1,1,1,256,512]{4,3,2,1,0:T(8,128)(2,1)S(1)}, u32[]{:S(2)}, u32[]{:S(2)}) collective-permute-start(bf16[1,1,1,256,512]{4,3,2,1,0:T(8,128)(2,1)S(1)} %pad_maximum_fusion.15), channel_id=1, source_target_pairs={{0,24},{1,25},{2,26},{3,27},{4,28},{5,29},{6,30},{7,31},{8,16},{9,... | collective-permute-start | bytes 786440 | tf_op jit(solution)/shard_map/ppermute | solution.py:23
  570.2 16.7 %collective-permute-start.117 = (bf16[1,1,464,512]{3,2,1,0:T(8,128)(2,1)S(1)}, bf16[1,1,464,512]{3,2,1,0:T(8,128)(2,1)S(1)}, u32[]{:S(2)}, u32[]{:S(2)}) collective-permute-start(bf16[1,1,464,512]{3,2,1,0:T(8,128)(2,1)S(1)} %maximum_bitcast_fusion), channel_id=1, source_target_pairs={{0,2},{1,3},{2,0},{3,1},{4,6},{5,7},{6,4},{7,5},{8,10},{9,11},{10,... | collective-permute-start | bytes 1425416 | tf_op jit(solution)/shard_map/ppermute | solution.py:23
  587.1 22.8 %collective-permute-start.123 = (bf16[2,1,464,512]{3,2,1,0:T(8,128)(2,1)S(1)}, bf16[2,1,464,512]{3,2,1,0:T(8,128)(2,1)S(1)}, u32[]{:S(2)}, u32[]{:S(2)}) collective-permute-start(bf16[2,1,464,512]{3,2,1,0:T(8,128)(2,1)S(1)} %pad_maximum_fusion.4), channel_id=1, source_target_pairs={{0,1},{1,0},{2,3},{3,2},{4,5},{5,4},{6,7},{7,6},{8,9},{9,8},{10,11... | collective-permute-start | bytes 2850824 | tf_op jit(solution)/shard_map/ppermute | solution.py:23
  587.3 14.9 %collective-permute-start.120 = (bf16[1,1,1,176,512]{4,3,2,1,0:T(8,128)(2,1)S(1)}, bf16[1,1,1,176,512]{4,3,2,1,0:T(8,128)(2,1)S(1)}, u32[]{:S(2)}, u32[]{:S(2)}) collective-permute-start(bf16[1,1,1,176,512]{4,3,2,1,0:T(8,128)(2,1)S(1)} %pad_maximum_fusion.18), channel_id=1, source_target_pairs={{0,8},{1,9},{2,10},{3,11},{4,12},{5,13},{6,14},{7,15},{8,0},{9,1},... | collective-permute-start | bytes 540680 | tf_op jit(solution)/shard_map/ppermute | solution.py:23
  593.7 16.1 %collective-permute-start.121 = (bf16[1,1,1,176,512]{4,3,2,1,0:T(8,128)(2,1)S(1)}, bf16[1,1,1,176,512]{4,3,2,1,0:T(8,128)(2,1)S(1)}, u32[]{:S(2)}, u32[]{:S(2)}) collective-permute-start(bf16[1,1,1,176,512]{4,3,2,1,0:T(8,128)(2,1)S(1)} %pad_maximum_fusion.19), channel_id=1, source_target_pairs={{0,16},{1,17},{2,18},{3,19},{4,20},{5,21},{6,22},{7,23},{8,24},{9,... | collective-permute-start | bytes 540680 | tf_op jit(solution)/shard_map/ppermute | solution.py:23
  594.7 15.1 %collective-permute-start.122 = (bf16[1,1,1,176,512]{4,3,2,1,0:T(8,128)(2,1)S(1)}, bf16[1,1,1,176,512]{4,3,2,1,0:T(8,128)(2,1)S(1)}, u32[]{:S(2)}, u32[]{:S(2)}) collective-permute-start(bf16[1,1,1,176,512]{4,3,2,1,0:T(8,128)(2,1)S(1)} %pad_maximum_fusion.20), channel_id=1, source_target_pairs={{0,24},{1,25},{2,26},{3,27},{4,28},{5,29},{6,30},{7,31},{8,16},{9,... | collective-permute-start | bytes 540680 | tf_op jit(solution)/shard_map/ppermute | solution.py:23
  (172 other events, 1397.3 us)
Sparse Core Ops, SparseCore 0:
  11.5 79.4 all-gather.7
  94.5 77.3 all-gather.5
  363.0 146.6 reduce-scatter.1
